TPU v7x, 256 devices: a whole 4x4x8 slice. The times are simulated.
256 devices in a mesh: trainer: 32 (over z, y), vocab: 8 (over x, core).
Axes of the slice: x: 4, y: 4, z: 8, core: 2. Of those that a mesh axis runs over, the one named last changes fastest.
Arguments:
- hidden_table: bfloat16 [1024, 3072], P('trainer')
- head_weight: bfloat16 [3072, 8, 12288], P(None, 'vocab', 'trainer'), may hold values from -0.109375 to 0.109375
- targets: bfloat16 [1024, 8, 12288], P('trainer', 'vocab')
- counts: int32 [32], replicated, may hold values from 8 to 32, as said below
- dest: int32 [1024], replicated, may hold values from 0 to 31
- token: int32 [1024], replicated, may hold values from 0 to 31
Outputs:
- head_grad: float32 [3072, 8, 12288], P(None, 'vocab', 'trainer')
- table_grad: float32 [1024, 3072], P('trainer', 'vocab')
- mean_loss: float32 [], replicated
Inputs may be any that keep to these rules, and one draw needn't show every extreme that they name: `counts`: some replica has all 32 rows live and some has 8.
All inputs are finite; a program needn't handle non-finite values.
Results may differ from a plain program's by a relative error of at most 0.00095.
The roundings to bfloat16 on the way count: a program that leaves them out, or rounds other values in their place, can miss the bound.
Values may be sent and summed in bfloat16 or wider, within the bound.
No kernel may reach another device: no remote copies, remote signals or barrier semaphores. Data moves between devices by JAX's collectives and lax.ppermute only.
A program may use at most 128 MiB of HBM per device.

v0:
```python
import functools
import math

import jax
import jax.numpy as jnp
from jax import lax
from jax.experimental import pallas as pl
from jax.experimental.pallas import tpu as pltpu
from jax.sharding import PartitionSpec as P

D = 3072
VOCAB = 98304
ROWS = 1024
TRAINERS = 32
SLOTS = 32
SHARDS = 8
LOCAL = VOCAB // (TRAINERS * SHARDS)
HALF = D // 2
BLOCK = 256
BF16 = jnp.bfloat16
F32 = jnp.float32
PARAMS = pltpu.CompilerParams(vmem_limit_bytes=24 * 1024 * 1024)
FULL = pltpu.CompilerParams(vmem_limit_bytes=60 * 1024 * 1024)
VMEM = pl.BlockSpec(memory_space=pltpu.VMEM)
SMEM = pl.BlockSpec(memory_space=pltpu.SMEM)
ANY = pl.BlockSpec(memory_space=pl.ANY)


def dot(a, b, dims=((1,), (0,))):
    return lax.dot_general(a, b, (dims, ((), ())), preferred_element_type=F32)


def split_kernel(x_ref, o_ref):
    for j in range(TRAINERS):
        o_ref[j] = x_ref[:, j * LOCAL : (j + 1) * LOCAL]


def split_targets(x):
    return pl.pallas_call(
        split_kernel,
        out_shape=jax.ShapeDtypeStruct((TRAINERS, SLOTS, LOCAL), BF16),
        in_specs=[VMEM],
        out_specs=VMEM,
        compiler_params=FULL,
    )(x)


Z = 8
Y = 4


def order_kernel(z_ref, *refs):
    pieces, outs = refs[:Z], refs[Z:]
    for k, piece in enumerate(pieces):
        at = lax.rem(z_ref[0] + Z - k, Z)
        for side, out in enumerate(outs):

            @pl.when(at // (Z // 2) == side)
            def _():
                out[lax.rem(at, Z // 2)] = piece[...]


def in_order(z, pieces):
    half = jax.ShapeDtypeStruct((Z // 2, SLOTS, HALF), BF16)
    return pl.pallas_call(
        order_kernel,
        out_shape=(half, half),
        in_specs=[SMEM] + [VMEM] * Z,
        out_specs=(VMEM, VMEM),
        compiler_params=PARAMS,
    )(z, *pieces)


def logit_kernel(at_ref, *refs):
    pieces, refs = refs[:16], refs[16:]
    far_ref, own_ref, other_ref, logits_ref, lse_ref, top_ref, *refs = refs
    tabs, w_ref, logit_buf, in_sems, out_sems = refs
    c, y = at_ref[0], at_ref[1]
    copies = [[], []]
    for side in range(2):
        rows = pl.ds(pl.multiple_of((c + side) % 2 * HALF, HALF), HALF)
        copies[side].append(
            pltpu.make_async_copy(far_ref.at[rows], w_ref.at[side], in_sems.at[16 + side])
        )
        for dy in range(Y):
            y_at = lax.rem(y + Y - dy, Y)
            for high in range(2):
                n = side * 8 + dy * 2 + high
                place = tabs.at[side, pl.ds(high * (Z // 2), Z // 2), y_at]
                copies[side].append(pltpu.make_async_copy(pieces[n], place, in_sems.at[n]))
        for copy in copies[side]:
            copy.start()
    step = BLOCK // (Y * SLOTS)

    def part(side, i):
        block = tabs[side, pl.ds(i * step, step)].reshape(BLOCK, HALF)
        return dot(block, w_ref[side])

    def store(i):
        rows = pl.ds(pl.multiple_of(i * BLOCK, BLOCK), BLOCK)
        return pltpu.make_async_copy(logit_buf.at[rows], logits_ref.at[rows], out_sems.at[2 + i])

    stores = []
    for side, out in enumerate((own_ref, other_ref)):
        for copy in copies[side]:
            copy.wait()
        stores.append(pltpu.make_async_copy(tabs.at[side], out, out_sems.at[side]))
        stores[-1].start()

        @pl.loop(0, ROWS // BLOCK)
        def _(i):
            rows = pl.ds(pl.multiple_of(i * BLOCK, BLOCK), BLOCK)
            if side == 0:
                logit_buf[rows, :] = part(side, i)
                return
            logits = logit_buf[rows, :] + part(side, i)
            logit_buf[rows, :] = logits
            store(i).start()
            top = jnp.max(logits, axis=1, keepdims=True)
            lse = top + jnp.log(jnp.sum(jnp.exp(logits - top), axis=1, keepdims=True))
            for value, out in ((lse, lse_ref), (top, top_ref)):
                flat = jnp.broadcast_to(value, (BLOCK, 128)).T
                for j in range(BLOCK // 128):
                    row = flat[0:1, j * 128 : (j + 1) * 128]
                    out[pl.ds(i * (BLOCK // 128) + j, 1), :] = row

    for copy in stores + [store(i) for i in range(ROWS // BLOCK)]:
        copy.wait()


def logits_and_stats(at, pieces, weight):
    table = jax.ShapeDtypeStruct((Z, Y, SLOTS, HALF), BF16)
    own, other, logits, lse, top = pl.pallas_call(
        logit_kernel,
        out_shape=(
            table,
            table,
            jax.ShapeDtypeStruct((ROWS, LOCAL), F32),
            jax.ShapeDtypeStruct((8, 128), F32),
            jax.ShapeDtypeStruct((8, 128), F32),
        ),
        in_specs=[SMEM] + [ANY] * 17,
        out_specs=(ANY, ANY, ANY, VMEM, VMEM),
        scratch_shapes=[
            pltpu.VMEM((2, Z, Y, SLOTS, HALF), BF16),
            pltpu.VMEM((2, HALF, LOCAL), BF16),
            pltpu.VMEM((ROWS, LOCAL), F32),
            pltpu.SemaphoreType.DMA((18,)),
            pltpu.SemaphoreType.DMA((6,)),
        ],
        compiler_params=FULL,
    )(at, *pieces, weight)
    return own.reshape(ROWS, HALF), other.reshape(ROWS, HALF), logits, lse, top


def merge(x):
    top = jnp.max(x, axis=0)
    return top + jnp.log(jnp.sum(jnp.exp(x - top[None]), axis=0))


def merge_kernel(copies, *refs):
    lse = merge(jnp.stack([ref[...] for ref in refs[:-1]]))
    if copies == 1:
        refs[-1][...] = lse
    for k in range(copies if copies > 1 else 0):
        refs[-1][k] = lse


def merge_stats(parts, copies=1):
    shape = (8, 128) if copies == 1 else (copies, 8, 128)
    return pl.pallas_call(
        functools.partial(merge_kernel, copies),
        out_shape=jax.ShapeDtypeStruct(shape, F32),
        in_specs=[VMEM] * len(parts),
        out_specs=VMEM,
        compiler_params=PARAMS if copies == 1 else FULL,
    )(*parts)


def column(row):
    return jnp.broadcast_to(row, (128, row.shape[1])).T


def select_kernel(
    top_ref, far_ref, targets_ref, gid_ref, live_ref, e_ref, mass_ref, cross_ref, *scratch
):
    logits_ref, p_ref, top_col, parts_ref, out_ref, sems = scratch
    fetch = pltpu.make_async_copy(far_ref, logits_ref, sems.at[0])
    fetch.start()
    fetch_targets = pltpu.make_async_copy(targets_ref, p_ref, sems.at[1])
    fetch_targets.start()
    for j in range(8):
        top_col[pl.ds(j * 128, 128), :] = column(top_ref[j : j + 1, :])
    fetch.wait()

    @pl.loop(0, ROWS // 128)
    def _(i):
        rows = pl.ds(pl.multiple_of(i * 128, 128), 128)
        for j in range(LOCAL // 128):
            p = jnp.exp(logits_ref[rows, pl.ds(j * 128, 128)] - top_col[rows, :])
            first = p.astype(BF16)
            p = p - first.astype(F32)
            second = p.astype(BF16)
            third = (p - second.astype(F32)).astype(BF16)
            parts_ref[rows, pl.ds(j * 128, 128)] = first
            parts_ref[rows, pl.ds(LOCAL + j * 128, 128)] = second
            parts_ref[rows, pl.ds(2 * LOCAL + j * 128, 128)] = third

    def store(i):
        rows = pl.ds(pl.multiple_of(i * BLOCK, BLOCK), BLOCK)
        return pltpu.make_async_copy(out_ref.at[rows], e_ref.at[rows], sems.at[2 + i])

    @pl.loop(0, ROWS // BLOCK)
    def _(i):
        rows = pl.ds(pl.multiple_of(i * BLOCK, BLOCK), BLOCK)
        gid = column(gid_ref[:, rows])
        lane = lax.broadcasted_iota(jnp.int32, (BLOCK, 128), 1).astype(F32)
        hot = jnp.concatenate(
            [
                jnp.where(gid == lane + float(128 * k), 1.0, 0.0).astype(BF16)
                for k in range(ROWS // 128)
            ],
            axis=1,
        )
        sel = dot(hot, parts_ref[...])
        out_ref[rows, :] = sel[:, 0:LOCAL] + sel[:, LOCAL : 2 * LOCAL] + sel[:, 2 * LOCAL :]
        store(i).start()

    fetch_targets.wait()

    def total(i, cross):
        rows = pl.ds(pl.multiple_of(i * BLOCK, BLOCK), BLOCK)
        row = lax.broadcasted_iota(jnp.int32, (BLOCK, ROWS), 0) + i * BLOCK
        hot = jnp.where(gid_ref[...] == row.astype(F32), live_ref[...], 0.0).astype(BF16)
        sums = dot(hot, p_ref[...])
        mass = jnp.broadcast_to(jnp.sum(sums, axis=1, keepdims=True), (BLOCK, 128)).T[0:1]
        for j in range(BLOCK // 128):
            mass_ref[pl.ds(i * (BLOCK // 128) + j, 1), :] = mass[:, j * 128 : (j + 1) * 128]
        return cross + jnp.sum(sums * logits_ref[rows, :])

    cross_ref[0, 0] = lax.fori_loop(0, ROWS // BLOCK, total, jnp.float32(0))
    for i in range(ROWS // BLOCK):
        store(i).wait()


def select_rows(top, logits, probs, gid, live):
    return pl.pallas_call(
        select_kernel,
        out_shape=(
            jax.ShapeDtypeStruct((ROWS, LOCAL), F32),
            jax.ShapeDtypeStruct((8, 128), F32),
            jax.ShapeDtypeStruct((1, 1), F32),
        ),
        in_specs=[VMEM, ANY, ANY, VMEM, VMEM],
        out_specs=(ANY, VMEM, SMEM),
        scratch_shapes=[
            pltpu.VMEM((ROWS, LOCAL), F32),
            pltpu.VMEM((ROWS, LOCAL), BF16),
            pltpu.VMEM((ROWS, 128), F32),
            pltpu.VMEM((ROWS, 3 * LOCAL), BF16),
            pltpu.VMEM((ROWS, LOCAL), F32),
            pltpu.SemaphoreType.DMA((6,)),
        ],
        compiler_params=FULL,
        cost_estimate=pl.CostEstimate(
            flops=4 * 2 * ROWS * ROWS * LOCAL, bytes_accessed=8 * 1024 * 1024, transcendentals=0
        ),
    )(top, logits, probs, gid, live)


def grad_kernel(
    x_ref, top_ref, mass_ref, cross_ref, far_ref, targets_ref, gid_ref, live_ref, *refs
):
    high_ref, both_ref, loss_ref, e_ref, p_ref, g_ref, sums_ref, sems = refs
    fetch = pltpu.make_async_copy(far_ref, e_ref, sems.at[0])
    fetch.start()
    fetch_targets = pltpu.make_async_copy(targets_ref, p_ref, sems.at[1])
    fetch_targets.start()
    lse = merge(x_ref[...])
    loss_ref[0, 0] = jnp.sum(lse * mass_ref[...]) - cross_ref[0, 0]
    share = jnp.exp(top_ref[...] - lse)
    scale = VOCAB / math.sqrt(ROWS)
    fetch.wait()
    fetch_targets.wait()
    lane = lax.broadcasted_iota(jnp.int32, (128, 128), 1).astype(F32)

    @pl.loop(0, ROWS // 128)
    def _(i):
        rows = pl.ds(pl.multiple_of(i * 128, 128), 128)
        gid = column(gid_ref[:, rows])
        factor = column(live_ref[:, rows]) * scale
        found = jnp.zeros((128, 128), F32)
        for k in range(ROWS // 128):
            found += jnp.where(gid == lane + float(128 * k), share[k : k + 1], 0.0)
        found = jnp.sum(found, axis=1, keepdims=True)
        for j in range(LOCAL // 128):
            cols = pl.ds(j * 128, 128)
            diff = e_ref[rows, cols] * found - p_ref[rows, cols].astype(F32)
            g_ref[rows, cols] = (factor * diff).astype(BF16)

    def stores(i):
        rows = pl.ds(pl.multiple_of(i * BLOCK, BLOCK), BLOCK)
        high = sums_ref.at[rows, pl.ds(0, LOCAL)]
        yield pltpu.make_async_copy(high, high_ref.at[rows], sems.at[2 + i])
        yield pltpu.make_async_copy(sums_ref.at[rows], both_ref.at[rows], sems.at[6 + i])

    @pl.loop(0, ROWS // BLOCK)
    def _(i):
        rows = pl.ds(pl.multiple_of(i * BLOCK, BLOCK), BLOCK)
        row = lax.broadcasted_iota(jnp.int32, (BLOCK, ROWS), 0) + i * BLOCK
        hot = jnp.where(gid_ref[...] == row.astype(F32), 1.0, 0.0).astype(BF16)
        sums = dot(hot, g_ref[...])
        high = sums.astype(BF16)
        sums_ref[rows, 0:LOCAL] = high
        sums_ref[rows, LOCAL:] = (sums - high.astype(F32)).astype(BF16)
        for store in stores(i):
            store.start()

    for i in range(ROWS // BLOCK):
        for store in stores(i):
            store.wait()


def gradients(x, top, mass, cross, e, probs, gid, live):
    return pl.pallas_call(
        grad_kernel,
        out_shape=(
            jax.ShapeDtypeStruct((ROWS, LOCAL), BF16),
            jax.ShapeDtypeStruct((ROWS, 2 * LOCAL), BF16),
            jax.ShapeDtypeStruct((1, 1), F32),
        ),
        in_specs=[VMEM, VMEM, VMEM, SMEM, ANY, ANY, VMEM, VMEM],
        out_specs=(ANY, ANY, SMEM),
        scratch_shapes=[
            pltpu.VMEM((ROWS, LOCAL), F32),
            pltpu.VMEM((ROWS, LOCAL), BF16),
            pltpu.VMEM((ROWS, LOCAL), BF16),
            pltpu.VMEM((ROWS, 2 * LOCAL), BF16),
            pltpu.SemaphoreType.DMA((10,)),
        ],
        compiler_params=FULL,
    )(x, top, mass, cross, e, probs, gid, live)


TOP = 32700.0
ROWS2 = ROWS // 2
TAIL = 16
I16 = jnp.int16


def exponent(x):
    return jnp.ceil(jnp.log(jnp.maximum(x, 1e-30) / TOP) * (256.0 / math.log(2.0)))


def power(e):
    return jnp.exp2(e * (1.0 / 256.0))


def to16(x):
    return x.astype(jnp.int32).astype(I16)


def from16(x):
    return x.astype(jnp.int32).astype(F32)


def encode(val):
    e = exponent(jnp.max(jnp.abs(val), axis=1, keepdims=True))
    return to16(jnp.round(val * power(-e))), jnp.broadcast_to(e, (128, 128)).T[0:1]


def wide(row):
    return jnp.concatenate([row] + [jnp.zeros_like(row)] * (LOCAL // 128 - 1), axis=1)


def write_message(out_ref, block_of, loss, tail_ref):
    @pl.loop(0, ROWS2 // 128)
    def _(j):
        code, e = encode(block_of(j))
        out_ref[pl.ds(pl.multiple_of(j * 128, 128), 128), :] = code
        tail_ref[pl.ds(j, 1), :] = e

    tail = [tail_ref[0 : ROWS2 // 128, :], loss, jnp.zeros((TAIL - ROWS2 // 128 - 1, 128), F32)]
    tail = jnp.concatenate(tail, axis=0)
    zeros = [jnp.zeros_like(tail)] * (LOCAL // 128 - 1)
    out_ref[pl.ds(ROWS2, TAIL), :] = to16(jnp.concatenate([tail] + zeros, axis=1))


def encode_loss(loss):
    e = exponent(jnp.abs(loss))
    whole = loss * power(-e)
    first = jnp.round(whole)
    rest = jnp.round((whole - first) * TOP)
    lane = lax.broadcasted_iota(jnp.int32, (1, 128), 1)
    return jnp.where(lane == 0, e, jnp.where(lane == 1, first, jnp.where(lane == 2, rest, 0.0)))


def decode_loss(code):
    return (code[:, 1:2] + code[:, 2:3] * (1.0 / TOP)) * power(code[:, 0:1])


def read_tail(ref, tail_ref):
    tail_ref[...] = from16(ref[pl.ds(ROWS2, TAIL), 0:128])


def tail_loss(tail_ref):
    return tail_ref[ROWS2 // 128 : ROWS2 // 128 + 1, :]


def read_message(ref, tail_ref, j):
    scale = power(column(tail_ref[pl.ds(j, 1), :]))
    rows = pl.ds(pl.multiple_of(j * 128, 128), 128)
    parts = [from16(ref[rows, k * 128 : (k + 1) * 128]) * scale for k in range(LOCAL // 128)]
    return jnp.concatenate(parts, axis=1)


TAIL_REF = pltpu.VMEM((TAIL, 128), F32)
MESSAGE = jax.ShapeDtypeStruct((ROWS2 + TAIL, LOCAL), I16)


def weight_kernel(at_ref, all_ref, keep_ref, give_ref, block_ref, sems):
    c, x = at_ref[0], at_ref[1]

    def fetch(n):
        source = all_ref.at[lax.rem(x + n % 4, 4), lax.rem(c + n // 4, 2)]
        return pltpu.make_async_copy(source, block_ref.at[n], sems.at[n])

    for n in range(8):
        fetch(n).start()
    for n in range(8):
        fetch(n).wait()
        out = (keep_ref, give_ref)[n // 4]
        out[:, n % 4 * LOCAL : (n % 4 + 1) * LOCAL] = block_ref[n].T


def turn_weights(at, blocks):
    half = jax.ShapeDtypeStruct((LOCAL, 4 * LOCAL), BF16)
    return pl.pallas_call(
        weight_kernel,
        out_shape=(half, half),
        in_specs=[SMEM, ANY],
        out_specs=(VMEM, VMEM),
        scratch_shapes=[
            pltpu.VMEM((8, LOCAL, LOCAL), BF16),
            pltpu.SemaphoreType.DMA((8,)),
        ],
        compiler_params=FULL,
    )(at, blocks)


def term_kernel(
    loss_ref, more_ref, own_ref, other_ref, w_own, w_other, c0, l1, h1, l2, h2, l3, h3, sum_ref, *refs
):
    g_ref, w_ref, val_ref, tail_ref, sems = refs
    fetches = [
        pltpu.make_async_copy(ref, g_ref.at[:, pl.ds(k * LOCAL, LOCAL)], sems.at[k])
        for k, ref in enumerate((own_ref, other_ref))
    ] + [
        pltpu.make_async_copy(ref, w_ref.at[pl.ds(k * LOCAL, LOCAL)], sems.at[2 + k])
        for k, ref in enumerate((w_own, w_other))
    ]
    for fetch in fetches:
        fetch.start()
    loss = encode_loss(jnp.full((1, 128), loss_ref[0, 0] + more_ref[0, 0], F32))
    sum_ref[...] = loss
    for fetch in fetches:
        fetch.wait()

    @pl.loop(0, ROWS // BLOCK)
    def _(i):
        rows = pl.ds(pl.multiple_of(i * BLOCK, BLOCK), BLOCK)
        val_ref[rows, :] = dot(g_ref[rows, :], w_ref[...])

    c0[...] = val_ref[:, 0:LOCAL]
    for i, k, out in ((0, 2, l2), (1, 2, h2), (1, 1, h1), (0, 3, l3), (0, 1, l1), (1, 3, h3)):
        cols = slice(k * LOCAL, (k + 1) * LOCAL)
        if out.dtype == F32:
            out[...] = val_ref[i * ROWS2 : (i + 1) * ROWS2, cols]
        else:

            def block(j):
                at = pl.multiple_of(i * ROWS2 + j * 128, 128)
                return val_ref[pl.ds(at, 128), cols]

            write_message(out, block, loss, tail_ref)


def terms(loss, more, own, other, w_own, w_other):
    part = jax.ShapeDtypeStruct((ROWS2, LOCAL), F32)
    return pl.pallas_call(
        term_kernel,
        out_shape=(
            jax.ShapeDtypeStruct((ROWS, LOCAL), F32),
            part,
            MESSAGE,
            MESSAGE,
            MESSAGE,
            MESSAGE,
            part,
            jax.ShapeDtypeStruct((1, 128), F32),
        ),
        in_specs=[SMEM, SMEM] + [ANY] * 4,
        out_specs=(VMEM,) * 8,
        scratch_shapes=[
            pltpu.VMEM((ROWS, 2 * LOCAL), BF16),
            pltpu.VMEM((2 * LOCAL, 4 * LOCAL), BF16),
            pltpu.VMEM((ROWS, 4 * LOCAL), F32),
            TAIL_REF,
            pltpu.SemaphoreType.DMA((4,)),
        ],
        compiler_params=PARAMS,
    )(loss, more, own, other, w_own, w_other)


def relay_kernel(own_ref, got_ref, out_ref, got_tail, tail_ref):
    read_tail(got_ref, got_tail)

    def block(j):
        rows = pl.ds(pl.multiple_of(j * 128, 128), 128)
        return own_ref[rows, :] + read_message(got_ref, got_tail, j)

    write_message(out_ref, block, tail_loss(got_tail), tail_ref)


def relay(own, got):
    return pl.pallas_call(
        relay_kernel,
        out_shape=MESSAGE,
        in_specs=[VMEM] * 2,
        out_specs=VMEM,
        scratch_shapes=[TAIL_REF] * 2,
        compiler_params=PARAMS,
    )(own, got)


PACKED = 3 * SLOTS + TAIL


def pack_kernel(loss_ref, own_ref, low_r, low_l, high_r, high_l, o_ref, *tails):
    messages = (low_r, low_l, high_r, high_l)
    for ref, tail_ref in zip(messages, tails):
        read_tail(ref, tail_ref)
    codes = [loss_ref[...]] + [tail_loss(tail_ref) for tail_ref in tails[:3]]
    loss = decode_loss(jnp.concatenate(codes, axis=0))
    loss = (loss[0:1] + loss[1:2]) + (loss[2:3] + loss[3:4])
    loss = encode_loss(jnp.broadcast_to(loss, (1, 128)))
    pad = jnp.zeros((TAIL - 2, 128), F32)
    for i in range(2):

        @pl.loop(0, ROWS2 // 128)
        def _(j):
            at = i * (ROWS2 // 128) + j
            val = own_ref[pl.ds(pl.multiple_of(at * 128, 128), 128), :]
            got = [read_message(messages[n], tails[n], j) for n in (2 * i, 2 * i + 1)]
            code, e = encode(val + (got[0] + got[1]))
            tail = to16(jnp.concatenate([e, loss, pad], axis=0))
            for n in range(128 // SLOTS):
                for k in range(3):
                    o_ref[at * 4 + n, k * SLOTS : (k + 1) * SLOTS, :] = code[
                        n * SLOTS : (n + 1) * SLOTS, k * 128 : (k + 1) * 128
                    ]
                o_ref[at * 4 + n, 3 * SLOTS :, :] = tail


def pack(loss, own, low_r, low_l, high_r, high_l):
    return pl.pallas_call(
        pack_kernel,
        out_shape=jax.ShapeDtypeStruct((TRAINERS, PACKED, 128), I16),
        in_specs=[VMEM] * 6,
        out_specs=VMEM,
        scratch_shapes=[TAIL_REF] * 4,
        compiler_params=PARAMS,
    )(loss, own, low_r, low_l, high_r, high_l)


def finish_kernel(at_ref, x_ref, grad_ref, loss_ref, e_ref):
    tail = from16(x_ref[:, 3 * SLOTS :, :])
    e = tail[:, 0, :]
    e_ref[...] = jnp.concatenate([e, jnp.zeros((128 - TRAINERS, 128), F32)], axis=0).T
    scale = power(e_ref[pl.ds(pl.multiple_of(at_ref[0] * SLOTS, SLOTS), SLOTS), :])
    total = [jnp.zeros((SLOTS, 128), F32)] * 3
    for s in range(TRAINERS):
        for k in range(3):
            total[k] += from16(x_ref[s, k * SLOTS : (k + 1) * SLOTS, :]) * scale[:, s : s + 1]
    for k in range(3):
        grad_ref[:, k * 128 : (k + 1) * 128] = total[k]
    loss_ref[0, 0] = jnp.sum(decode_loss(tail[:, 1, :]))


def finish(at, x):
    return pl.pallas_call(
        finish_kernel,
        out_shape=(
            jax.ShapeDtypeStruct((SLOTS, LOCAL), F32),
            jax.ShapeDtypeStruct((1, 1), F32),
        ),
        in_specs=[SMEM, VMEM],
        out_specs=(VMEM, SMEM),
        scratch_shapes=[pltpu.VMEM((128, 128), F32)],
        compiler_params=PARAMS,
    )(at, x)


HEAD_BLOCK = 256
HEAD_STEPS = HALF // HEAD_BLOCK


def head_kernel(c_ref, own_ref, other_ref, sums_ref, o_ref):
    i = pl.program_id(0)

    def work(t_ref):
        both = dot(t_ref[...], sums_ref[...], ((0,), (0,)))
        both = both[:, 0:LOCAL] + both[:, LOCAL:]
        for j in range(LOCAL // 128):
            o_ref[pl.ds(j, HEAD_BLOCK, stride=LOCAL // 128), :] = both[:, j * 128 : (j + 1) * 128]

    @pl.when(i < HEAD_STEPS)
    def _():
        work(own_ref)

    @pl.when(i >= HEAD_STEPS)
    def _():
        work(other_ref)


def head_gradient(c, own, other, sums):
    def place(i, c):
        mine = i < HEAD_STEPS
        side = jnp.where(mine, c[0], 1 - c[0])
        return (side * HEAD_STEPS + jnp.where(mine, i, i - HEAD_STEPS), 0)

    return pl.pallas_call(
        head_kernel,
        grid_spec=pltpu.PrefetchScalarGridSpec(
            num_scalar_prefetch=1,
            grid=(2 * HEAD_STEPS,),
            in_specs=[
                pl.BlockSpec((ROWS, HEAD_BLOCK), lambda i, c: (0, jnp.minimum(i, HEAD_STEPS - 1))),
                pl.BlockSpec((ROWS, HEAD_BLOCK), lambda i, c: (0, jnp.maximum(i - HEAD_STEPS, 0))),
                pl.BlockSpec((ROWS, 2 * LOCAL), lambda i, c: (0, 0)),
            ],
            out_specs=pl.BlockSpec((HEAD_BLOCK * LOCAL // 128, 128), place),
        ),
        out_shape=jax.ShapeDtypeStruct((D * LOCAL // 128, 128), F32),
        compiler_params=PARAMS,
        cost_estimate=pl.CostEstimate(
            flops=4 * ROWS * D * LOCAL, bytes_accessed=12 * 1024 * 1024, transcendentals=0
        ),
    )(c, own, other, sums)


PAIR = [(i, i ^ 1) for i in range(SHARDS)]


def along_x(k):
    return [(i, (i + 2 * k) % SHARDS) for i in range(SHARDS)]


RIGHT, LEFT = along_x(1), along_x(-1)


def along_z(k):
    return [(i, (i // Y + k) % Z * Y + i % Y) for i in range(TRAINERS)]


def along_y(k):
    return [(i, i // Y * Y + (i + k) % Y) for i in range(TRAINERS)]


def on_device(hidden_table, head_weight, targets, counts, dest, token):
    me = lax.axis_index("vocab")
    trainer = lax.axis_index("trainer")
    c = lax.rem(me, 2)
    x = me // 2
    y = lax.rem(trainer, Y)
    c1 = c.reshape(1).astype(jnp.int32)
    at_cx = jnp.stack([c, x]).astype(jnp.int32)
    at_cy = jnp.stack([c, y]).astype(jnp.int32)
    z1 = (trainer // Y).reshape(1).astype(jnp.int32)
    weight = head_weight[:, 0, :]

    half = lax.dynamic_slice(hidden_table, (0, c * HALF), (SLOTS, HALF))
    near = [half] + [lax.ppermute(half, "trainer", along_z(k)) for k in range(1, Z)]

    split = split_targets(targets[:, 0, :])

    gid = dest * SLOTS + token
    index = jnp.arange(ROWS, dtype=jnp.int32)
    live = (index % SLOTS < jnp.repeat(counts, SLOTS)).astype(F32).reshape(1, ROWS)
    gid = gid.astype(F32).reshape(1, ROWS)

    w_own, w_give = turn_weights(at_cx, weight.reshape(4, 2, LOCAL, LOCAL))
    z1, split, gid, live, w_own, w_give = lax.optimization_barrier(
        (z1, split, gid, live, w_own, w_give)
    )
    low0, high0 = in_order(z1, near)
    low1 = lax.ppermute(low0, "trainer", along_y(1))
    high3 = lax.ppermute(high0, "trainer", along_y(-1))
    high1 = lax.ppermute(high0, "trainer", along_y(1))
    low3 = lax.ppermute(low0, "trainer", along_y(-1))
    low2 = lax.ppermute(low1, "trainer", along_y(1))
    high2 = lax.ppermute(high3, "trainer", along_y(-1))
    pieces = (low0, high0, low1, high1, low2, high2, low3, high3)
    pieces += tuple(lax.ppermute(p, "vocab", PAIR) for p in pieces)
    split, _ = lax.optimization_barrier((split, (low2, high2) + pieces[8:12] + pieces[14:]))
    probs = lax.all_to_all(split, "trainer", split_axis=0, concat_axis=0, tiled=True)

    own, other, logits, stats, top = logits_and_stats(at_cy, pieces, weight)
    stats = merge_stats([stats, lax.ppermute(stats, "vocab", PAIR)])
    stats = [stats] + [lax.ppermute(stats, "vocab", along_x(k)) for k in (1, 2, 3)]
    stats = merge_stats(stats, TRAINERS)
    stats, probs = lax.optimization_barrier((stats, probs.reshape(ROWS, LOCAL)))
    stats = lax.all_to_all(stats, "trainer", split_axis=0, concat_axis=0, tiled=True)

    w_give, _ = lax.optimization_barrier((w_give, top))
    w_other = lax.ppermute(w_give, "vocab", PAIR)
    e, mass, cross = select_rows(top, logits, probs, gid, live)
    high, sums, loss = gradients(stats, top, mass, cross, e, probs, gid, live)

    more = lax.ppermute(loss, "vocab", PAIR)
    far = lax.ppermute(high, "vocab", PAIR)
    t0, l1, h1, l2, h2, l3, h3, loss = terms(loss, more, high, far, w_own, w_other)
    low_r = lax.ppermute(l2, "vocab", RIGHT)
    high_l = lax.ppermute(h2, "vocab", LEFT)
    high_r = lax.ppermute(h1, "vocab", RIGHT)
    low_l = lax.ppermute(l3, "vocab", LEFT)
    low_r = lax.ppermute(relay(l1, low_r), "vocab", RIGHT)
    high_l = lax.ppermute(relay(h3, high_l), "vocab", LEFT)
    head = head_gradient(c1, own, other, sums)
    packed = pack(loss, t0, low_r, low_l, high_r, high_l)
    packed = lax.all_to_all(packed, "trainer", split_axis=0, concat_axis=0, tiled=True)
    table_grad, loss = finish(lax.rem(trainer, 4).reshape(1).astype(jnp.int32), packed)
    mean_loss = loss[0, 0] / jnp.sum(counts).astype(F32)
    return head.reshape(D, 1, LOCAL), table_grad, mean_loss


def solution(mesh):
    return jax.shard_map(
        on_device,
        mesh=mesh,
        in_specs=(
            P("trainer", None),
            P(None, "vocab", "trainer"),
            P("trainer", "vocab", None),
            P(),
            P(),
            P(),
        ),
        out_specs=(P(None, "vocab", "trainer"), P("trainer", "vocab"), P()),
        check_vma=False,
    )
```

profile of v0, /device:TPU:8, one launch (start us, length us, event | category | flops | bytes accessed | tf_op | source)
XLA Modules:
  0.0 216.4 jit_solution(7149755225413925222)
XLA Ops:
  1.6 2.0 collective-permute-start
  3.6 3.3 %collective-permute-start.1 = (bf16[32,1536]{1,0:T(8,128)(2,1)S(1)}, bf16[32,1536]{1,0:T(8,128)(2,1)S(1)}, u32[]{:S(2)}, u32[]{:S(2)}) collective-permute-start(bf16[32,1536]{1,0:T(8,128)(2,1)S(1)} %constant_dynamic-slice_fusion.refs_0_), channel_id=1, source_target_pairs={{0,64},{8,72},{16,80},{24,88},{32,96},{40,104},{48,112},{56,120},{... | collective-permute-start | bytes 294920 | tf_op jit(solution)/shard_map/ppermute | solution.py:683
  6.8 4.0 %collective-permute-start.2 = (bf16[32,1536]{1,0:T(8,128)(2,1)S(1)}, bf16[32,1536]{1,0:T(8,128)(2,1)S(1)}, u32[]{:S(2)}, u32[]{:S(2)}) collective-permute-start(bf16[32,1536]{1,0:T(8,128)(2,1)S(1)} %constant_dynamic-slice_fusion.refs_0_), channel_id=1, source_target_pairs={{0,96},{8,104},{16,112},{24,120},{32,128},{40,136},{48,144},{56,15... | collective-permute-start | bytes 294920 | tf_op jit(solution)/shard_map/ppermute | solution.py:683
  11.4 4.9 %collective-permute-start.4 = (bf16[32,1536]{1,0:T(8,128)(2,1)S(1)}, bf16[32,1536]{1,0:T(8,128)(2,1)S(1)}, u32[]{:S(2)}, u32[]{:S(2)}) collective-permute-start(bf16[32,1536]{1,0:T(8,128)(2,1)S(1)} %constant_dynamic-slice_fusion.refs_0_), channel_id=1, source_target_pairs={{0,160},{8,168},{16,176},{24,184},{32,192},{40,200},{48,208},{56,2... | collective-permute-start | bytes 294920 | tf_op jit(solution)/shard_map/ppermute | solution.py:683
  17.2 1.3 add_convert_fusion
  19.1 2.1 shard_map.85
  21.2 2.7 %collective-permute-start.5 = (bf16[32,1536]{1,0:T(8,128)(2,1)S(1)}, bf16[32,1536]{1,0:T(8,128)(2,1)S(1)}, u32[]{:S(2)}, u32[]{:S(2)}) collective-permute-start(bf16[32,1536]{1,0:T(8,128)(2,1)S(1)} %constant_dynamic-slice_fusion.refs_0_), channel_id=1, source_target_pairs={{0,192},{8,200},{16,208},{24,216},{32,224},{40,232},{48,240},{56,2... | collective-permute-start | bytes 294920 | tf_op jit(solution)/shard_map/ppermute | solution.py:683
  25.4 4.2 %shard_map.86 = (bf16[384,1536]{1,0:T(8,128)(2,1)}, bf16[384,1536]{1,0:T(8,128)(2,1)}) custom-call(s32[2]{0:T(128)} %pad_add_fusion.1.at_ref, bf16[4,2,384,384]{3,2,1,0:T(8,128)(2,1)} %bitcast.15), custom_call_target="tpu_custom_call" | custom-call | tf_op jit(solution)/shard_map/pallas_call | solution.py:438
  30.0 1.6 collective-permute-done.6.refs_7_
  32.4 1.6 collective-permute-start.7
  34.0 1.6 collective-permute-start.8
  36.0 8.0 %collective-permute-done.10.refs_7_ = bf16[4,32,1536]{2,1,0:T(8,128)(2,1)S(1)} collective-permute-done((bf16[4,32,1536]{2,1,0:T(8,128)(2,1)S(1)}, bf16[4,32,1536]{2,1,0:T(8,128)(2,1)S(1)}, u32[]{:S(2)}, u32[]{:S(2)}) %collective-permute-start.10) | collective-permute-done | bytes 393248 | tf_op jit(solution)/shard_map/ppermute | solution.py:698
  44.0 1.4 collective-permute-done.7.refs_2_
  45.4 3.2 %collective-permute-start.11 = (bf16[4,32,1536]{2,1,0:T(8,128)(2,1)S(1)}, bf16[4,32,1536]{2,1,0:T(8,128)(2,1)S(1)}, u32[]{:S(2)}, u32[]{:S(2)}) collective-permute-start(bf16[4,32,1536]{2,1,0:T(8,128)(2,1)S(1)} %collective-permute-done.10.refs_7_), channel_id=1, source_target_pairs={{0,24},{8,0},{16,8},{24,16},{32,56},{40,32},{48,40},{56,48},{64,88... | collective-permute-start | bytes 1179656 | tf_op jit(solution)/shard_map/ppermute | solution.py:702
  48.7 2.7 %collective-permute-done.8.refs_3_ = bf16[4,32,1536]{2,1,0:T(8,128)(2,1)S(1)} collective-permute-done((bf16[4,32,1536]{2,1,0:T(8,128)(2,1)S(1)}, bf16[4,32,1536]{2,1,0:T(8,128)(2,1)S(1)}, u32[]{:S(2)}, u32[]{:S(2)}) %collective-permute-start.8) | collective-permute-done | bytes 393248 | tf_op jit(solution)/shard_map/ppermute | solution.py:699
  51.4 1.0 collective-permute-done.12.refs_6_
  53.0 5.3 %collective-permute-done.11.refs_5_ = bf16[4,32,1536]{2,1,0:T(8,128)(2,1)S(1)} collective-permute-done((bf16[4,32,1536]{2,1,0:T(8,128)(2,1)S(1)}, bf16[4,32,1536]{2,1,0:T(8,128)(2,1)S(1)}, u32[]{:S(2)}, u32[]{:S(2)}) %collective-permute-start.11) | collective-permute-done | bytes 393248 | tf_op jit(solution)/shard_map/ppermute | solution.py:702
  58.3 1.6 collective-permute-start.9
  61.7 5.6 %collective-permute-done.9.refs_4_ = bf16[4,32,1536]{2,1,0:T(8,128)(2,1)} collective-permute-done((bf16[4,32,1536]{2,1,0:T(8,128)(2,1)S(1)}, bf16[4,32,1536]{2,1,0:T(8,128)(2,1)}, u32[]{:S(2)}, u32[]{:S(2)}) %collective-permute-start.9) | collective-permute-done | bytes 393248 | tf_op jit(solution)/shard_map/ppermute | solution.py:701
  67.3 10.4 %all-to-all-start = ((bf16[32,32,384]{2,1,0:T(8,128)(2,1)}), bf16[32,32,384]{2,1,0:T(8,128)(2,1)S(1)}, u32[]{:S(2)}, u32[]{:S(2)}) async-start(bf16[32,32,384]{2,1,0:T(8,128)(2,1)} %shard_map.85), calls=%async_computation | async-start | bytes 1572864 | tf_op jit(solution)/shard_map/all_to_all | solution.py:706
  80.5 9.8 %shard_map.88 = (bf16[8,4,32,1536]{3,2,1,0:T(8,128)(2,1)}, bf16[8,4,32,1536]{3,2,1,0:T(8,128)(2,1)}, f32[1024,384]{1,0:T(8,128)}, f32[8,128]{1,0:T(8,128)}, f32[8,128]{1,0:T(8,128)}) custom-call(s32[2]{0:T(128)} %pad_add_fusion.at_ref, bf16[4,32,1536]{2,1,0:T(8,128)(2,1)} %copy-done.3, bf16[4,32,1536]{2,1,0:T(8,128)(2,1)} %copy-done.4, ...), custom_call_target="tpu_custom_call" | custom-call | tf_op jit(solution)/shard_map/pallas_call | solution.py:133
  90.9 2.6 %collective-permute-done.21.refs_1_ = f32[8,128]{1,0:T(8,128)S(1)} collective-permute-done((f32[8,128]{1,0:T(8,128)}, f32[8,128]{1,0:T(8,128)S(1)}, u32[]{:S(2)}, u32[]{:S(2)}) %collective-permute-start.21) | collective-permute-done | bytes 4128 | tf_op jit(solution)/shard_map/ppermute | solution.py:709
  94.2 1.6 collective-permute-start.22
  95.7 2.7 %collective-permute-start.23 = (f32[8,128]{1,0:T(8,128)S(1)}, f32[8,128]{1,0:T(8,128)S(1)}, u32[]{:S(2)}, u32[]{:S(2)}) collective-permute-start(f32[8,128]{1,0:T(8,128)S(1)} %shard_map.89.refs_0_), channel_id=1, source_target_pairs={{0,4},{1,5},{2,6},{3,7},{4,0},{5,1},{6,2},{7,3},{8,12},{9,13},{10,... | collective-permute-start | bytes 12296 | tf_op jit(solution)/shard_map/ppermute | solution.py:710
  98.5 1.4 collective-permute-start.24
  100.9 1.2 collective-permute-done.24.refs_3_
  102.7 1.4 shard_map.90
  104.1 9.8 %all-to-all-start.1 = ((f32[32,8,128]{2,1,0:T(8,128)}), f32[32,8,128]{2,1,0:T(8,128)S(1)}, u32[]{:S(2)}, u32[]{:S(2)}) async-start(f32[32,8,128]{2,1,0:T(8,128)} %shard_map.90), calls=%async_computation.1 | async-start | bytes 262144 | tf_op jit(solution)/shard_map/all_to_all | solution.py:713
  113.9 9.4 %shard_map.91 = (f32[1024,384]{1,0:T(8,128)}, f32[8,128]{1,0:T(8,128)}, f32[1,1]{1,0:T(1,128)}) custom-call(f32[8,128]{1,0:T(8,128)} %get-tuple-element.49.top_ref, f32[1024,384]{1,0:T(8,128)} %get-tuple-element.50.far_ref, bf16[1024,384]{1,0:T(8,128)(2,1)} %bitcast.17, f32[1,1024]{1,0:T(1,128)} %bitcast.20, f32[1,1024]{1,0:T(1,128)} %compare_convert_fusion.live_ref), custom_call_target="tpu_custom_call" | custom-call | flops 3221225472 | bytes 8388608 | tf_op jit(solution)/shard_map/pallas_call | solution.py:247
  124.0 8.0 %shard_map.92 = (bf16[1024,384]{1,0:T(8,128)(2,1)}, bf16[1024,768]{1,0:T(8,128)(2,1)}, f32[1,1]{1,0:T(1,128)}) custom-call(f32[32,8,128]{2,1,0:T(8,128)} %copy-done.11, f32[8,128]{1,0:T(8,128)} %get-tuple-element.49.top_ref, f32[8,128]{1,0:T(8,128)} %get-tuple-element.54.mass_ref, f32[1,1]{1,0:T(1,128)} %get-tuple-element.55.cross_ref, ...), custom_call_target="tpu_custom_call" | custom-call | tf_op jit(solution)/shard_map/pallas_call | solution.py:325
  132.6 1.9 collective-permute-done.25.more_ref
  134.6 1.1 copy-done.2
  135.7 7.8 %shard_map.94 = (f32[1024,384]{1,0:T(8,128)S(1)}, f32[512,384]{1,0:T(8,128)S(1)}, s16[528,384]{1,0:T(8,128)(2,1)S(1)}, s16[528,384]{1,0:T(8,128)(2,1)S(1)}, s16[...) custom-call(f32[1,1]{1,0:T(1,128)} %get-tuple-element.58.loss_ref, ...), custom_call_target="tpu_custom_call" | custom-call | tf_op jit(solution)/shard_map/pallas_call | solution.py:490
  143.5 2.7 %collective-permute-start.32 = (s16[528,384]{1,0:T(8,128)(2,1)S(1)}, s16[528,384]{1,0:T(8,128)(2,1)S(1)}, u32[]{:S(2)}, u32[]{:S(2)}) collective-permute-start(s16[528,384]{1,0:T(8,128)(2,1)S(1)} %get-tuple-element.70), channel_id=1, source_target_pairs={{0,6},{1,7},{2,0},{3,1},{4,2},{5,3},{6,4},{7,5},{8,14},{9,15},{10,... | collective-permute-start | bytes 1216520 | tf_op jit(solution)/shard_map/ppermute | solution.py:724
  146.3 3.2 %collective-permute-start.30 = (s16[528,384]{1,0:T(8,128)(2,1)S(1)}, s16[528,384]{1,0:T(8,128)(2,1)S(1)}, u32[]{:S(2)}, u32[]{:S(2)}) collective-permute-start(s16[528,384]{1,0:T(8,128)(2,1)S(1)} %get-tuple-element.67), channel_id=1, source_target_pairs={{0,6},{1,7},{2,0},{3,1},{4,2},{5,3},{6,4},{7,5},{8,14},{9,15},{10,... | collective-permute-start | bytes 1216520 | tf_op jit(solution)/shard_map/ppermute | solution.py:726
  149.5 6.5 %collective-permute-done.32.got_ref = s16[528,384]{1,0:T(8,128)(2,1)S(1)} collective-permute-done((s16[528,384]{1,0:T(8,128)(2,1)S(1)}, s16[528,384]{1,0:T(8,128)(2,1)S(1)}, u32[]{:S(2)}, u32[]{:S(2)}) %collective-permute-start.32) | collective-permute-done | bytes 405536 | tf_op jit(solution)/shard_map/ppermute | solution.py:724
  157.0 3.7 %collective-permute-start.33 = (s16[528,384]{1,0:T(8,128)(2,1)S(1)}, s16[528,384]{1,0:T(8,128)(2,1)S(1)}, u32[]{:S(2)}, u32[]{:S(2)}) collective-permute-start(s16[528,384]{1,0:T(8,128)(2,1)S(1)} %shard_map.96), channel_id=1, source_target_pairs={{0,6},{1,7},{2,0},{3,1},{4,2},{5,3},{6,4},{7,5},{8,14},{9,15},{10,... | collective-permute-start | bytes 1216520 | tf_op jit(solution)/shard_map/ppermute | solution.py:728
  161.8 2.9 %collective-permute-done.30.low_l = s16[528,384]{1,0:T(8,128)(2,1)S(1)} collective-permute-done((s16[528,384]{1,0:T(8,128)(2,1)S(1)}, s16[528,384]{1,0:T(8,128)(2,1)S(1)}, u32[]{:S(2)}, u32[]{:S(2)}) %collective-permute-start.30) | collective-permute-done | bytes 405536 | tf_op jit(solution)/shard_map/ppermute | solution.py:726
  164.7 3.7 %collective-permute-done.31.high_r = s16[528,384]{1,0:T(8,128)(2,1)S(1)} collective-permute-done((s16[528,384]{1,0:T(8,128)(2,1)S(1)}, s16[528,384]{1,0:T(8,128)(2,1)S(1)}, u32[]{:S(2)}, u32[]{:S(2)}) %collective-permute-start.31) | collective-permute-done | bytes 405536 | tf_op jit(solution)/shard_map/ppermute | solution.py:725
  168.4 4.2 %collective-permute-done.33.high_l = s16[528,384]{1,0:T(8,128)(2,1)S(1)} collective-permute-done((s16[528,384]{1,0:T(8,128)(2,1)S(1)}, s16[528,384]{1,0:T(8,128)(2,1)S(1)}, u32[]{:S(2)}, u32[]{:S(2)}) %collective-permute-start.33) | collective-permute-done | bytes 405536 | tf_op jit(solution)/shard_map/ppermute | solution.py:728
  172.6 3.4 %collective-permute-done.29.low_r = s16[528,384]{1,0:T(8,128)(2,1)S(1)} collective-permute-done((s16[528,384]{1,0:T(8,128)(2,1)S(1)}, s16[528,384]{1,0:T(8,128)(2,1)S(1)}, u32[]{:S(2)}, u32[]{:S(2)}) %collective-permute-start.29) | collective-permute-done | bytes 405536 | tf_op jit(solution)/shard_map/ppermute | solution.py:727
  176.0 3.1 %shard_map.97 = s16[32,112,128]{2,1,0:T(8,128)(2,1)} custom-call(f32[1,128]{1,0:T(1,128)S(1)} %get-tuple-element.63.loss_ref, f32[1024,384]{1,0:T(8,128)S(1)} %get-tuple-element.64.own_ref, s16[528,384]{1,0:T(8,128)(2,1)S(1)} %collective-permute-done.29.low_r, s16[528,384]{1,0:T(8,128)(2,1)S(1)} %collective-permute-done.30.low_l, ...), custom_call_target="tpu_custom_call" | custom-call | tf_op jit(solution)/shard_map/pallas_call | solution.py:566
  179.1 9.9 %all-to-all-start.2 = ((s16[32,112,128]{2,1,0:T(8,128)(2,1)}), s16[32,112,128]{2,1,0:T(8,128)(2,1)S(1)}, u32[]{:S(2)}, u32[]{:S(2)}) async-start(s16[32,112,128]{2,1,0:T(8,128)(2,1)} %shard_map.97), calls=%async_computation.2 | async-start | bytes 1835008 | tf_op jit(solution)/shard_map/all_to_all | solution.py:731
  190.3 1.9 copy-done.7
  192.2 1.9 copy-done.8
  194.1 9.2 %shard_map.93 = f32[9216,128]{1,0:T(8,128)} custom-call(s32[1]{0:T(128)} %bitcast.c_ref, bf16[1024,1536]{1,0:T(8,128)(2,1)S(1)} %bitcast.13, bf16[1024,1536]{1,0:T(8,128)(2,1)S(1)} %bitcast.14, bf16[1024,768]{1,0:T(8,128)(2,1)S(1)} %copy-done.9), custom_call_target="tpu_custom_call" | custom-call | flops 4831838208 | bytes 12582912 | tf_op jit(solution)/shard_map/pallas_call | solution.py:632
  203.3 10.1 %all-to-all-done.2.x_ref = s16[32,112,128]{2,1,0:T(8,128)(2,1)S(1)} async-done(((s16[32,112,128]{2,1,0:T(8,128)(2,1)}), s16[32,112,128]{2,1,0:T(8,128)(2,1)S(1)}, u32[]{:S(2)}, u32[]{:S(2)}) %all-to-all-start.2) | async-done | bytes 917536 | tf_op jit(solution)/shard_map/all_to_all | solution.py:731
  213.4 1.2 shard_map.98
  (104 shorter events, 18.0 us)
Async XLA Ops:
  1.6 19.6 %collective-permute-start = (bf16[32,1536]{1,0:T(8,128)(2,1)S(1)}, bf16[32,1536]{1,0:T(8,128)(2,1)S(1)}, u32[]{:S(2)}, u32[]{:S(2)}) collective-permute-start(bf16[32,1536]{1,0:T(8,128)(2,1)S(1)} %constant_dynamic-slice_fusion.refs_0_), channel_id=1, source_target_pairs={{0,32},{8,40},{16,48},{24,56},{32,64},{40,72},{48,80},{56,88},{64,... | collective-permute-start | bytes 294920 | tf_op jit(solution)/shard_map/ppermute | solution.py:683
  3.6 20.3 %collective-permute-start.1 = (bf16[32,1536]{1,0:T(8,128)(2,1)S(1)}, bf16[32,1536]{1,0:T(8,128)(2,1)S(1)}, u32[]{:S(2)}, u32[]{:S(2)}) collective-permute-start(bf16[32,1536]{1,0:T(8,128)(2,1)S(1)} %constant_dynamic-slice_fusion.refs_0_), channel_id=1, source_target_pairs={{0,64},{8,72},{16,80},{24,88},{32,96},{40,104},{48,112},{56,120},{... | collective-permute-start | bytes 294920 | tf_op jit(solution)/shard_map/ppermute | solution.py:683
  6.8 22.8 %collective-permute-start.2 = (bf16[32,1536]{1,0:T(8,128)(2,1)S(1)}, bf16[32,1536]{1,0:T(8,128)(2,1)S(1)}, u32[]{:S(2)}, u32[]{:S(2)}) collective-permute-start(bf16[32,1536]{1,0:T(8,128)(2,1)S(1)} %constant_dynamic-slice_fusion.refs_0_), channel_id=1, source_target_pairs={{0,96},{8,104},{16,112},{24,120},{32,128},{40,136},{48,144},{56,15... | collective-permute-start | bytes 294920 | tf_op jit(solution)/shard_map/ppermute | solution.py:683
  10.9 18.7 %collective-permute-start.3 = (bf16[32,1536]{1,0:T(8,128)(2,1)S(1)}, bf16[32,1536]{1,0:T(8,128)(2,1)S(1)}, u32[]{:S(2)}, u32[]{:S(2)}) collective-permute-start(bf16[32,1536]{1,0:T(8,128)(2,1)S(1)} %constant_dynamic-slice_fusion.refs_0_), channel_id=1, source_target_pairs={{0,128},{8,136},{16,144},{24,152},{32,160},{40,168},{48,176},{56,1... | collective-permute-start | bytes 294920 | tf_op jit(solution)/shard_map/ppermute | solution.py:683
  11.4 18.2 %collective-permute-start.4 = (bf16[32,1536]{1,0:T(8,128)(2,1)S(1)}, bf16[32,1536]{1,0:T(8,128)(2,1)S(1)}, u32[]{:S(2)}, u32[]{:S(2)}) collective-permute-start(bf16[32,1536]{1,0:T(8,128)(2,1)S(1)} %constant_dynamic-slice_fusion.refs_0_), channel_id=1, source_target_pairs={{0,160},{8,168},{16,176},{24,184},{32,192},{40,200},{48,208},{56,2... | collective-permute-start | bytes 294920 | tf_op jit(solution)/shard_map/ppermute | solution.py:683
  21.2 8.9 %collective-permute-start.5 = (bf16[32,1536]{1,0:T(8,128)(2,1)S(1)}, bf16[32,1536]{1,0:T(8,128)(2,1)S(1)}, u32[]{:S(2)}, u32[]{:S(2)}) collective-permute-start(bf16[32,1536]{1,0:T(8,128)(2,1)S(1)} %constant_dynamic-slice_fusion.refs_0_), channel_id=1, source_target_pairs={{0,192},{8,200},{16,208},{24,216},{32,224},{40,232},{48,240},{56,2... | collective-permute-start | bytes 294920 | tf_op jit(solution)/shard_map/ppermute | solution.py:683
  23.8 7.8 %collective-permute-start.6 = (bf16[32,1536]{1,0:T(8,128)(2,1)S(1)}, bf16[32,1536]{1,0:T(8,128)(2,1)S(1)}, u32[]{:S(2)}, u32[]{:S(2)}) collective-permute-start(bf16[32,1536]{1,0:T(8,128)(2,1)S(1)} %constant_dynamic-slice_fusion.refs_0_), channel_id=1, source_target_pairs={{0,224},{8,232},{16,240},{24,248},{32,0},{40,8},{48,16},{56,24},{6... | collective-permute-start | bytes 294920 | tf_op jit(solution)/shard_map/ppermute | solution.py:683
  31.8 48.6 %copy-start.3 = (bf16[4,32,1536]{2,1,0:T(8,128)(2,1)}, bf16[4,32,1536]{2,1,0:T(8,128)(2,1)S(1)}, u32[]{:S(2)}) copy-start(bf16[4,32,1536]{2,1,0:T(8,128)(2,1)S(1)} %get-tuple-element.41.refs_0_) | copy-start | bytes 1179652
  31.8 48.6 %copy-start.4 = (bf16[4,32,1536]{2,1,0:T(8,128)(2,1)}, bf16[4,32,1536]{2,1,0:T(8,128)(2,1)S(1)}, u32[]{:S(2)}) copy-start(bf16[4,32,1536]{2,1,0:T(8,128)(2,1)S(1)} %get-tuple-element.42.refs_1_) | copy-start | bytes 1179652
  31.9 12.1 %collective-permute-start.10 = (bf16[4,32,1536]{2,1,0:T(8,128)(2,1)S(1)}, bf16[4,32,1536]{2,1,0:T(8,128)(2,1)S(1)}, u32[]{:S(2)}, u32[]{:S(2)}) collective-permute-start(bf16[4,32,1536]{2,1,0:T(8,128)(2,1)S(1)} %get-tuple-element.42.refs_1_), channel_id=1, source_target_pairs={{0,24},{8,0},{16,8},{24,16},{32,56},{40,32},{48,40},{56,48},{64,88... | collective-permute-start | bytes 1179656 | tf_op jit(solution)/shard_map/ppermute | solution.py:698
  32.4 13.0 %collective-permute-start.7 = (bf16[4,32,1536]{2,1,0:T(8,128)(2,1)S(1)}, bf16[4,32,1536]{2,1,0:T(8,128)(2,1)S(1)}, u32[]{:S(2)}, u32[]{:S(2)}) collective-permute-start(bf16[4,32,1536]{2,1,0:T(8,128)(2,1)S(1)} %get-tuple-element.41.refs_0_), channel_id=1, source_target_pairs={{0,8},{8,16},{16,24},{24,0},{32,40},{40,48},{48,56},{56,32},{64,72... | collective-permute-start | bytes 1179656 | tf_op jit(solution)/shard_map/ppermute | solution.py:697
  34.0 17.4 %collective-permute-start.8 = (bf16[4,32,1536]{2,1,0:T(8,128)(2,1)S(1)}, bf16[4,32,1536]{2,1,0:T(8,128)(2,1)S(1)}, u32[]{:S(2)}, u32[]{:S(2)}) collective-permute-start(bf16[4,32,1536]{2,1,0:T(8,128)(2,1)S(1)} %get-tuple-element.42.refs_1_), channel_id=1, source_target_pairs={{0,8},{8,16},{16,24},{24,0},{32,40},{40,48},{48,56},{56,32},{64,72... | collective-permute-start | bytes 1179656 | tf_op jit(solution)/shard_map/ppermute | solution.py:699
  35.5 16.9 %collective-permute-start.12 = (bf16[4,32,1536]{2,1,0:T(8,128)(2,1)S(1)}, bf16[4,32,1536]{2,1,0:T(8,128)(2,1)S(1)}, u32[]{:S(2)}, u32[]{:S(2)}) collective-permute-start(bf16[4,32,1536]{2,1,0:T(8,128)(2,1)S(1)} %get-tuple-element.41.refs_0_), channel_id=1, source_target_pairs={{0,24},{8,0},{16,8},{24,16},{32,56},{40,32},{48,40},{56,48},{64,88... | collective-permute-start | bytes 1179656 | tf_op jit(solution)/shard_map/ppermute | solution.py:700
  36.0 16.4 %collective-permute-start.13 = (bf16[4,32,1536]{2,1,0:T(8,128)(2,1)S(1)}, bf16[4,32,1536]{2,1,0:T(8,128)(2,1)S(1)}, u32[]{:S(2)}, u32[]{:S(2)}) collective-permute-start(bf16[4,32,1536]{2,1,0:T(8,128)(2,1)S(1)} %get-tuple-element.41.refs_0_), channel_id=1, source_target_pairs={{0,1},{1,0},{2,3},{3,2},{4,5},{5,4},{6,7},{7,6},{8,9},{9,8},{10,11... | collective-permute-start | bytes 1179656 | tf_op jit(solution)/shard_map/ppermute | solution.py:704
  44.0 36.5 %copy-start.12 = (bf16[4,32,1536]{2,1,0:T(8,128)(2,1)}, bf16[4,32,1536]{2,1,0:T(8,128)(2,1)S(1)}, u32[]{:S(2)}) copy-start(bf16[4,32,1536]{2,1,0:T(8,128)(2,1)S(1)} %collective-permute-done.10.refs_7_) | copy-start | bytes 1179652
  44.0 8.9 %collective-permute-start.14 = (bf16[4,32,1536]{2,1,0:T(8,128)(2,1)S(1)}, bf16[4,32,1536]{2,1,0:T(8,128)(2,1)S(1)}, u32[]{:S(2)}, u32[]{:S(2)}) collective-permute-start(bf16[4,32,1536]{2,1,0:T(8,128)(2,1)S(1)} %get-tuple-element.42.refs_1_), channel_id=1, source_target_pairs={{0,1},{1,0},{2,3},{3,2},{4,5},{5,4},{6,7},{7,6},{8,9},{9,8},{10,11... | collective-permute-start | bytes 1179656 | tf_op jit(solution)/shard_map/ppermute | solution.py:704
  45.4 35.0 %copy-start.13 = (bf16[4,32,1536]{2,1,0:T(8,128)(2,1)}, bf16[4,32,1536]{2,1,0:T(8,128)(2,1)S(1)}, u32[]{:S(2)}) copy-start(bf16[4,32,1536]{2,1,0:T(8,128)(2,1)S(1)} %collective-permute-done.7.refs_2_) | copy-start | bytes 1179652
  45.4 12.9 %collective-permute-start.11 = (bf16[4,32,1536]{2,1,0:T(8,128)(2,1)S(1)}, bf16[4,32,1536]{2,1,0:T(8,128)(2,1)S(1)}, u32[]{:S(2)}, u32[]{:S(2)}) collective-permute-start(bf16[4,32,1536]{2,1,0:T(8,128)(2,1)S(1)} %collective-permute-done.10.refs_7_), channel_id=1, source_target_pairs={{0,24},{8,0},{16,8},{24,16},{32,56},{40,32},{48,40},{56,48},{64,88... | collective-permute-start | bytes 1179656 | tf_op jit(solution)/shard_map/ppermute | solution.py:702
  51.4 29.1 %copy-start.14 = (bf16[4,32,1536]{2,1,0:T(8,128)(2,1)}, bf16[4,32,1536]{2,1,0:T(8,128)(2,1)S(1)}, u32[]{:S(2)}) copy-start(bf16[4,32,1536]{2,1,0:T(8,128)(2,1)S(1)} %collective-permute-done.8.refs_3_) | copy-start | bytes 1179652
  51.4 8.6 %collective-permute-start.20 = (bf16[4,32,1536]{2,1,0:T(8,128)(2,1)S(1)}, bf16[4,32,1536]{2,1,0:T(8,128)(2,1)S(1)}, u32[]{:S(2)}, u32[]{:S(2)}) collective-permute-start(bf16[4,32,1536]{2,1,0:T(8,128)(2,1)S(1)} %collective-permute-done.10.refs_7_), channel_id=1, source_target_pairs={{0,1},{1,0},{2,3},{3,2},{4,5},{5,4},{6,7},{7,6},{8,9},{9,8},{10,11... | collective-permute-start | bytes 1179656 | tf_op jit(solution)/shard_map/ppermute | solution.py:704
  52.4 28.1 %copy-start.15 = (bf16[4,32,1536]{2,1,0:T(8,128)(2,1)}, bf16[4,32,1536]{2,1,0:T(8,128)(2,1)S(1)}, u32[]{:S(2)}) copy-start(bf16[4,32,1536]{2,1,0:T(8,128)(2,1)S(1)} %collective-permute-done.12.refs_6_) | copy-start | bytes 1179652
  52.4 7.5 %collective-permute-start.15 = (bf16[4,32,1536]{2,1,0:T(8,128)(2,1)S(1)}, bf16[4,32,1536]{2,1,0:T(8,128)(2,1)S(1)}, u32[]{:S(2)}, u32[]{:S(2)}) collective-permute-start(bf16[4,32,1536]{2,1,0:T(8,128)(2,1)S(1)} %collective-permute-done.7.refs_2_), channel_id=1, source_target_pairs={{0,1},{1,0},{2,3},{3,2},{4,5},{5,4},{6,7},{7,6},{8,9},{9,8},{10,11... | collective-permute-start | bytes 1179656 | tf_op jit(solution)/shard_map/ppermute | solution.py:704
  52.4 14.9 %copy-start.16 = (bf16[4,32,1536]{2,1,0:T(8,128)(2,1)}, bf16[4,32,1536]{2,1,0:T(8,128)(2,1)S(1)}, u32[]{:S(2)}) copy-start(bf16[4,32,1536]{2,1,0:T(8,128)(2,1)S(1)} %collective-permute-done.13.refs_8_) | copy-start | bytes 1179652
  52.4 7.5 %collective-permute-start.16 = (bf16[4,32,1536]{2,1,0:T(8,128)(2,1)S(1)}, bf16[4,32,1536]{2,1,0:T(8,128)(2,1)S(1)}, u32[]{:S(2)}, u32[]{:S(2)}) collective-permute-start(bf16[4,32,1536]{2,1,0:T(8,128)(2,1)S(1)} %collective-permute-done.8.refs_3_), channel_id=1, source_target_pairs={{0,1},{1,0},{2,3},{3,2},{4,5},{5,4},{6,7},{7,6},{8,9},{9,8},{10,11... | collective-permute-start | bytes 1179656 | tf_op jit(solution)/shard_map/ppermute | solution.py:704
  52.9 14.4 %copy-start.17 = (bf16[4,32,1536]{2,1,0:T(8,128)(2,1)}, bf16[4,32,1536]{2,1,0:T(8,128)(2,1)S(1)}, u32[]{:S(2)}) copy-start(bf16[4,32,1536]{2,1,0:T(8,128)(2,1)S(1)} %collective-permute-done.14.refs_9_) | copy-start | bytes 1179652
  52.9 7.0 %collective-permute-start.19 = (bf16[4,32,1536]{2,1,0:T(8,128)(2,1)S(1)}, bf16[4,32,1536]{2,1,0:T(8,128)(2,1)S(1)}, u32[]{:S(2)}, u32[]{:S(2)}) collective-permute-start(bf16[4,32,1536]{2,1,0:T(8,128)(2,1)S(1)} %collective-permute-done.12.refs_6_), channel_id=1, source_target_pairs={{0,1},{1,0},{2,3},{3,2},{4,5},{5,4},{6,7},{7,6},{8,9},{9,8},{10,11... | collective-permute-start | bytes 1179656 | tf_op jit(solution)/shard_map/ppermute | solution.py:704
  58.3 8.9 %collective-permute-start.9 = (bf16[4,32,1536]{2,1,0:T(8,128)(2,1)S(1)}, bf16[4,32,1536]{2,1,0:T(8,128)(2,1)}, u32[]{:S(2)}, u32[]{:S(2)}) collective-permute-start(bf16[4,32,1536]{2,1,0:T(8,128)(2,1)S(1)} %collective-permute-done.7.refs_2_), channel_id=1, source_target_pairs={{0,8},{8,16},{16,24},{24,0},{32,40},{40,48},{48,56},{56,32},{64,72... | collective-permute-start | bytes 1179656 | tf_op jit(solution)/shard_map/ppermute | solution.py:701
  67.3 36.8 %all-to-all-start = ((bf16[32,32,384]{2,1,0:T(8,128)(2,1)}), bf16[32,32,384]{2,1,0:T(8,128)(2,1)S(1)}, u32[]{:S(2)}, u32[]{:S(2)}) async-start(bf16[32,32,384]{2,1,0:T(8,128)(2,1)} %shard_map.85), calls=%async_computation | async-start | bytes 1572864 | tf_op jit(solution)/shard_map/all_to_all | solution.py:706
  77.7 2.0 collective-permute-start.17
  77.8 2.6 %collective-permute-start.18 = (bf16[4,32,1536]{2,1,0:T(8,128)(2,1)}, bf16[4,32,1536]{2,1,0:T(8,128)(2,1)}, u32[]{:S(2)}, u32[]{:S(2)}) collective-permute-start(bf16[4,32,1536]{2,1,0:T(8,128)(2,1)} %copy-done.18), channel_id=1, source_target_pairs={{0,1},{1,0},{2,3},{3,2},{4,5},{5,4},{6,7},{7,6},{8,9},{9,8},{10,11... | collective-permute-start | bytes 1179656 | tf_op jit(solution)/shard_map/ppermute | solution.py:704
  90.3 42.3 %collective-permute-start.27 = (bf16[384,1536]{1,0:T(8,128)(2,1)}, bf16[384,1536]{1,0:T(8,128)(2,1)S(1)}, u32[]{:S(2)}, u32[]{:S(2)}) collective-permute-start(bf16[384,1536]{1,0:T(8,128)(2,1)} %get-tuple-element.62), channel_id=1, source_target_pairs={{0,1},{1,0},{2,3},{3,2},{4,5},{5,4},{6,7},{7,6},{8,9},{9,8},{10,11... | collective-permute-start | bytes 3538952 | tf_op jit(solution)/shard_map/ppermute | solution.py:716
  90.5 2.9 %collective-permute-start.21 = (f32[8,128]{1,0:T(8,128)}, f32[8,128]{1,0:T(8,128)S(1)}, u32[]{:S(2)}, u32[]{:S(2)}) collective-permute-start(f32[8,128]{1,0:T(8,128)} %get-tuple-element.45.refs_0_), channel_id=1, source_target_pairs={{0,1},{1,0},{2,3},{3,2},{4,5},{5,4},{6,7},{7,6},{8,9},{9,8},{10,11... | collective-permute-start | bytes 12296 | tf_op jit(solution)/shard_map/ppermute | solution.py:709
  94.2 5.7 %collective-permute-start.22 = (f32[8,128]{1,0:T(8,128)S(1)}, f32[8,128]{1,0:T(8,128)S(1)}, u32[]{:S(2)}, u32[]{:S(2)}) collective-permute-start(f32[8,128]{1,0:T(8,128)S(1)} %shard_map.89.refs_0_), channel_id=1, source_target_pairs={{0,2},{1,3},{2,4},{3,5},{4,6},{5,7},{6,0},{7,1},{8,10},{9,11},{10,... | collective-permute-start | bytes 12296 | tf_op jit(solution)/shard_map/ppermute | solution.py:710
  95.7 5.1 %collective-permute-start.23 = (f32[8,128]{1,0:T(8,128)S(1)}, f32[8,128]{1,0:T(8,128)S(1)}, u32[]{:S(2)}, u32[]{:S(2)}) collective-permute-start(f32[8,128]{1,0:T(8,128)S(1)} %shard_map.89.refs_0_), channel_id=1, source_target_pairs={{0,4},{1,5},{2,6},{3,7},{4,0},{5,1},{6,2},{7,3},{8,12},{9,13},{10,... | collective-permute-start | bytes 12296 | tf_op jit(solution)/shard_map/ppermute | solution.py:710
  98.5 3.6 %collective-permute-start.24 = (f32[8,128]{1,0:T(8,128)S(1)}, f32[8,128]{1,0:T(8,128)S(1)}, u32[]{:S(2)}, u32[]{:S(2)}) collective-permute-start(f32[8,128]{1,0:T(8,128)S(1)} %shard_map.89.refs_0_), channel_id=1, source_target_pairs={{0,6},{1,7},{2,0},{3,1},{4,2},{5,3},{6,4},{7,5},{8,14},{9,15},{10,... | collective-permute-start | bytes 12296 | tf_op jit(solution)/shard_map/ppermute | solution.py:710
  104.1 19.2 %all-to-all-start.1 = ((f32[32,8,128]{2,1,0:T(8,128)}), f32[32,8,128]{2,1,0:T(8,128)S(1)}, u32[]{:S(2)}, u32[]{:S(2)}) async-start(f32[32,8,128]{2,1,0:T(8,128)} %shard_map.90), calls=%async_computation.1 | async-start | bytes 262144 | tf_op jit(solution)/shard_map/all_to_all | solution.py:713
  123.3 11.3 %copy-start.1 = (bf16[384,1536]{1,0:T(8,128)(2,1)S(1)}, bf16[384,1536]{1,0:T(8,128)(2,1)}, u32[]{:S(2)}) copy-start(bf16[384,1536]{1,0:T(8,128)(2,1)} %get-tuple-element.60.w_own) | copy-start | bytes 3538948
  132.0 2.6 %collective-permute-start.26 = (bf16[1024,384]{1,0:T(8,128)(2,1)}, bf16[1024,384]{1,0:T(8,128)(2,1)S(1)}, u32[]{:S(2)}, u32[]{:S(2)}) collective-permute-start(bf16[1024,384]{1,0:T(8,128)(2,1)} %get-tuple-element.59.own_ref), channel_id=1, source_target_pairs={{0,1},{1,0},{2,3},{3,2},{4,5},{5,4},{6,7},{7,6},{8,9},{9,8},{10,11... | collective-permute-start | bytes 2359304 | tf_op jit(solution)/shard_map/ppermute | solution.py:721
  132.1 2.4 %collective-permute-start.25 = (f32[1,1]{1,0:T(1,128)}, f32[1,1]{1,0:T(1,128)}, u32[]{:S(2)}, u32[]{:S(2)}) collective-permute-start(f32[1,1]{1,0:T(1,128)} %get-tuple-element.58.loss_ref), channel_id=1, source_target_pairs={{0,1},{1,0},{2,3},{3,2},{4,5},{5,4},{6,7},{7,6},{8,9},{9,8},{10,11... | collective-permute-start | bytes 20 | tf_op jit(solution)/shard_map/ppermute | solution.py:720
  143.5 12.5 %collective-permute-start.32 = (s16[528,384]{1,0:T(8,128)(2,1)S(1)}, s16[528,384]{1,0:T(8,128)(2,1)S(1)}, u32[]{:S(2)}, u32[]{:S(2)}) collective-permute-start(s16[528,384]{1,0:T(8,128)(2,1)S(1)} %get-tuple-element.70), channel_id=1, source_target_pairs={{0,6},{1,7},{2,0},{3,1},{4,2},{5,3},{6,4},{7,5},{8,14},{9,15},{10,... | collective-permute-start | bytes 1216520 | tf_op jit(solution)/shard_map/ppermute | solution.py:724
  146.3 14.5 %collective-permute-start.28 = (s16[528,384]{1,0:T(8,128)(2,1)S(1)}, s16[528,384]{1,0:T(8,128)(2,1)S(1)}, u32[]{:S(2)}, u32[]{:S(2)}) collective-permute-start(s16[528,384]{1,0:T(8,128)(2,1)S(1)} %get-tuple-element.66), channel_id=1, source_target_pairs={{0,2},{1,3},{2,4},{3,5},{4,6},{5,7},{6,0},{7,1},{8,10},{9,11},{10,... | collective-permute-start | bytes 1216520 | tf_op jit(solution)/shard_map/ppermute | solution.py:723
  146.3 18.4 %collective-permute-start.30 = (s16[528,384]{1,0:T(8,128)(2,1)S(1)}, s16[528,384]{1,0:T(8,128)(2,1)S(1)}, u32[]{:S(2)}, u32[]{:S(2)}) collective-permute-start(s16[528,384]{1,0:T(8,128)(2,1)S(1)} %get-tuple-element.67), channel_id=1, source_target_pairs={{0,6},{1,7},{2,0},{3,1},{4,2},{5,3},{6,4},{7,5},{8,14},{9,15},{10,... | collective-permute-start | bytes 1216520 | tf_op jit(solution)/shard_map/ppermute | solution.py:726
  149.5 18.9 %collective-permute-start.31 = (s16[528,384]{1,0:T(8,128)(2,1)S(1)}, s16[528,384]{1,0:T(8,128)(2,1)S(1)}, u32[]{:S(2)}, u32[]{:S(2)}) collective-permute-start(s16[528,384]{1,0:T(8,128)(2,1)S(1)} %get-tuple-element.68), channel_id=1, source_target_pairs={{0,2},{1,3},{2,4},{3,5},{4,6},{5,7},{6,0},{7,1},{8,10},{9,11},{10,... | collective-permute-start | bytes 1216520 | tf_op jit(solution)/shard_map/ppermute | solution.py:725
  157.0 15.6 %collective-permute-start.33 = (s16[528,384]{1,0:T(8,128)(2,1)S(1)}, s16[528,384]{1,0:T(8,128)(2,1)S(1)}, u32[]{:S(2)}, u32[]{:S(2)}) collective-permute-start(s16[528,384]{1,0:T(8,128)(2,1)S(1)} %shard_map.96), channel_id=1, source_target_pairs={{0,6},{1,7},{2,0},{3,1},{4,2},{5,3},{6,4},{7,5},{8,14},{9,15},{10,... | collective-permute-start | bytes 1216520 | tf_op jit(solution)/shard_map/ppermute | solution.py:728
  161.7 14.3 %collective-permute-start.29 = (s16[528,384]{1,0:T(8,128)(2,1)S(1)}, s16[528,384]{1,0:T(8,128)(2,1)S(1)}, u32[]{:S(2)}, u32[]{:S(2)}) collective-permute-start(s16[528,384]{1,0:T(8,128)(2,1)S(1)} %shard_map.95), channel_id=1, source_target_pairs={{0,2},{1,3},{2,4},{3,5},{4,6},{5,7},{6,0},{7,1},{8,10},{9,11},{10,... | collective-permute-start | bytes 1216520 | tf_op jit(solution)/shard_map/ppermute | solution.py:727
  179.1 9.9 %copy-start.27 = (s32[32]{0:T(128)S(1)}, s32[32]{0:T(128)}, u32[]{:S(2)}) copy-start(s32[32]{0:T(128)} %param.9) | copy-start | bytes 388
  179.1 11.2 %copy-start.9 = (bf16[1024,768]{1,0:T(8,128)(2,1)S(1)}, bf16[1024,768]{1,0:T(8,128)(2,1)}, u32[]{:S(2)}) copy-start(bf16[1024,768]{1,0:T(8,128)(2,1)} %get-tuple-element.57.sums_ref) | copy-start | bytes 4718596
  179.1 34.3 %all-to-all-start.2 = ((s16[32,112,128]{2,1,0:T(8,128)(2,1)}), s16[32,112,128]{2,1,0:T(8,128)(2,1)S(1)}, u32[]{:S(2)}, u32[]{:S(2)}) async-start(s16[32,112,128]{2,1,0:T(8,128)(2,1)} %shard_map.97), calls=%async_computation.2 | async-start | bytes 1835008 | tf_op jit(solution)/shard_map/all_to_all | solution.py:731
  (17 other events, 34.8 us)
where the time goes:
time: 217 us; the launch traced here: 216 us
  starting transfers between devices  75.4 us (35%)
  waiting for transfers between devices  65.1 us (30%)
  Pallas kernels  58.4 us (27%)
  local copies, waits for them, and re-layouts  10.4 us (5%)
  other arithmetic  3.76 us (2%)
  between operations  3.45 us (2%)
    ppermute x7, starting transfers between devices, on_device(): lax.ppermute(half, 'trainer', along_z(k))  18.5 us
    all_to_all x1, starting transfers between devices, on_device(): lax.all_to_all(split, 'trainer', split_axis=0, concat_axis=0, tiled=True)  10.4 us
    all_to_all x1, waiting for transfers between devices, on_device(): lax.all_to_all(packed, 'trainer', split_axis=0, concat_axis=0, tiled=True)  10.1 us
    all_to_all x1, starting transfers between devices, on_device(): lax.all_to_all(packed, 'trainer', split_axis=0, concat_axis=0, tiled=True)  9.91 us
    pallas_call x1, Pallas kernels, logits_and_stats(): pl.pallas_call(logit_kernel, out_shape=(table, table, jax.ShapeDtypeStruc...  9.78 us
    all_to_all x1, starting transfers between devices, on_device(): lax.all_to_all(stats, 'trainer', split_axis=0, concat_axis=0, tiled=True)  9.78 us
    unnamed x56, local copies, waits for them, and re-layouts  9.54 us
    pallas_call x1, Pallas kernels, select_rows(): pl.pallas_call(select_kernel, out_shape=(jax.ShapeDtypeStruct((ROWS, LOCA...  9.42 us
  transfers between devices with their start and end apart: 37, of which 21 were waited for; matrix products, arithmetic and copies ran while one was open for 2% of the time, Pallas kernels for 21%

commit v1 on v0

--- a/solution.py
+++ b/solution.py
@@ -49,31 +49,27 @@
 Y = 4
 
 
+PLACES = (((0, 0), (0, 4)), ((1, 0), (1, 8)), ((2, 0), (2, 4)), ((1, 12), (1, 4)))
+
+
 def order_kernel(z_ref, *refs):
-    pieces, outs = refs[:Z], refs[Z:]
-    for k, piece in enumerate(pieces):
-        at = lax.rem(z_ref[0] + Z - k, Z)
-        for side, out in enumerate(outs):
-
-            @pl.when(at // (Z // 2) == side)
-            def _():
-                out[lax.rem(at, Z // 2)] = piece[...]
+    for k, piece in enumerate(refs[:Z]):
+        refs[Z][lax.rem(z_ref[0] + Z - k, Z)] = piece[...]
 
 
 def in_order(z, pieces):
-    half = jax.ShapeDtypeStruct((Z // 2, SLOTS, HALF), BF16)
     return pl.pallas_call(
         order_kernel,
-        out_shape=(half, half),
+        out_shape=jax.ShapeDtypeStruct((Z, SLOTS, HALF), BF16),
         in_specs=[SMEM] + [VMEM] * Z,
-        out_specs=(VMEM, VMEM),
+        out_specs=VMEM,
         compiler_params=PARAMS,
     )(z, *pieces)
 
 
 def logit_kernel(at_ref, *refs):
-    pieces, refs = refs[:16], refs[16:]
-    far_ref, own_ref, other_ref, logits_ref, lse_ref, top_ref, *refs = refs
+    pieces, refs = refs[:6], refs[6:]
+    far_ref, table_ref, logits_ref, lse_ref, top_ref, *refs = refs
     tabs, w_ref, logit_buf, in_sems, out_sems = refs
     c, y = at_ref[0], at_ref[1]
     copies = [[], []]
@@ -85,62 +81,63 @@
         for dy in range(Y):
             y_at = lax.rem(y + Y - dy, Y)
             for high in range(2):
-                n = side * 8 + dy * 2 + high
+                which, first = PLACES[dy][high]
+                piece = pieces[side * 3 + which].at[pl.ds(first, Z // 2)]
                 place = tabs.at[side, pl.ds(high * (Z // 2), Z // 2), y_at]
-                copies[side].append(pltpu.make_async_copy(pieces[n], place, in_sems.at[n]))
+                sem = in_sems.at[side * 8 + dy * 2 + high]
+                copies[side].append(pltpu.make_async_copy(piece, place, sem))
         for copy in copies[side]:
             copy.start()
-    step = BLOCK // (Y * SLOTS)
+    block = 2 * BLOCK
+    step = block // (Y * SLOTS)
 
     def part(side, i):
-        block = tabs[side, pl.ds(i * step, step)].reshape(BLOCK, HALF)
-        return dot(block, w_ref[side])
+        rows = tabs[side, pl.ds(i * step, step)].reshape(block, HALF)
+        return dot(rows, w_ref[side])
 
     def store(i):
-        rows = pl.ds(pl.multiple_of(i * BLOCK, BLOCK), BLOCK)
+        rows = pl.ds(i * block, block)
         return pltpu.make_async_copy(logit_buf.at[rows], logits_ref.at[rows], out_sems.at[2 + i])
 
     stores = []
-    for side, out in enumerate((own_ref, other_ref)):
+    for side in range(2):
         for copy in copies[side]:
             copy.wait()
-        stores.append(pltpu.make_async_copy(tabs.at[side], out, out_sems.at[side]))
+        stores.append(
+            pltpu.make_async_copy(tabs.at[side], table_ref.at[side], out_sems.at[side])
+        )
         stores[-1].start()
-
-        @pl.loop(0, ROWS // BLOCK)
-        def _(i):
-            rows = pl.ds(pl.multiple_of(i * BLOCK, BLOCK), BLOCK)
+        for i in range(ROWS // block):
+            rows = pl.ds(i * block, block)
             if side == 0:
                 logit_buf[rows, :] = part(side, i)
-                return
+                continue
             logits = logit_buf[rows, :] + part(side, i)
             logit_buf[rows, :] = logits
             store(i).start()
             top = jnp.max(logits, axis=1, keepdims=True)
             lse = top + jnp.log(jnp.sum(jnp.exp(logits - top), axis=1, keepdims=True))
             for value, out in ((lse, lse_ref), (top, top_ref)):
-                flat = jnp.broadcast_to(value, (BLOCK, 128)).T
-                for j in range(BLOCK // 128):
+                flat = jnp.broadcast_to(value, (block, 128)).T
+                for j in range(block // 128):
                     row = flat[0:1, j * 128 : (j + 1) * 128]
-                    out[pl.ds(i * (BLOCK // 128) + j, 1), :] = row
-
-    for copy in stores + [store(i) for i in range(ROWS // BLOCK)]:
+                    out[pl.ds(i * (block // 128) + j, 1), :] = row
+
+    for copy in stores + [store(i) for i in range(ROWS // block)]:
         copy.wait()
 
 
 def logits_and_stats(at, pieces, weight):
-    table = jax.ShapeDtypeStruct((Z, Y, SLOTS, HALF), BF16)
-    own, other, logits, lse, top = pl.pallas_call(
+    table, logits, lse, top = pl.pallas_call(
         logit_kernel,
         out_shape=(
-            table,
-            table,
+            jax.ShapeDtypeStruct((2, Z, Y, SLOTS, HALF), BF16),
             jax.ShapeDtypeStruct((ROWS, LOCAL), F32),
             jax.ShapeDtypeStruct((8, 128), F32),
             jax.ShapeDtypeStruct((8, 128), F32),
         ),
-        in_specs=[SMEM] + [ANY] * 17,
-        out_specs=(ANY, ANY, ANY, VMEM, VMEM),
+        in_specs=[SMEM] + [ANY] * 7,
+        out_specs=(ANY, ANY, VMEM, VMEM),
         scratch_shapes=[
             pltpu.VMEM((2, Z, Y, SLOTS, HALF), BF16),
             pltpu.VMEM((2, HALF, LOCAL), BF16),
@@ -150,7 +147,7 @@
         ],
         compiler_params=FULL,
     )(at, *pieces, weight)
-    return own.reshape(ROWS, HALF), other.reshape(ROWS, HALF), logits, lse, top
+    return table.reshape(2, ROWS, HALF), logits, lse, top
 
 
 def merge(x):
@@ -283,10 +280,8 @@
     fetch.wait()
     fetch_targets.wait()
     lane = lax.broadcasted_iota(jnp.int32, (128, 128), 1).astype(F32)
-
-    @pl.loop(0, ROWS // 128)
-    def _(i):
-        rows = pl.ds(pl.multiple_of(i * 128, 128), 128)
+    for i in range(ROWS // 128):
+        rows = pl.ds(i * 128, 128)
         gid = column(gid_ref[:, rows])
         factor = column(live_ref[:, rows]) * scale
         found = jnp.zeros((128, 128), F32)
@@ -374,12 +369,10 @@
 
 
 def write_message(out_ref, block_of, loss, tail_ref):
-    @pl.loop(0, ROWS2 // 128)
-    def _(j):
+    for j in range(ROWS2 // 128):
         code, e = encode(block_of(j))
-        out_ref[pl.ds(pl.multiple_of(j * 128, 128), 128), :] = code
+        out_ref[pl.ds(j * 128, 128), :] = code
         tail_ref[pl.ds(j, 1), :] = e
-
     tail = [tail_ref[0 : ROWS2 // 128, :], loss, jnp.zeros((TAIL - ROWS2 // 128 - 1, 128), F32)]
     tail = jnp.concatenate(tail, axis=0)
     zeros = [jnp.zeros_like(tail)] * (LOCAL // 128 - 1)
@@ -409,7 +402,7 @@
 
 def read_message(ref, tail_ref, j):
     scale = power(column(tail_ref[pl.ds(j, 1), :]))
-    rows = pl.ds(pl.multiple_of(j * 128, 128), 128)
+    rows = pl.ds(j * 128, 128)
     parts = [from16(ref[rows, k * 128 : (k + 1) * 128]) * scale for k in range(LOCAL // 128)]
     return jnp.concatenate(parts, axis=1)
 
@@ -422,7 +415,7 @@
     c, x = at_ref[0], at_ref[1]
 
     def fetch(n):
-        source = all_ref.at[lax.rem(x + n % 4, 4), lax.rem(c + n // 4, 2)]
+        source = all_ref.at[lax.rem(x + (2, 1, 3, 0)[n % 4], 4), lax.rem(c + n // 4, 2)]
         return pltpu.make_async_copy(source, block_ref.at[n], sems.at[n])
 
     for n in range(8):
@@ -448,75 +441,92 @@
     )(at, blocks)
 
 
-def term_kernel(
-    loss_ref, more_ref, own_ref, other_ref, w_own, w_other, c0, l1, h1, l2, h2, l3, h3, sum_ref, *refs
-):
-    g_ref, w_ref, val_ref, tail_ref, sems = refs
-    fetches = [
+def fetch_pair(own_ref, other_ref, w_own, w_other, first, n, g_ref, w_ref, sems):
+    cols = pl.ds(first * LOCAL, n * LOCAL)
+    copies = [
         pltpu.make_async_copy(ref, g_ref.at[:, pl.ds(k * LOCAL, LOCAL)], sems.at[k])
         for k, ref in enumerate((own_ref, other_ref))
     ] + [
-        pltpu.make_async_copy(ref, w_ref.at[pl.ds(k * LOCAL, LOCAL)], sems.at[2 + k])
+        pltpu.make_async_copy(ref.at[:, cols], w_ref.at[pl.ds(k * LOCAL, LOCAL)], sems.at[2 + k])
         for k, ref in enumerate((w_own, w_other))
     ]
-    for fetch in fetches:
-        fetch.start()
+    for copy in copies:
+        copy.start()
+    return copies
+
+
+def far_kernel(
+    loss_ref, more_ref, own_ref, other_ref, w_own, w_other, low, high, sum_ref, *refs
+):
+    g_ref, w_ref, val_ref, tail_ref, sems = refs
+    copies = fetch_pair(own_ref, other_ref, w_own, w_other, 0, 1, g_ref, w_ref, sems)
     loss = encode_loss(jnp.full((1, 128), loss_ref[0, 0] + more_ref[0, 0], F32))
     sum_ref[...] = loss
-    for fetch in fetches:
-        fetch.wait()
-
-    @pl.loop(0, ROWS // BLOCK)
-    def _(i):
-        rows = pl.ds(pl.multiple_of(i * BLOCK, BLOCK), BLOCK)
-        val_ref[rows, :] = dot(g_ref[rows, :], w_ref[...])
-
-    c0[...] = val_ref[:, 0:LOCAL]
-    for i, k, out in ((0, 2, l2), (1, 2, h2), (1, 1, h1), (0, 3, l3), (0, 1, l1), (1, 3, h3)):
-        cols = slice(k * LOCAL, (k + 1) * LOCAL)
-        if out.dtype == F32:
-            out[...] = val_ref[i * ROWS2 : (i + 1) * ROWS2, cols]
-        else:
-
-            def block(j):
-                at = pl.multiple_of(i * ROWS2 + j * 128, 128)
-                return val_ref[pl.ds(at, 128), cols]
-
-            write_message(out, block, loss, tail_ref)
-
-
-def terms(loss, more, own, other, w_own, w_other):
-    part = jax.ShapeDtypeStruct((ROWS2, LOCAL), F32)
-    return pl.pallas_call(
-        term_kernel,
-        out_shape=(
-            jax.ShapeDtypeStruct((ROWS, LOCAL), F32),
-            part,
-            MESSAGE,
-            MESSAGE,
-            MESSAGE,
-            MESSAGE,
-            part,
-            jax.ShapeDtypeStruct((1, 128), F32),
-        ),
+    for copy in copies:
+        copy.wait()
+    for i, out in enumerate((low, high)):
+        val_ref[...] = dot(g_ref[pl.ds(i * ROWS2, ROWS2), :], w_ref[...])
+        write_message(out, lambda j: val_ref[pl.ds(j * 128, 128), :], loss, tail_ref)
+
+
+def near_kernel(
+    loss_ref, own_ref, other_ref, w_own, w_other, l1, h1, l3, h3, c0, g_ref, w_ref, val_ref, tail_ref, sems
+):
+    copies = fetch_pair(own_ref, other_ref, w_own, w_other, 1, 3, g_ref, w_ref, sems)
+    for copy in copies:
+        copy.wait()
+    for i in range(2):
+        rows = pl.ds(i * ROWS2, ROWS2)
+        val_ref[...] = dot(g_ref[rows, :], w_ref[...])
+        for k, out in enumerate(((l1, h1)[i], (l3, h3)[i])):
+            cols = slice(k * LOCAL, (k + 1) * LOCAL)
+            if out.dtype == F32:
+                out[...] = val_ref[:, cols]
+            else:
+                write_message(
+                    out, lambda j: val_ref[pl.ds(j * 128, 128), cols], loss_ref[...], tail_ref
+                )
+        c0[rows, :] = val_ref[:, 2 * LOCAL :]
+
+
+def pair_scratch(n):
+    return [
+        pltpu.VMEM((ROWS, 2 * LOCAL), BF16),
+        pltpu.VMEM((2 * LOCAL, n * LOCAL), BF16),
+        pltpu.VMEM((ROWS2, n * LOCAL), F32),
+        TAIL_REF,
+        pltpu.SemaphoreType.DMA((4,)),
+    ]
+
+
+def far_terms(loss, more, own, other, w_own, w_other):
+    return pl.pallas_call(
+        far_kernel,
+        out_shape=(MESSAGE, MESSAGE, jax.ShapeDtypeStruct((1, 128), F32)),
         in_specs=[SMEM, SMEM] + [ANY] * 4,
-        out_specs=(VMEM,) * 8,
-        scratch_shapes=[
-            pltpu.VMEM((ROWS, 2 * LOCAL), BF16),
-            pltpu.VMEM((2 * LOCAL, 4 * LOCAL), BF16),
-            pltpu.VMEM((ROWS, 4 * LOCAL), F32),
-            TAIL_REF,
-            pltpu.SemaphoreType.DMA((4,)),
-        ],
+        out_specs=(VMEM,) * 3,
+        scratch_shapes=pair_scratch(1),
         compiler_params=PARAMS,
     )(loss, more, own, other, w_own, w_other)
 
 
+def near_terms(loss, own, other, w_own, w_other):
+    part = jax.ShapeDtypeStruct((ROWS2, LOCAL), F32)
+    return pl.pallas_call(
+        near_kernel,
+        out_shape=(part, MESSAGE, MESSAGE, part, jax.ShapeDtypeStruct((ROWS, LOCAL), F32)),
+        in_specs=[VMEM] + [ANY] * 4,
+        out_specs=(VMEM,) * 5,
+        scratch_shapes=pair_scratch(3),
+        compiler_params=PARAMS,
+    )(loss, own, other, w_own, w_other)
+
+
 def relay_kernel(own_ref, got_ref, out_ref, got_tail, tail_ref):
     read_tail(got_ref, got_tail)
 
     def block(j):
-        rows = pl.ds(pl.multiple_of(j * 128, 128), 128)
+        rows = pl.ds(j * 128, 128)
         return own_ref[rows, :] + read_message(got_ref, got_tail, j)
 
     write_message(out_ref, block, tail_loss(got_tail), tail_ref)
@@ -546,11 +556,9 @@
     loss = encode_loss(jnp.broadcast_to(loss, (1, 128)))
     pad = jnp.zeros((TAIL - 2, 128), F32)
     for i in range(2):
-
-        @pl.loop(0, ROWS2 // 128)
-        def _(j):
+        for j in range(ROWS2 // 128):
             at = i * (ROWS2 // 128) + j
-            val = own_ref[pl.ds(pl.multiple_of(at * 128, 128), 128), :]
+            val = own_ref[pl.ds(at * 128, 128), :]
             got = [read_message(messages[n], tails[n], j) for n in (2 * i, 2 * i + 1)]
             code, e = encode(val + (got[0] + got[1]))
             tail = to16(jnp.concatenate([e, loss, pad], axis=0))
@@ -605,29 +613,17 @@
 HEAD_STEPS = HALF // HEAD_BLOCK
 
 
-def head_kernel(c_ref, own_ref, other_ref, sums_ref, o_ref):
-    i = pl.program_id(0)
-
-    def work(t_ref):
-        both = dot(t_ref[...], sums_ref[...], ((0,), (0,)))
-        both = both[:, 0:LOCAL] + both[:, LOCAL:]
-        for j in range(LOCAL // 128):
-            o_ref[pl.ds(j, HEAD_BLOCK, stride=LOCAL // 128), :] = both[:, j * 128 : (j + 1) * 128]
-
-    @pl.when(i < HEAD_STEPS)
-    def _():
-        work(own_ref)
-
-    @pl.when(i >= HEAD_STEPS)
-    def _():
-        work(other_ref)
-
-
-def head_gradient(c, own, other, sums):
+def head_kernel(c_ref, table_ref, sums_ref, o_ref):
+    both = dot(table_ref[0], sums_ref[...], ((0,), (0,)))
+    both = both[:, 0:LOCAL] + both[:, LOCAL:]
+    for j in range(LOCAL // 128):
+        o_ref[pl.ds(j, HEAD_BLOCK, stride=LOCAL // 128), :] = both[:, j * 128 : (j + 1) * 128]
+
+
+def head_gradient(c, table, sums):
     def place(i, c):
-        mine = i < HEAD_STEPS
-        side = jnp.where(mine, c[0], 1 - c[0])
-        return (side * HEAD_STEPS + jnp.where(mine, i, i - HEAD_STEPS), 0)
+        side = lax.rem(c[0] + i // HEAD_STEPS, 2)
+        return (side * HEAD_STEPS + i % HEAD_STEPS, 0)
 
     return pl.pallas_call(
         head_kernel,
@@ -635,8 +631,9 @@
             num_scalar_prefetch=1,
             grid=(2 * HEAD_STEPS,),
             in_specs=[
-                pl.BlockSpec((ROWS, HEAD_BLOCK), lambda i, c: (0, jnp.minimum(i, HEAD_STEPS - 1))),
-                pl.BlockSpec((ROWS, HEAD_BLOCK), lambda i, c: (0, jnp.maximum(i - HEAD_STEPS, 0))),
+                pl.BlockSpec(
+                    (1, ROWS, HEAD_BLOCK), lambda i, c: (i // HEAD_STEPS, 0, i % HEAD_STEPS)
+                ),
                 pl.BlockSpec((ROWS, 2 * LOCAL), lambda i, c: (0, 0)),
             ],
             out_specs=pl.BlockSpec((HEAD_BLOCK * LOCAL // 128, 128), place),
@@ -646,7 +643,7 @@
         cost_estimate=pl.CostEstimate(
             flops=4 * ROWS * D * LOCAL, bytes_accessed=12 * 1024 * 1024, transcendentals=0
         ),
-    )(c, own, other, sums)
+    )(c, table, sums)
 
 
 PAIR = [(i, i ^ 1) for i in range(SHARDS)]
@@ -682,51 +679,52 @@
     half = lax.dynamic_slice(hidden_table, (0, c * HALF), (SLOTS, HALF))
     near = [half] + [lax.ppermute(half, "trainer", along_z(k)) for k in range(1, Z)]
 
-    split = split_targets(targets[:, 0, :])
-
     gid = dest * SLOTS + token
     index = jnp.arange(ROWS, dtype=jnp.int32)
     live = (index % SLOTS < jnp.repeat(counts, SLOTS)).astype(F32).reshape(1, ROWS)
     gid = gid.astype(F32).reshape(1, ROWS)
 
-    w_own, w_give = turn_weights(at_cx, weight.reshape(4, 2, LOCAL, LOCAL))
-    z1, split, gid, live, w_own, w_give = lax.optimization_barrier(
-        (z1, split, gid, live, w_own, w_give)
-    )
-    low0, high0 = in_order(z1, near)
+    z1, gid, live = lax.optimization_barrier((z1, gid, live))
+    plane = in_order(z1, near)
+    low0, high0 = plane[: Z // 2], plane[Z // 2 :]
     low1 = lax.ppermute(low0, "trainer", along_y(1))
     high3 = lax.ppermute(high0, "trainer", along_y(-1))
     high1 = lax.ppermute(high0, "trainer", along_y(1))
     low3 = lax.ppermute(low0, "trainer", along_y(-1))
     low2 = lax.ppermute(low1, "trainer", along_y(1))
     high2 = lax.ppermute(high3, "trainer", along_y(-1))
-    pieces = (low0, high0, low1, high1, low2, high2, low3, high3)
-    pieces += tuple(lax.ppermute(p, "vocab", PAIR) for p in pieces)
-    split, _ = lax.optimization_barrier((split, (low2, high2) + pieces[8:12] + pieces[14:]))
+    at_cx, targets, _ = lax.optimization_barrier((at_cx, targets, low1))
+    split = split_targets(targets[:, 0, :])
+    w_own, w_give = turn_weights(at_cx, weight.reshape(4, 2, LOCAL, LOCAL))
+    high1, split, w_own, w_give = lax.optimization_barrier((high1, split, w_own, w_give))
+    pieces = [plane, jnp.concatenate([low1, high3, high1, low3]), jnp.concatenate([low2, high2])]
+    pieces += [lax.ppermute(p, "vocab", PAIR) for p in pieces]
+    split, _ = lax.optimization_barrier((split, (pieces[2], pieces[3], pieces[4])))
     probs = lax.all_to_all(split, "trainer", split_axis=0, concat_axis=0, tiled=True)
 
-    own, other, logits, stats, top = logits_and_stats(at_cy, pieces, weight)
+    table, logits, stats, top = logits_and_stats(at_cy, pieces, weight)
     stats = merge_stats([stats, lax.ppermute(stats, "vocab", PAIR)])
     stats = [stats] + [lax.ppermute(stats, "vocab", along_x(k)) for k in (1, 2, 3)]
     stats = merge_stats(stats, TRAINERS)
+    w_give, _ = lax.optimization_barrier((w_give, stats))
+    w_other = lax.ppermute(w_give, "vocab", PAIR)
     stats, probs = lax.optimization_barrier((stats, probs.reshape(ROWS, LOCAL)))
     stats = lax.all_to_all(stats, "trainer", split_axis=0, concat_axis=0, tiled=True)
 
-    w_give, _ = lax.optimization_barrier((w_give, top))
-    w_other = lax.ppermute(w_give, "vocab", PAIR)
     e, mass, cross = select_rows(top, logits, probs, gid, live)
     high, sums, loss = gradients(stats, top, mass, cross, e, probs, gid, live)
 
     more = lax.ppermute(loss, "vocab", PAIR)
     far = lax.ppermute(high, "vocab", PAIR)
-    t0, l1, h1, l2, h2, l3, h3, loss = terms(loss, more, high, far, w_own, w_other)
+    l2, h2, loss = far_terms(loss, more, high, far, w_own, w_other)
     low_r = lax.ppermute(l2, "vocab", RIGHT)
     high_l = lax.ppermute(h2, "vocab", LEFT)
+    l1, h1, l3, h3, t0 = near_terms(loss, high, far, w_own, w_other)
     high_r = lax.ppermute(h1, "vocab", RIGHT)
     low_l = lax.ppermute(l3, "vocab", LEFT)
     low_r = lax.ppermute(relay(l1, low_r), "vocab", RIGHT)
     high_l = lax.ppermute(relay(h3, high_l), "vocab", LEFT)
-    head = head_gradient(c1, own, other, sums)
+    head = head_gradient(c1, table, sums)
     packed = pack(loss, t0, low_r, low_l, high_r, high_l)
     packed = lax.all_to_all(packed, "trainer", split_axis=0, concat_axis=0, tiled=True)
     table_grad, loss = finish(lax.rem(trainer, 4).reshape(1).astype(jnp.int32), packed)

time: 217 us -> 208 us (0.959)
  Pallas kernels: 58.4 us -> 51.9 us
  starting transfers between devices: 75.4 us -> 71.7 us
  local copies, waits for them, and re-layouts: 10.4 us -> 13.7 us
  waiting for transfers between devices: 65.1 us -> 62.7 us
    ppermute x1, waiting for transfers between devices: 7.99 us -> 0.01 us  [on_device(): high3 = lax.ppermute(high0, 'trainer', along_y(-1))]
    ppermute x7, waiting for transfers between devices: 2.02 us -> 7.88 us  [on_device(): lax.ppermute(half, 'trainer', along_z(k))]
    ppermute x1, waiting for transfers between devices: 1.43 us -> 6.39 us  [on_device(): low1 = lax.ppermute(low0, 'trainer', along_y(1))]
    ppermute x1, waiting for transfers between devices: 5.29 us -> 0.57 us  [on_device(): high2 = lax.ppermute(high3, 'trainer', along_y(-1))]
    pallas_call x3 -> x4, Pallas kernels: 17.8 us -> 13.9 us  [the longest x1 8.51 us: logits_and_stats(): pl.pallas_call(logit_kernel, out_shape=(jax.ShapeDtypeStruct((2, Z, Y, SL...]
    ppermute x1, waiting for transfers between devices: 5.55 us -> 9.26 us  [on_device(): low2 = lax.ppermute(low1, 'trainer', along_y(1))]
    ppermute x1, waiting for transfers between devices: 6.5 us -> 3.86 us  [on_device(): high_l = lax.ppermute(h2, 'vocab', LEFT)]
    ppermute x1, waiting for transfers between devices: 2.71 us -> 0.36 us  [on_device(): high1 = lax.ppermute(high0, 'trainer', along_y(1))]
  transfers between devices with their start and end apart: 37 -> 32, of which waited for: 21 -> 21; matrix products, arithmetic and copies ran while one was open for 2% -> 3% of each run, Pallas kernels for 21% -> 22%
where the time goes in v1:
time: 208 us; the launch traced here: 207 us
  starting transfers between devices  71.7 us (34%)
  waiting for transfers between devices  62.7 us (30%)
  Pallas kernels  51.9 us (25%)
  local copies, waits for them, and re-layouts  13.7 us (7%)
  other arithmetic  3.71 us (2%)
  between operations  3.37 us (2%)
    ppermute x7, starting transfers between devices, on_device(): lax.ppermute(half, 'trainer', along_z(k))  18.5 us
    all_to_all x1, waiting for transfers between devices, on_device(): lax.all_to_all(packed, 'trainer', split_axis=0, concat_axis=0, tiled=True)  11.2 us
    unnamed x42, local copies, waits for them, and re-layouts  11.1 us
    all_to_all x1, starting transfers between devices, on_device(): lax.all_to_all(packed, 'trainer', split_axis=0, concat_axis=0, tiled=True)  9.91 us
    all_to_all x1, starting transfers between devices, on_device(): lax.all_to_all(stats, 'trainer', split_axis=0, concat_axis=0, tiled=True)  9.79 us
    pallas_call x1, Pallas kernels, select_rows(): pl.pallas_call(select_kernel, out_shape=(jax.ShapeDtypeStruct((ROWS, LOCA...  9.41 us
    all_to_all x1, starting transfers between devices, on_device(): lax.all_to_all(split, 'trainer', split_axis=0, concat_axis=0, tiled=True)  9.37 us
    ppermute x1, waiting for transfers between devices, on_device(): low2 = lax.ppermute(low1, 'trainer', along_y(1))  9.26 us
  transfers between devices with their start and end apart: 32, of which 21 were waited for; matrix products, arithmetic and copies ran while one was open for 3% of the time, Pallas kernels for 22%

profile of v1, /device:TPU:8, one launch (start us, length us, event | category | flops | bytes accessed | tf_op | source)
XLA Modules:
  0.0 207.1 jit_solution(14616915191075967811)
XLA Ops:
  1.6 2.0 collective-permute-start
  3.6 3.3 %collective-permute-start.1 = (bf16[32,1536]{1,0:T(8,128)(2,1)S(1)}, bf16[32,1536]{1,0:T(8,128)(2,1)S(1)}, u32[]{:S(2)}, u32[]{:S(2)}) collective-permute-start(bf16[32,1536]{1,0:T(8,128)(2,1)S(1)} %constant_dynamic-slice_fusion.refs_0_), channel_id=1, source_target_pairs={{0,64},{8,72},{16,80},{24,88},{32,96},{40,104},{48,112},{56,120},{... | collective-permute-start | bytes 294920 | tf_op jit(solution)/shard_map/ppermute | solution.py:680
  6.8 4.0 %collective-permute-start.2 = (bf16[32,1536]{1,0:T(8,128)(2,1)S(1)}, bf16[32,1536]{1,0:T(8,128)(2,1)S(1)}, u32[]{:S(2)}, u32[]{:S(2)}) collective-permute-start(bf16[32,1536]{1,0:T(8,128)(2,1)S(1)} %constant_dynamic-slice_fusion.refs_0_), channel_id=1, source_target_pairs={{0,96},{8,104},{16,112},{24,120},{32,128},{40,136},{48,144},{56,15... | collective-permute-start | bytes 294920 | tf_op jit(solution)/shard_map/ppermute | solution.py:680
  11.4 4.9 %collective-permute-start.4 = (bf16[32,1536]{1,0:T(8,128)(2,1)S(1)}, bf16[32,1536]{1,0:T(8,128)(2,1)S(1)}, u32[]{:S(2)}, u32[]{:S(2)}) collective-permute-start(bf16[32,1536]{1,0:T(8,128)(2,1)S(1)} %constant_dynamic-slice_fusion.refs_0_), channel_id=1, source_target_pairs={{0,160},{8,168},{16,176},{24,184},{32,192},{40,200},{48,208},{56,2... | collective-permute-start | bytes 294920 | tf_op jit(solution)/shard_map/ppermute | solution.py:680
  16.4 1.3 add_convert_fusion
  18.5 2.7 %collective-permute-start.5 = (bf16[32,1536]{1,0:T(8,128)(2,1)S(1)}, bf16[32,1536]{1,0:T(8,128)(2,1)S(1)}, u32[]{:S(2)}, u32[]{:S(2)}) collective-permute-start(bf16[32,1536]{1,0:T(8,128)(2,1)S(1)} %constant_dynamic-slice_fusion.refs_0_), channel_id=1, source_target_pairs={{0,192},{8,200},{16,208},{24,216},{32,224},{40,232},{48,240},{56,2... | collective-permute-start | bytes 294920 | tf_op jit(solution)/shard_map/ppermute | solution.py:680
  22.8 1.4 collective-permute-done.2.refs_3_
  24.2 4.1 %collective-permute-done.4.refs_5_ = bf16[32,1536]{1,0:T(8,128)(2,1)S(1)} collective-permute-done((bf16[32,1536]{1,0:T(8,128)(2,1)S(1)}, bf16[32,1536]{1,0:T(8,128)(2,1)S(1)}, u32[]{:S(2)}, u32[]{:S(2)}) %collective-permute-start.4) | collective-permute-done | bytes 98336 | tf_op jit(solution)/shard_map/ppermute | solution.py:680
  28.3 1.7 collective-permute-done.5.refs_6_
  30.8 1.0 fusion
  31.8 1.6 collective-permute-start.7
  33.4 1.3 collective-permute-start.9
  36.0 1.7 collective-permute-start.10
  37.7 6.4 %collective-permute-done.7 = bf16[4,32,1536]{2,1,0:T(8,128)(2,1)S(1)} collective-permute-done((bf16[4,32,1536]{2,1,0:T(8,128)(2,1)}, bf16[4,32,1536]{2,1,0:T(8,128)(2,1)S(1)}, u32[]{:S(2)}, u32[]{:S(2)}) %collective-permute-start.7) | collective-permute-done | bytes 393248 | tf_op jit(solution)/shard_map/ppermute | solution.py:690
  44.1 2.1 %shard_map.86 = bf16[32,32,384]{2,1,0:T(8,128)(2,1)} custom-call(bf16[32,12288]{1,0:T(8,128)(2,1)} %bitcast.17), custom_call_target="tpu_custom_call" | custom-call | tf_op jit(solution)/shard_map/pallas_call | solution.py:39
  46.2 4.1 %shard_map.87 = (bf16[384,1536]{1,0:T(8,128)(2,1)}, bf16[384,1536]{1,0:T(8,128)(2,1)}) custom-call(s32[2]{0:T(128)} %pad_add_fusion.1.at_ref, bf16[4,2,384,384]{3,2,1,0:T(8,128)(2,1)} %bitcast.13), custom_call_target="tpu_custom_call" | custom-call | tf_op jit(solution)/shard_map/pallas_call | solution.py:431
  53.1 1.2 collective-permute-start.11
  55.4 9.3 %collective-permute-done.11 = bf16[4,32,1536]{2,1,0:T(8,128)(2,1)S(1)} collective-permute-done((bf16[4,32,1536]{2,1,0:T(8,128)(2,1)S(1)}, bf16[4,32,1536]{2,1,0:T(8,128)(2,1)S(1)}, u32[]{:S(2)}, u32[]{:S(2)}) %collective-permute-start.11) | collective-permute-done | bytes 393248 | tf_op jit(solution)/shard_map/ppermute | solution.py:694
  67.7 9.4 %all-to-all-start = ((bf16[32,32,384]{2,1,0:T(8,128)(2,1)}), bf16[32,32,384]{2,1,0:T(8,128)(2,1)S(1)}, u32[]{:S(2)}, u32[]{:S(2)}) async-start(bf16[32,32,384]{2,1,0:T(8,128)(2,1)} %shard_map.86), calls=%async_computation | async-start | bytes 1572864 | tf_op jit(solution)/shard_map/all_to_all | solution.py:703
  77.7 1.9 collective-permute-done.15.refs_5_
  80.5 8.5 %shard_map.88 = (bf16[2,8,4,32,1536]{4,3,2,1,0:T(8,128)(2,1)}, f32[1024,384]{1,0:T(8,128)}, f32[8,128]{1,0:T(8,128)}, f32[8,128]{1,0:T(8,128)}) custom-call(s32[2]{0:T(128)} %pad_add_fusion.at_ref, bf16[8,32,1536]{2,1,0:T(8,128)(2,1)} %copy-done.1, bf16[16,32,1536]{2,1,0:T(8,128)(2,1)} %copy-done.9, ...), custom_call_target="tpu_custom_call" | custom-call | tf_op jit(solution)/shard_map/pallas_call | solution.py:131
  89.2 1.2 collective-permute-done.16.refs_1_
  91.2 1.6 collective-permute-start.17
  92.8 2.7 %collective-permute-start.18 = (f32[8,128]{1,0:T(8,128)S(1)}, f32[8,128]{1,0:T(8,128)S(1)}, u32[]{:S(2)}, u32[]{:S(2)}) collective-permute-start(f32[8,128]{1,0:T(8,128)S(1)} %shard_map.89.refs_0_), channel_id=1, source_target_pairs={{0,4},{1,5},{2,6},{3,7},{4,0},{5,1},{6,2},{7,3},{8,12},{9,13},{10,... | collective-permute-start | bytes 12296 | tf_op jit(solution)/shard_map/ppermute | solution.py:707
  95.5 1.4 collective-permute-start.19
  97.9 1.2 collective-permute-done.19.refs_3_
  99.7 1.4 shard_map.90
  101.1 9.8 %all-to-all-start.1 = ((f32[32,8,128]{2,1,0:T(8,128)}), f32[32,8,128]{2,1,0:T(8,128)S(1)}, u32[]{:S(2)}, u32[]{:S(2)}) async-start(f32[32,8,128]{2,1,0:T(8,128)} %shard_map.90), calls=%async_computation.1 | async-start | bytes 262144 | tf_op jit(solution)/shard_map/all_to_all | solution.py:712
  110.9 9.4 %shard_map.91 = (f32[1024,384]{1,0:T(8,128)}, f32[8,128]{1,0:T(8,128)}, f32[1,1]{1,0:T(1,128)}) custom-call(f32[8,128]{1,0:T(8,128)} %get-tuple-element.49.top_ref, f32[1024,384]{1,0:T(8,128)} %get-tuple-element.50.far_ref, bf16[1024,384]{1,0:T(8,128)(2,1)} %bitcast.15, f32[1,1024]{1,0:T(1,128)} %bitcast.18, f32[1,1024]{1,0:T(1,128)} %compare_convert_fusion.live_ref), custom_call_target="tpu_custom_call" | custom-call | flops 3221225472 | bytes 8388608 | tf_op jit(solution)/shard_map/pallas_call | solution.py:244
  121.0 7.3 %shard_map.92 = (bf16[1024,384]{1,0:T(8,128)(2,1)}, bf16[1024,768]{1,0:T(8,128)(2,1)}, f32[1,1]{1,0:T(1,128)}) custom-call(f32[32,8,128]{2,1,0:T(8,128)} %copy-done.12, f32[8,128]{1,0:T(8,128)} %get-tuple-element.49.top_ref, f32[8,128]{1,0:T(8,128)} %get-tuple-element.54.mass_ref, f32[1,1]{1,0:T(1,128)} %get-tuple-element.55.cross_ref, ...), custom_call_target="tpu_custom_call" | custom-call | tf_op jit(solution)/shard_map/pallas_call | solution.py:320
  128.9 1.9 collective-permute-done.20.more_ref
  130.9 1.1 copy-done.3
  132.0 2.8 %shard_map.94 = (s16[528,384]{1,0:T(8,128)(2,1)S(1)}, s16[528,384]{1,0:T(8,128)(2,1)S(1)}, f32[1,128]{1,0:T(1,128)S(1)}) custom-call(f32[1,1]{1,0:T(1,128)} %get-tuple-element.58.loss_ref, f32[1,1]{1,0:T(1,128)} %collective-permute-done.20.more_ref, bf16[1024,384]{1,0:T(8,128)(2,1)S(1)} %copy-done.3, ...), custom_call_target="tpu_custom_call" | custom-call | tf_op jit(solution)/shard_map/pallas_call | solution.py:503
  134.8 2.7 %collective-permute-start.27 = (s16[528,384]{1,0:T(8,128)(2,1)S(1)}, s16[528,384]{1,0:T(8,128)(2,1)S(1)}, u32[]{:S(2)}, u32[]{:S(2)}) collective-permute-start(s16[528,384]{1,0:T(8,128)(2,1)S(1)} %get-tuple-element.70), channel_id=1, source_target_pairs={{0,6},{1,7},{2,0},{3,1},{4,2},{5,3},{6,4},{7,5},{8,14},{9,15},{10,... | collective-permute-start | bytes 1216520 | tf_op jit(solution)/shard_map/ppermute | solution.py:721
  137.5 2.6 %shard_map.95 = (f32[512,384]{1,0:T(8,128)S(1)}, s16[528,384]{1,0:T(8,128)(2,1)S(1)}, s16[528,384]{1,0:T(8,128)(2,1)S(1)}, f32[512,384]{1,0:T(8,128)S(1)}, f32[1024,384]{1,0:T(8,128)S(1)}) custom-call(f32[1,128]{1,0:T(1,128)S(1)} %get-tuple-element.63.loss_ref, bf16[1024,384]{1,0:T(8,128)(2,1)S(1)} %copy-done.3, ...), custom_call_target="tpu_custom_call" | custom-call | tf_op jit(solution)/shard_map/pallas_call | solution.py:515
  140.1 3.3 %collective-permute-start.25 = (s16[528,384]{1,0:T(8,128)(2,1)S(1)}, s16[528,384]{1,0:T(8,128)(2,1)S(1)}, u32[]{:S(2)}, u32[]{:S(2)}) collective-permute-start(s16[528,384]{1,0:T(8,128)(2,1)S(1)} %get-tuple-element.67), channel_id=1, source_target_pairs={{0,6},{1,7},{2,0},{3,1},{4,2},{5,3},{6,4},{7,5},{8,14},{9,15},{10,... | collective-permute-start | bytes 1216520 | tf_op jit(solution)/shard_map/ppermute | solution.py:724
  143.4 3.9 %collective-permute-done.27.got_ref = s16[528,384]{1,0:T(8,128)(2,1)S(1)} collective-permute-done((s16[528,384]{1,0:T(8,128)(2,1)S(1)}, s16[528,384]{1,0:T(8,128)(2,1)S(1)}, u32[]{:S(2)}, u32[]{:S(2)}) %collective-permute-start.27) | collective-permute-done | bytes 405536 | tf_op jit(solution)/shard_map/ppermute | solution.py:721
  147.7 3.7 %collective-permute-start.28 = (s16[528,384]{1,0:T(8,128)(2,1)S(1)}, s16[528,384]{1,0:T(8,128)(2,1)S(1)}, u32[]{:S(2)}, u32[]{:S(2)}) collective-permute-start(s16[528,384]{1,0:T(8,128)(2,1)S(1)} %shard_map.97), channel_id=1, source_target_pairs={{0,6},{1,7},{2,0},{3,1},{4,2},{5,3},{6,4},{7,5},{8,14},{9,15},{10,... | collective-permute-start | bytes 1216520 | tf_op jit(solution)/shard_map/ppermute | solution.py:726
  151.9 4.1 %collective-permute-done.25.low_l = s16[528,384]{1,0:T(8,128)(2,1)S(1)} collective-permute-done((s16[528,384]{1,0:T(8,128)(2,1)S(1)}, s16[528,384]{1,0:T(8,128)(2,1)S(1)}, u32[]{:S(2)}, u32[]{:S(2)}) %collective-permute-start.25) | collective-permute-done | bytes 405536 | tf_op jit(solution)/shard_map/ppermute | solution.py:724
  156.0 3.7 %collective-permute-done.26.high_r = s16[528,384]{1,0:T(8,128)(2,1)S(1)} collective-permute-done((s16[528,384]{1,0:T(8,128)(2,1)S(1)}, s16[528,384]{1,0:T(8,128)(2,1)S(1)}, u32[]{:S(2)}, u32[]{:S(2)}) %collective-permute-start.26) | collective-permute-done | bytes 405536 | tf_op jit(solution)/shard_map/ppermute | solution.py:723
  159.7 4.2 %collective-permute-done.28.high_l = s16[528,384]{1,0:T(8,128)(2,1)S(1)} collective-permute-done((s16[528,384]{1,0:T(8,128)(2,1)S(1)}, s16[528,384]{1,0:T(8,128)(2,1)S(1)}, u32[]{:S(2)}, u32[]{:S(2)}) %collective-permute-start.28) | collective-permute-done | bytes 405536 | tf_op jit(solution)/shard_map/ppermute | solution.py:726
  163.9 3.4 %collective-permute-done.24.low_r = s16[528,384]{1,0:T(8,128)(2,1)S(1)} collective-permute-done((s16[528,384]{1,0:T(8,128)(2,1)S(1)}, s16[528,384]{1,0:T(8,128)(2,1)S(1)}, u32[]{:S(2)}, u32[]{:S(2)}) %collective-permute-start.24) | collective-permute-done | bytes 405536 | tf_op jit(solution)/shard_map/ppermute | solution.py:725
  167.3 2.4 %shard_map.98 = s16[32,112,128]{2,1,0:T(8,128)(2,1)} custom-call(f32[1,128]{1,0:T(1,128)S(1)} %get-tuple-element.63.loss_ref, f32[1024,384]{1,0:T(8,128)S(1)} %get-tuple-element.64.own_ref, s16[528,384]{1,0:T(8,128)(2,1)S(1)} %collective-permute-done.24.low_r, s16[528,384]{1,0:T(8,128)(2,1)S(1)} %collective-permute-done.25.low_l, ...), custom_call_target="tpu_custom_call" | custom-call | tf_op jit(solution)/shard_map/pallas_call | solution.py:574
  169.7 9.9 %all-to-all-start.2 = ((s16[32,112,128]{2,1,0:T(8,128)(2,1)}), s16[32,112,128]{2,1,0:T(8,128)(2,1)S(1)}, u32[]{:S(2)}, u32[]{:S(2)}) async-start(s16[32,112,128]{2,1,0:T(8,128)(2,1)} %shard_map.98), calls=%async_computation.2 | async-start | bytes 1835008 | tf_op jit(solution)/shard_map/all_to_all | solution.py:729
  180.9 2.8 %copy-done.6 = bf16[2,8,4,32,1536]{4,3,2,1,0:T(8,128)(2,1)S(1)} copy-done((bf16[2,8,4,32,1536]{4,3,2,1,0:T(8,128)(2,1)S(1)}, bf16[2,8,4,32,1536]{4,3,2,1,0:T(8,128)(2,1)}, u32[]{:S(2)}) %copy-start.6) | copy-done | bytes 6291480
  183.7 9.1 %shard_map.93 = f32[9216,128]{1,0:T(8,128)} custom-call(s32[1]{0:T(128)} %bitcast.c_ref, bf16[2,1024,1536]{2,1,0:T(8,128)(2,1)S(1)} %bitcast.12, bf16[1024,768]{1,0:T(8,128)(2,1)S(1)} %copy-done.7), custom_call_target="tpu_custom_call" | custom-call | flops 4831838208 | bytes 12582912 | tf_op jit(solution)/shard_map/pallas_call | solution.py:628
  192.8 11.2 %all-to-all-done.2.x_ref = s16[32,112,128]{2,1,0:T(8,128)(2,1)S(1)} async-done(((s16[32,112,128]{2,1,0:T(8,128)(2,1)}), s16[32,112,128]{2,1,0:T(8,128)(2,1)S(1)}, u32[]{:S(2)}, u32[]{:S(2)}) %all-to-all-start.2) | async-done | bytes 917536 | tf_op jit(solution)/shard_map/all_to_all | solution.py:729
  204.0 1.2 shard_map.99
  (84 shorter events, 19.7 us)
Async XLA Ops:
  0.6 0.9 copy-start
  1.6 16.9 %collective-permute-start = (bf16[32,1536]{1,0:T(8,128)(2,1)S(1)}, bf16[32,1536]{1,0:T(8,128)(2,1)S(1)}, u32[]{:S(2)}, u32[]{:S(2)}) collective-permute-start(bf16[32,1536]{1,0:T(8,128)(2,1)S(1)} %constant_dynamic-slice_fusion.refs_0_), channel_id=1, source_target_pairs={{0,32},{8,40},{16,48},{24,56},{32,64},{40,72},{48,80},{56,88},{64,... | collective-permute-start | bytes 294920 | tf_op jit(solution)/shard_map/ppermute | solution.py:680
  3.6 17.6 %collective-permute-start.1 = (bf16[32,1536]{1,0:T(8,128)(2,1)S(1)}, bf16[32,1536]{1,0:T(8,128)(2,1)S(1)}, u32[]{:S(2)}, u32[]{:S(2)}) collective-permute-start(bf16[32,1536]{1,0:T(8,128)(2,1)S(1)} %constant_dynamic-slice_fusion.refs_0_), channel_id=1, source_target_pairs={{0,64},{8,72},{16,80},{24,88},{32,96},{40,104},{48,112},{56,120},{... | collective-permute-start | bytes 294920 | tf_op jit(solution)/shard_map/ppermute | solution.py:680
  6.8 17.4 %collective-permute-start.2 = (bf16[32,1536]{1,0:T(8,128)(2,1)S(1)}, bf16[32,1536]{1,0:T(8,128)(2,1)S(1)}, u32[]{:S(2)}, u32[]{:S(2)}) collective-permute-start(bf16[32,1536]{1,0:T(8,128)(2,1)S(1)} %constant_dynamic-slice_fusion.refs_0_), channel_id=1, source_target_pairs={{0,96},{8,104},{16,112},{24,120},{32,128},{40,136},{48,144},{56,15... | collective-permute-start | bytes 294920 | tf_op jit(solution)/shard_map/ppermute | solution.py:680
  10.9 13.3 %collective-permute-start.3 = (bf16[32,1536]{1,0:T(8,128)(2,1)S(1)}, bf16[32,1536]{1,0:T(8,128)(2,1)S(1)}, u32[]{:S(2)}, u32[]{:S(2)}) collective-permute-start(bf16[32,1536]{1,0:T(8,128)(2,1)S(1)} %constant_dynamic-slice_fusion.refs_0_), channel_id=1, source_target_pairs={{0,128},{8,136},{16,144},{24,152},{32,160},{40,168},{48,176},{56,1... | collective-permute-start | bytes 294920 | tf_op jit(solution)/shard_map/ppermute | solution.py:680
  11.4 16.9 %collective-permute-start.4 = (bf16[32,1536]{1,0:T(8,128)(2,1)S(1)}, bf16[32,1536]{1,0:T(8,128)(2,1)S(1)}, u32[]{:S(2)}, u32[]{:S(2)}) collective-permute-start(bf16[32,1536]{1,0:T(8,128)(2,1)S(1)} %constant_dynamic-slice_fusion.refs_0_), channel_id=1, source_target_pairs={{0,160},{8,168},{16,176},{24,184},{32,192},{40,200},{48,208},{56,2... | collective-permute-start | bytes 294920 | tf_op jit(solution)/shard_map/ppermute | solution.py:680
  18.5 11.5 %collective-permute-start.5 = (bf16[32,1536]{1,0:T(8,128)(2,1)S(1)}, bf16[32,1536]{1,0:T(8,128)(2,1)S(1)}, u32[]{:S(2)}, u32[]{:S(2)}) collective-permute-start(bf16[32,1536]{1,0:T(8,128)(2,1)S(1)} %constant_dynamic-slice_fusion.refs_0_), channel_id=1, source_target_pairs={{0,192},{8,200},{16,208},{24,216},{32,224},{40,232},{48,240},{56,2... | collective-permute-start | bytes 294920 | tf_op jit(solution)/shard_map/ppermute | solution.py:680
  21.2 9.5 %collective-permute-start.6 = (bf16[32,1536]{1,0:T(8,128)(2,1)S(1)}, bf16[32,1536]{1,0:T(8,128)(2,1)S(1)}, u32[]{:S(2)}, u32[]{:S(2)}) collective-permute-start(bf16[32,1536]{1,0:T(8,128)(2,1)S(1)} %constant_dynamic-slice_fusion.refs_0_), channel_id=1, source_target_pairs={{0,224},{8,232},{16,240},{24,248},{32,0},{40,8},{48,16},{56,24},{6... | collective-permute-start | bytes 294920 | tf_op jit(solution)/shard_map/ppermute | solution.py:680
  30.7 23.5 %copy-start.1 = (bf16[8,32,1536]{2,1,0:T(8,128)(2,1)}, bf16[8,32,1536]{2,1,0:T(8,128)(2,1)S(1)}, u32[]{:S(2)}) copy-start(bf16[8,32,1536]{2,1,0:T(8,128)(2,1)S(1)} %shard_map.85.refs_0_) | copy-start | bytes 2359300
  31.8 12.3 %collective-permute-start.7 = (bf16[4,32,1536]{2,1,0:T(8,128)(2,1)}, bf16[4,32,1536]{2,1,0:T(8,128)(2,1)S(1)}, u32[]{:S(2)}, u32[]{:S(2)}) collective-permute-start(bf16[4,32,1536]{2,1,0:T(8,128)(2,1)} %get-tuple-element.77), channel_id=1, source_target_pairs={{0,8},{8,16},{16,24},{24,0},{32,40},{40,48},{48,56},{56,32},{64,72... | collective-permute-start | bytes 1179656 | tf_op jit(solution)/shard_map/ppermute | solution.py:690
  33.4 17.3 %collective-permute-start.9 = (bf16[4,32,1536]{2,1,0:T(8,128)(2,1)}, bf16[4,32,1536]{2,1,0:T(8,128)(2,1)S(1)}, u32[]{:S(2)}, u32[]{:S(2)}) collective-permute-start(bf16[4,32,1536]{2,1,0:T(8,128)(2,1)} %get-tuple-element.76), channel_id=1, source_target_pairs={{0,8},{8,16},{16,24},{24,0},{32,40},{40,48},{48,56},{56,32},{64,72... | collective-permute-start | bytes 1179656 | tf_op jit(solution)/shard_map/ppermute | solution.py:692
  34.7 16.8 %collective-permute-start.8 = (bf16[4,32,1536]{2,1,0:T(8,128)(2,1)}, bf16[4,32,1536]{2,1,0:T(8,128)(2,1)S(1)}, u32[]{:S(2)}, u32[]{:S(2)}) collective-permute-start(bf16[4,32,1536]{2,1,0:T(8,128)(2,1)} %get-tuple-element.76), channel_id=1, source_target_pairs={{0,24},{8,0},{16,8},{24,16},{32,56},{40,32},{48,40},{56,48},{64,88... | collective-permute-start | bytes 1179656 | tf_op jit(solution)/shard_map/ppermute | solution.py:691
  36.0 17.0 %collective-permute-start.10 = (bf16[4,32,1536]{2,1,0:T(8,128)(2,1)}, bf16[4,32,1536]{2,1,0:T(8,128)(2,1)S(1)}, u32[]{:S(2)}, u32[]{:S(2)}) collective-permute-start(bf16[4,32,1536]{2,1,0:T(8,128)(2,1)} %get-tuple-element.77), channel_id=1, source_target_pairs={{0,24},{8,0},{16,8},{24,16},{32,56},{40,32},{48,40},{56,48},{64,88... | collective-permute-start | bytes 1179656 | tf_op jit(solution)/shard_map/ppermute | solution.py:693
  50.7 0.8 copy-start.13
  51.4 1.0 copy-start.14
  53.0 14.7 %copy-start.9 = (bf16[16,32,1536]{2,1,0:T(8,128)(2,1)}, bf16[16,32,1536]{2,1,0:T(8,128)(2,1)S(1)}, u32[]{:S(2)}) copy-start(bf16[16,32,1536]{2,1,0:T(8,128)(2,1)S(1)} %constant_dynamic-update-slice_fusion.refs_1_) | copy-start | bytes 4718596
  53.0 14.6 %collective-permute-start.14 = (bf16[16,32,1536]{2,1,0:T(8,128)(2,1)S(1)}, bf16[16,32,1536]{2,1,0:T(8,128)(2,1)}, u32[]{:S(2)}, u32[]{:S(2)}) collective-permute-start(bf16[16,32,1536]{2,1,0:T(8,128)(2,1)S(1)} %constant_dynamic-update-slice_fusion.refs_1_), channel_id=1, source_target_pairs={{0,1},{1,0},{2,3},{3,2},{4,5},{5,4},{6,7},{7,6},{8,9},{9,8},{10,11... | collective-permute-start | bytes 4718600 | tf_op jit(solution)/shard_map/ppermute | solution.py:701
  53.1 11.5 %collective-permute-start.11 = (bf16[4,32,1536]{2,1,0:T(8,128)(2,1)S(1)}, bf16[4,32,1536]{2,1,0:T(8,128)(2,1)S(1)}, u32[]{:S(2)}, u32[]{:S(2)}) collective-permute-start(bf16[4,32,1536]{2,1,0:T(8,128)(2,1)S(1)} %collective-permute-done.7), channel_id=1, source_target_pairs={{0,8},{8,16},{16,24},{24,0},{32,40},{40,48},{48,56},{56,32},{64,72... | collective-permute-start | bytes 1179656 | tf_op jit(solution)/shard_map/ppermute | solution.py:694
  54.3 12.5 %collective-permute-start.13 = (bf16[8,32,1536]{2,1,0:T(8,128)(2,1)S(1)}, bf16[8,32,1536]{2,1,0:T(8,128)(2,1)S(1)}, u32[]{:S(2)}, u32[]{:S(2)}) collective-permute-start(bf16[8,32,1536]{2,1,0:T(8,128)(2,1)S(1)} %shard_map.85.refs_0_), channel_id=1, source_target_pairs={{0,1},{1,0},{2,3},{3,2},{4,5},{5,4},{6,7},{7,6},{8,9},{9,8},{10,11... | collective-permute-start | bytes 2359304 | tf_op jit(solution)/shard_map/ppermute | solution.py:701
  54.4 11.6 %collective-permute-start.12 = (bf16[4,32,1536]{2,1,0:T(8,128)(2,1)S(1)}, bf16[4,32,1536]{2,1,0:T(8,128)(2,1)S(1)}, u32[]{:S(2)}, u32[]{:S(2)}) collective-permute-start(bf16[4,32,1536]{2,1,0:T(8,128)(2,1)S(1)} %collective-permute-done.8), channel_id=1, source_target_pairs={{0,24},{8,0},{16,8},{24,16},{32,56},{40,32},{48,40},{56,48},{64,88... | collective-permute-start | bytes 1179656 | tf_op jit(solution)/shard_map/ppermute | solution.py:695
  66.8 0.9 copy-start.10
  67.7 33.4 %all-to-all-start = ((bf16[32,32,384]{2,1,0:T(8,128)(2,1)}), bf16[32,32,384]{2,1,0:T(8,128)(2,1)S(1)}, u32[]{:S(2)}, u32[]{:S(2)}) async-start(bf16[32,32,384]{2,1,0:T(8,128)(2,1)} %shard_map.86), calls=%async_computation | async-start | bytes 1572864 | tf_op jit(solution)/shard_map/all_to_all | solution.py:703
  77.0 2.6 %collective-permute-start.15 = (bf16[8,32,1536]{2,1,0:T(8,128)(2,1)}, bf16[8,32,1536]{2,1,0:T(8,128)(2,1)S(1)}, u32[]{:S(2)}, u32[]{:S(2)}) collective-permute-start(bf16[8,32,1536]{2,1,0:T(8,128)(2,1)} %constant_dynamic-update-slice_fusion.4.refs_2_), channel_id=1, source_target_pairs={{0,1},{1,0},{2,3},{3,2},{4,5},{5,4},{6,7},{7,6},{8,9},{9,8},{10,11... | collective-permute-start | bytes 2359304 | tf_op jit(solution)/shard_map/ppermute | solution.py:701
  79.6 0.9 copy-start.11
  89.0 1.5 collective-permute-start.16
  91.2 7.9 %copy-start.4 = (f32[8,128]{1,0:T(8,128)}, f32[8,128]{1,0:T(8,128)S(1)}, u32[]{:S(2)}) copy-start(f32[8,128]{1,0:T(8,128)S(1)} %shard_map.89.refs_0_) | copy-start | bytes 12292
  91.2 5.7 %collective-permute-start.17 = (f32[8,128]{1,0:T(8,128)S(1)}, f32[8,128]{1,0:T(8,128)S(1)}, u32[]{:S(2)}, u32[]{:S(2)}) collective-permute-start(f32[8,128]{1,0:T(8,128)S(1)} %shard_map.89.refs_0_), channel_id=1, source_target_pairs={{0,2},{1,3},{2,4},{3,5},{4,6},{5,7},{6,0},{7,1},{8,10},{9,11},{10,... | collective-permute-start | bytes 12296 | tf_op jit(solution)/shard_map/ppermute | solution.py:707
  92.8 5.1 %collective-permute-start.18 = (f32[8,128]{1,0:T(8,128)S(1)}, f32[8,128]{1,0:T(8,128)S(1)}, u32[]{:S(2)}, u32[]{:S(2)}) collective-permute-start(f32[8,128]{1,0:T(8,128)S(1)} %shard_map.89.refs_0_), channel_id=1, source_target_pairs={{0,4},{1,5},{2,6},{3,7},{4,0},{5,1},{6,2},{7,3},{8,12},{9,13},{10,... | collective-permute-start | bytes 12296 | tf_op jit(solution)/shard_map/ppermute | solution.py:707
  95.5 3.6 %collective-permute-start.19 = (f32[8,128]{1,0:T(8,128)S(1)}, f32[8,128]{1,0:T(8,128)S(1)}, u32[]{:S(2)}, u32[]{:S(2)}) collective-permute-start(f32[8,128]{1,0:T(8,128)S(1)} %shard_map.89.refs_0_), channel_id=1, source_target_pairs={{0,6},{1,7},{2,0},{3,1},{4,2},{5,3},{6,4},{7,5},{8,14},{9,15},{10,... | collective-permute-start | bytes 12296 | tf_op jit(solution)/shard_map/ppermute | solution.py:707
  96.9 2.2 %copy-start.15 = (f32[8,128]{1,0:T(8,128)}, f32[8,128]{1,0:T(8,128)S(1)}, u32[]{:S(2)}) copy-start(f32[8,128]{1,0:T(8,128)S(1)} %collective-permute-done.17.refs_1_) | copy-start | bytes 12292
  97.9 1.2 copy-start.16
  101.1 27.8 %collective-permute-start.22 = (bf16[384,1536]{1,0:T(8,128)(2,1)}, bf16[384,1536]{1,0:T(8,128)(2,1)S(1)}, u32[]{:S(2)}, u32[]{:S(2)}) collective-permute-start(bf16[384,1536]{1,0:T(8,128)(2,1)} %get-tuple-element.62), channel_id=1, source_target_pairs={{0,1},{1,0},{2,3},{3,2},{4,5},{5,4},{6,7},{7,6},{8,9},{9,8},{10,11... | collective-permute-start | bytes 3538952 | tf_op jit(solution)/shard_map/ppermute | solution.py:710
  101.1 9.8 %copy-start.8 = (bf16[32,32,384]{2,1,0:T(8,128)(2,1)}, bf16[32,32,384]{2,1,0:T(8,128)(2,1)S(1)}, u32[]{:S(2)}) copy-start(bf16[32,32,384]{2,1,0:T(8,128)(2,1)S(1)} %all-to-all-done) | copy-start | bytes 2359300
  101.1 19.2 %all-to-all-start.1 = ((f32[32,8,128]{2,1,0:T(8,128)}), f32[32,8,128]{2,1,0:T(8,128)S(1)}, u32[]{:S(2)}, u32[]{:S(2)}) async-start(f32[32,8,128]{2,1,0:T(8,128)} %shard_map.90), calls=%async_computation.1 | async-start | bytes 262144 | tf_op jit(solution)/shard_map/all_to_all | solution.py:712
  120.3 10.5 %copy-start.2 = (bf16[384,1536]{1,0:T(8,128)(2,1)S(1)}, bf16[384,1536]{1,0:T(8,128)(2,1)}, u32[]{:S(2)}) copy-start(bf16[384,1536]{1,0:T(8,128)(2,1)} %get-tuple-element.60.w_own) | copy-start | bytes 3538948
  128.3 2.6 %collective-permute-start.21 = (bf16[1024,384]{1,0:T(8,128)(2,1)}, bf16[1024,384]{1,0:T(8,128)(2,1)S(1)}, u32[]{:S(2)}, u32[]{:S(2)}) collective-permute-start(bf16[1024,384]{1,0:T(8,128)(2,1)} %get-tuple-element.59.own_ref), channel_id=1, source_target_pairs={{0,1},{1,0},{2,3},{3,2},{4,5},{5,4},{6,7},{7,6},{8,9},{9,8},{10,11... | collective-permute-start | bytes 2359304 | tf_op jit(solution)/shard_map/ppermute | solution.py:718
  128.4 2.4 %collective-permute-start.20 = (f32[1,1]{1,0:T(1,128)}, f32[1,1]{1,0:T(1,128)}, u32[]{:S(2)}, u32[]{:S(2)}) collective-permute-start(f32[1,1]{1,0:T(1,128)} %get-tuple-element.58.loss_ref), channel_id=1, source_target_pairs={{0,1},{1,0},{2,3},{3,2},{4,5},{5,4},{6,7},{7,6},{8,9},{9,8},{10,11... | collective-permute-start | bytes 20 | tf_op jit(solution)/shard_map/ppermute | solution.py:717
  130.9 1.1 copy-start.3
  134.8 12.5 %collective-permute-start.27 = (s16[528,384]{1,0:T(8,128)(2,1)S(1)}, s16[528,384]{1,0:T(8,128)(2,1)S(1)}, u32[]{:S(2)}, u32[]{:S(2)}) collective-permute-start(s16[528,384]{1,0:T(8,128)(2,1)S(1)} %get-tuple-element.70), channel_id=1, source_target_pairs={{0,6},{1,7},{2,0},{3,1},{4,2},{5,3},{6,4},{7,5},{8,14},{9,15},{10,... | collective-permute-start | bytes 1216520 | tf_op jit(solution)/shard_map/ppermute | solution.py:721
  137.5 13.9 %collective-permute-start.23 = (s16[528,384]{1,0:T(8,128)(2,1)S(1)}, s16[528,384]{1,0:T(8,128)(2,1)S(1)}, u32[]{:S(2)}, u32[]{:S(2)}) collective-permute-start(s16[528,384]{1,0:T(8,128)(2,1)S(1)} %get-tuple-element.66), channel_id=1, source_target_pairs={{0,2},{1,3},{2,4},{3,5},{4,6},{5,7},{6,0},{7,1},{8,10},{9,11},{10,... | collective-permute-start | bytes 1216520 | tf_op jit(solution)/shard_map/ppermute | solution.py:720
  140.1 15.9 %collective-permute-start.25 = (s16[528,384]{1,0:T(8,128)(2,1)S(1)}, s16[528,384]{1,0:T(8,128)(2,1)S(1)}, u32[]{:S(2)}, u32[]{:S(2)}) collective-permute-start(s16[528,384]{1,0:T(8,128)(2,1)S(1)} %get-tuple-element.67), channel_id=1, source_target_pairs={{0,6},{1,7},{2,0},{3,1},{4,2},{5,3},{6,4},{7,5},{8,14},{9,15},{10,... | collective-permute-start | bytes 1216520 | tf_op jit(solution)/shard_map/ppermute | solution.py:724
  143.4 16.3 %collective-permute-start.26 = (s16[528,384]{1,0:T(8,128)(2,1)S(1)}, s16[528,384]{1,0:T(8,128)(2,1)S(1)}, u32[]{:S(2)}, u32[]{:S(2)}) collective-permute-start(s16[528,384]{1,0:T(8,128)(2,1)S(1)} %get-tuple-element.68), channel_id=1, source_target_pairs={{0,2},{1,3},{2,4},{3,5},{4,6},{5,7},{6,0},{7,1},{8,10},{9,11},{10,... | collective-permute-start | bytes 1216520 | tf_op jit(solution)/shard_map/ppermute | solution.py:723
  147.7 16.2 %collective-permute-start.28 = (s16[528,384]{1,0:T(8,128)(2,1)S(1)}, s16[528,384]{1,0:T(8,128)(2,1)S(1)}, u32[]{:S(2)}, u32[]{:S(2)}) collective-permute-start(s16[528,384]{1,0:T(8,128)(2,1)S(1)} %shard_map.97), channel_id=1, source_target_pairs={{0,6},{1,7},{2,0},{3,1},{4,2},{5,3},{6,4},{7,5},{8,14},{9,15},{10,... | collective-permute-start | bytes 1216520 | tf_op jit(solution)/shard_map/ppermute | solution.py:726
  151.9 15.4 %collective-permute-start.24 = (s16[528,384]{1,0:T(8,128)(2,1)S(1)}, s16[528,384]{1,0:T(8,128)(2,1)S(1)}, u32[]{:S(2)}, u32[]{:S(2)}) collective-permute-start(s16[528,384]{1,0:T(8,128)(2,1)S(1)} %shard_map.96), channel_id=1, source_target_pairs={{0,2},{1,3},{2,4},{3,5},{4,6},{5,7},{6,0},{7,1},{8,10},{9,11},{10,... | collective-permute-start | bytes 1216520 | tf_op jit(solution)/shard_map/ppermute | solution.py:725
  169.7 9.9 %copy-start.18 = (s32[32]{0:T(128)S(1)}, s32[32]{0:T(128)}, u32[]{:S(2)}) copy-start(s32[32]{0:T(128)} %param.9) | copy-start | bytes 388
  169.7 11.2 %copy-start.7 = (bf16[1024,768]{1,0:T(8,128)(2,1)S(1)}, bf16[1024,768]{1,0:T(8,128)(2,1)}, u32[]{:S(2)}) copy-start(bf16[1024,768]{1,0:T(8,128)(2,1)} %get-tuple-element.57.sums_ref) | copy-start | bytes 4718596
  169.7 34.3 %all-to-all-start.2 = ((s16[32,112,128]{2,1,0:T(8,128)(2,1)}), s16[32,112,128]{2,1,0:T(8,128)(2,1)S(1)}, u32[]{:S(2)}, u32[]{:S(2)}) async-start(s16[32,112,128]{2,1,0:T(8,128)(2,1)} %shard_map.98), calls=%async_computation.2 | async-start | bytes 1835008 | tf_op jit(solution)/shard_map/all_to_all | solution.py:729
  180.9 2.8 %copy-start.6 = (bf16[2,8,4,32,1536]{4,3,2,1,0:T(8,128)(2,1)S(1)}, bf16[2,8,4,32,1536]{4,3,2,1,0:T(8,128)(2,1)}, u32[]{:S(2)}) copy-start(bf16[2,8,4,32,1536]{4,3,2,1,0:T(8,128)(2,1)} %get-tuple-element.44) | copy-start | bytes 18874372
  (3 other events, 1.9 us)

commit v2 on v1

--- a/solution.py
+++ b/solution.py
@@ -677,7 +677,12 @@
     weight = head_weight[:, 0, :]
 
     half = lax.dynamic_slice(hidden_table, (0, c * HALF), (SLOTS, HALF))
-    near = [half] + [lax.ppermute(half, "trainer", along_z(k)) for k in range(1, Z)]
+    near = [half] + [lax.ppermute(half, "trainer", along_z(k)) for k in (1, 2, -2, -1)]
+    near[3:3] = [
+        lax.ppermute(near[2], "trainer", along_z(1)),
+        lax.ppermute(near[2], "trainer", along_z(2)),
+        lax.ppermute(near[3], "trainer", along_z(-1)),
+    ]
 
     gid = dest * SLOTS + token
     index = jnp.arange(ROWS, dtype=jnp.int32)
@@ -693,11 +698,12 @@
     low3 = lax.ppermute(low0, "trainer", along_y(-1))
     low2 = lax.ppermute(low1, "trainer", along_y(1))
     high2 = lax.ppermute(high3, "trainer", along_y(-1))
-    at_cx, targets, _ = lax.optimization_barrier((at_cx, targets, low1))
+    middle = jnp.concatenate([low1, high3, high1, low3])
+    at_cx, targets, _ = lax.optimization_barrier((at_cx, targets, middle))
     split = split_targets(targets[:, 0, :])
     w_own, w_give = turn_weights(at_cx, weight.reshape(4, 2, LOCAL, LOCAL))
-    high1, split, w_own, w_give = lax.optimization_barrier((high1, split, w_own, w_give))
-    pieces = [plane, jnp.concatenate([low1, high3, high1, low3]), jnp.concatenate([low2, high2])]
+    low2, split, w_own, w_give = lax.optimization_barrier((low2, split, w_own, w_give))
+    pieces = [plane, middle, jnp.concatenate([low2, high2])]
     pieces += [lax.ppermute(p, "vocab", PAIR) for p in pieces]
     split, _ = lax.optimization_barrier((split, (pieces[2], pieces[3], pieces[4])))
     probs = lax.all_to_all(split, "trainer", split_axis=0, concat_axis=0, tiled=True)

time: 208 us -> 197 us (0.947)
  starting transfers between devices: 71.7 us -> 66.2 us
  waiting for transfers between devices: 62.7 us -> 58.4 us
    ppermute x7 -> x4, starting transfers between devices: 18.5 us -> 9.7 us  [on_device(): lax.ppermute(half, 'trainer', along_z(k))]
    ppermute x7 -> x4, waiting for transfers between devices: 7.88 us -> 0.01 us  [on_device(): lax.ppermute(half, 'trainer', along_z(k))]
    ppermute x1, waiting for transfers between devices: 9.26 us -> 2.33 us  [on_device(): low2 = lax.ppermute(low1, 'trainer', along_y(1))]
    ppermute x0 -> x3, waiting for transfers between devices: none -> 4.53 us  [the longest x1 2.69 us: on_device(): lax.ppermute(near[2], 'trainer', along_z(1))]
    ppermute x0 -> x3, starting transfers between devices: none -> 3.68 us  [the longest x1 1.88 us: on_device(): lax.ppermute(near[2], 'trainer', along_z(2))]
    ppermute x1, waiting for transfers between devices: 0.36 us -> 2.91 us  [on_device(): high1 = lax.ppermute(high0, 'trainer', along_y(1))]
    unnamed x42 -> x40, local copies, waits for them, and re-layouts: 11.1 us -> 10.5 us
  transfers between devices with their start and end apart: 32 -> 32, of which waited for: 21 -> 18; matrix products, arithmetic and copies ran while one was open for 3% -> 4% of each run, Pallas kernels for 22% -> 23%
where the time goes in v2:
time: 197 us; the launch traced here: 196 us
  starting transfers between devices  66.2 us (34%)
  waiting for transfers between devices  58.4 us (30%)
  Pallas kernels  51.7 us (26%)
  local copies, waits for them, and re-layouts  12.5 us (6%)
  other arithmetic  3.76 us (2%)
  between operations  3.41 us (2%)
    all_to_all x1, waiting for transfers between devices, on_device(): lax.all_to_all(packed, 'trainer', split_axis=0, concat_axis=0, tiled=True)  11.2 us
    unnamed x40, local copies, waits for them, and re-layouts  10.5 us
    all_to_all x1, starting transfers between devices, on_device(): lax.all_to_all(split, 'trainer', split_axis=0, concat_axis=0, tiled=True)  10.1 us
    all_to_all x1, starting transfers between devices, on_device(): lax.all_to_all(packed, 'trainer', split_axis=0, concat_axis=0, tiled=True)  9.91 us
    all_to_all x1, starting transfers between devices, on_device(): lax.all_to_all(stats, 'trainer', split_axis=0, concat_axis=0, tiled=True)  9.79 us
    ppermute x4, starting transfers between devices, on_device(): lax.ppermute(half, 'trainer', along_z(k))  9.7 us
    pallas_call x1, Pallas kernels, select_rows(): pl.pallas_call(select_kernel, out_shape=(jax.ShapeDtypeStruct((ROWS, LOCA...  9.41 us
    pallas_call x1, Pallas kernels, head_gradient(): pl.pallas_call(head_kernel, grid_spec=pltpu.PrefetchScalarGridSpec(num_sc...  9.12 us
  transfers between devices with their start and end apart: 32, of which 18 were waited for; matrix products, arithmetic and copies ran while one was open for 4% of the time, Pallas kernels for 23%

profile of v2, /device:TPU:8, one launch (start us, length us, event | category | flops | bytes accessed | tf_op | source)
XLA Modules:
  0.0 195.8 jit_solution(1142028304536436143)
XLA Ops:
  1.6 3.3 %collective-permute-start.1 = (bf16[32,1536]{1,0:T(8,128)(2,1)S(1)}, bf16[32,1536]{1,0:T(8,128)(2,1)S(1)}, u32[]{:S(2)}, u32[]{:S(2)}) collective-permute-start(bf16[32,1536]{1,0:T(8,128)(2,1)S(1)} %constant_dynamic-slice_fusion.refs_0_), channel_id=1, source_target_pairs={{0,64},{8,72},{16,80},{24,88},{32,96},{40,104},{48,112},{56,120},{... | collective-permute-start | bytes 294920 | tf_op jit(solution)/shard_map/ppermute | solution.py:680
  4.9 3.1 %collective-permute-start.4 = (bf16[32,1536]{1,0:T(8,128)(2,1)S(1)}, bf16[32,1536]{1,0:T(8,128)(2,1)S(1)}, u32[]{:S(2)}, u32[]{:S(2)}) collective-permute-start(bf16[32,1536]{1,0:T(8,128)(2,1)S(1)} %constant_dynamic-slice_fusion.refs_0_), channel_id=1, source_target_pairs={{0,192},{8,200},{16,208},{24,216},{32,224},{40,232},{48,240},{56,2... | collective-permute-start | bytes 294920 | tf_op jit(solution)/shard_map/ppermute | solution.py:680
  9.1 2.2 %collective-permute-start.6 = (bf16[32,1536]{1,0:T(8,128)(2,1)S(1)}, bf16[32,1536]{1,0:T(8,128)(2,1)S(1)}, u32[]{:S(2)}, u32[]{:S(2)}) collective-permute-start(bf16[32,1536]{1,0:T(8,128)(2,1)S(1)} %constant_dynamic-slice_fusion.refs_0_), channel_id=1, source_target_pairs={{0,224},{8,232},{16,240},{24,248},{32,0},{40,8},{48,16},{56,24},{6... | collective-permute-start | bytes 294920 | tf_op jit(solution)/shard_map/ppermute | solution.py:680
  11.3 1.3 add_convert_fusion
  14.4 1.9 collective-permute-start.3
  17.7 2.7 %collective-permute-done.2.refs_3_ = bf16[32,1536]{1,0:T(8,128)(2,1)S(1)} collective-permute-done((bf16[32,1536]{1,0:T(8,128)(2,1)S(1)}, bf16[32,1536]{1,0:T(8,128)(2,1)S(1)}, u32[]{:S(2)}, u32[]{:S(2)}) %collective-permute-start.2) | collective-permute-done | bytes 98336 | tf_op jit(solution)/shard_map/ppermute | solution.py:682
  20.4 1.8 collective-permute-done.3.refs_4_
  22.4 1.6 collective-permute-start.7
  24.5 1.6 collective-permute-start.9
  26.5 8.0 %collective-permute-done.7 = bf16[4,32,1536]{2,1,0:T(8,128)(2,1)S(1)} collective-permute-done((bf16[4,32,1536]{2,1,0:T(8,128)(2,1)S(1)}, bf16[4,32,1536]{2,1,0:T(8,128)(2,1)S(1)}, u32[]{:S(2)}, u32[]{:S(2)}) %collective-permute-start.7) | collective-permute-done | bytes 393248 | tf_op jit(solution)/shard_map/ppermute | solution.py:695
  34.5 1.6 collective-permute-done.8
  37.2 2.9 %collective-permute-done.9 = bf16[4,32,1536]{2,1,0:T(8,128)(2,1)S(1)} collective-permute-done((bf16[4,32,1536]{2,1,0:T(8,128)(2,1)S(1)}, bf16[4,32,1536]{2,1,0:T(8,128)(2,1)S(1)}, u32[]{:S(2)}, u32[]{:S(2)}) %collective-permute-start.9) | collective-permute-done | bytes 393248 | tf_op jit(solution)/shard_map/ppermute | solution.py:697
  40.1 1.2 collective-permute-done.10
  41.5 1.4 collective-permute-start.11
  44.5 2.1 %shard_map.86 = bf16[32,32,384]{2,1,0:T(8,128)(2,1)} custom-call(bf16[32,12288]{1,0:T(8,128)(2,1)} %bitcast.17), custom_call_target="tpu_custom_call" | custom-call | tf_op jit(solution)/shard_map/pallas_call | solution.py:39
  46.6 4.1 %shard_map.87 = (bf16[384,1536]{1,0:T(8,128)(2,1)}, bf16[384,1536]{1,0:T(8,128)(2,1)}) custom-call(s32[2]{0:T(128)} %pad_add_fusion.1.at_ref, bf16[4,2,384,384]{3,2,1,0:T(8,128)(2,1)} %bitcast.13), custom_call_target="tpu_custom_call" | custom-call | tf_op jit(solution)/shard_map/pallas_call | solution.py:431
  50.7 2.3 %collective-permute-done.11 = bf16[4,32,1536]{2,1,0:T(8,128)(2,1)S(1)} collective-permute-done((bf16[4,32,1536]{2,1,0:T(8,128)(2,1)S(1)}, bf16[4,32,1536]{2,1,0:T(8,128)(2,1)S(1)}, u32[]{:S(2)}, u32[]{:S(2)}) %collective-permute-start.11) | collective-permute-done | bytes 393248 | tf_op jit(solution)/shard_map/ppermute | solution.py:699
  54.8 1.0 constant_dynamic-update-slice_fusion.4.refs_2_
  55.9 10.1 %all-to-all-start = ((bf16[32,32,384]{2,1,0:T(8,128)(2,1)}), bf16[32,32,384]{2,1,0:T(8,128)(2,1)S(1)}, u32[]{:S(2)}, u32[]{:S(2)}) async-start(bf16[32,32,384]{2,1,0:T(8,128)(2,1)} %shard_map.86), calls=%async_computation | async-start | bytes 1572864 | tf_op jit(solution)/shard_map/all_to_all | solution.py:709
  66.7 1.7 collective-permute-done.15.refs_5_
  69.3 8.4 %shard_map.88 = (bf16[2,8,4,32,1536]{4,3,2,1,0:T(8,128)(2,1)}, f32[1024,384]{1,0:T(8,128)}, f32[8,128]{1,0:T(8,128)}, f32[8,128]{1,0:T(8,128)}) custom-call(s32[2]{0:T(128)} %pad_add_fusion.at_ref, bf16[8,32,1536]{2,1,0:T(8,128)(2,1)} %copy-done.1, bf16[16,32,1536]{2,1,0:T(8,128)(2,1)} %copy-done.9, bf16[8,32,1536]{2,1,0:T(8,128)(2,1)} %copy-done.10, ...), custom_call_target="tpu_custom_call" | custom-call | tf_op jit(solution)/shard_map/pallas_call | solution.py:131
  78.0 1.2 collective-permute-done.16.refs_1_
  79.9 1.6 collective-permute-start.17
  81.5 2.7 %collective-permute-start.18 = (f32[8,128]{1,0:T(8,128)S(1)}, f32[8,128]{1,0:T(8,128)S(1)}, u32[]{:S(2)}, u32[]{:S(2)}) collective-permute-start(f32[8,128]{1,0:T(8,128)S(1)} %shard_map.89.refs_0_), channel_id=1, source_target_pairs={{0,4},{1,5},{2,6},{3,7},{4,0},{5,1},{6,2},{7,3},{8,12},{9,13},{10,... | collective-permute-start | bytes 12296 | tf_op jit(solution)/shard_map/ppermute | solution.py:713
  84.2 1.4 collective-permute-start.19
  86.6 1.2 collective-permute-done.19.refs_3_
  88.4 1.4 shard_map.90
  89.9 9.8 %all-to-all-start.1 = ((f32[32,8,128]{2,1,0:T(8,128)}), f32[32,8,128]{2,1,0:T(8,128)S(1)}, u32[]{:S(2)}, u32[]{:S(2)}) async-start(f32[32,8,128]{2,1,0:T(8,128)} %shard_map.90), calls=%async_computation.1 | async-start | bytes 262144 | tf_op jit(solution)/shard_map/all_to_all | solution.py:718
  99.7 9.4 %shard_map.91 = (f32[1024,384]{1,0:T(8,128)}, f32[8,128]{1,0:T(8,128)}, f32[1,1]{1,0:T(1,128)}) custom-call(f32[8,128]{1,0:T(8,128)} %get-tuple-element.49.top_ref, f32[1024,384]{1,0:T(8,128)} %get-tuple-element.50.far_ref, bf16[1024,384]{1,0:T(8,128)(2,1)} %bitcast.15, f32[1,1024]{1,0:T(1,128)} %bitcast.18, f32[1,1024]{1,0:T(1,128)} %compare_convert_fusion.live_ref), custom_call_target="tpu_custom_call" | custom-call | flops 3221225472 | bytes 8388608 | tf_op jit(solution)/shard_map/pallas_call | solution.py:244
  109.8 7.2 %shard_map.92 = (bf16[1024,384]{1,0:T(8,128)(2,1)}, bf16[1024,768]{1,0:T(8,128)(2,1)}, f32[1,1]{1,0:T(1,128)}) custom-call(f32[32,8,128]{2,1,0:T(8,128)} %copy-done.12, f32[8,128]{1,0:T(8,128)} %get-tuple-element.49.top_ref, f32[8,128]{1,0:T(8,128)} %get-tuple-element.54.mass_ref, f32[1,1]{1,0:T(1,128)} %get-tuple-element.55.cross_ref, ...), custom_call_target="tpu_custom_call" | custom-call | tf_op jit(solution)/shard_map/pallas_call | solution.py:320
  117.6 2.1 %collective-permute-done.20.more_ref = f32[1,1]{1,0:T(1,128)} collective-permute-done((f32[1,1]{1,0:T(1,128)}, f32[1,1]{1,0:T(1,128)}, u32[]{:S(2)}, u32[]{:S(2)}) %collective-permute-start.20) | collective-permute-done | bytes 36 | tf_op jit(solution)/shard_map/ppermute | solution.py:723
  119.7 1.1 copy-done.3
  120.8 2.7 %shard_map.94 = (s16[528,384]{1,0:T(8,128)(2,1)S(1)}, s16[528,384]{1,0:T(8,128)(2,1)S(1)}, f32[1,128]{1,0:T(1,128)S(1)}) custom-call(f32[1,1]{1,0:T(1,128)} %get-tuple-element.58.loss_ref, f32[1,1]{1,0:T(1,128)} %collective-permute-done.20.more_ref, bf16[1024,384]{1,0:T(8,128)(2,1)S(1)} %copy-done.3, ...), custom_call_target="tpu_custom_call" | custom-call | tf_op jit(solution)/shard_map/pallas_call | solution.py:503
  123.5 2.7 %collective-permute-start.27 = (s16[528,384]{1,0:T(8,128)(2,1)S(1)}, s16[528,384]{1,0:T(8,128)(2,1)S(1)}, u32[]{:S(2)}, u32[]{:S(2)}) collective-permute-start(s16[528,384]{1,0:T(8,128)(2,1)S(1)} %get-tuple-element.70), channel_id=1, source_target_pairs={{0,6},{1,7},{2,0},{3,1},{4,2},{5,3},{6,4},{7,5},{8,14},{9,15},{10,... | collective-permute-start | bytes 1216520 | tf_op jit(solution)/shard_map/ppermute | solution.py:727
  126.2 2.6 %shard_map.95 = (f32[512,384]{1,0:T(8,128)S(1)}, s16[528,384]{1,0:T(8,128)(2,1)S(1)}, s16[528,384]{1,0:T(8,128)(2,1)S(1)}, f32[512,384]{1,0:T(8,128)S(1)}, f32[1024,384]{1,0:T(8,128)S(1)}) custom-call(f32[1,128]{1,0:T(1,128)S(1)} %get-tuple-element.63.loss_ref, bf16[1024,384]{1,0:T(8,128)(2,1)S(1)} %copy-done.3, ...), custom_call_target="tpu_custom_call" | custom-call | tf_op jit(solution)/shard_map/pallas_call | solution.py:515
  128.8 3.3 %collective-permute-start.25 = (s16[528,384]{1,0:T(8,128)(2,1)S(1)}, s16[528,384]{1,0:T(8,128)(2,1)S(1)}, u32[]{:S(2)}, u32[]{:S(2)}) collective-permute-start(s16[528,384]{1,0:T(8,128)(2,1)S(1)} %get-tuple-element.67), channel_id=1, source_target_pairs={{0,6},{1,7},{2,0},{3,1},{4,2},{5,3},{6,4},{7,5},{8,14},{9,15},{10,... | collective-permute-start | bytes 1216520 | tf_op jit(solution)/shard_map/ppermute | solution.py:730
  132.1 3.9 %collective-permute-done.27.got_ref = s16[528,384]{1,0:T(8,128)(2,1)S(1)} collective-permute-done((s16[528,384]{1,0:T(8,128)(2,1)S(1)}, s16[528,384]{1,0:T(8,128)(2,1)S(1)}, u32[]{:S(2)}, u32[]{:S(2)}) %collective-permute-start.27) | collective-permute-done | bytes 405536 | tf_op jit(solution)/shard_map/ppermute | solution.py:727
  136.4 3.7 %collective-permute-start.28 = (s16[528,384]{1,0:T(8,128)(2,1)S(1)}, s16[528,384]{1,0:T(8,128)(2,1)S(1)}, u32[]{:S(2)}, u32[]{:S(2)}) collective-permute-start(s16[528,384]{1,0:T(8,128)(2,1)S(1)} %shard_map.97), channel_id=1, source_target_pairs={{0,6},{1,7},{2,0},{3,1},{4,2},{5,3},{6,4},{7,5},{8,14},{9,15},{10,... | collective-permute-start | bytes 1216520 | tf_op jit(solution)/shard_map/ppermute | solution.py:732
  140.6 4.1 %collective-permute-done.25.low_l = s16[528,384]{1,0:T(8,128)(2,1)S(1)} collective-permute-done((s16[528,384]{1,0:T(8,128)(2,1)S(1)}, s16[528,384]{1,0:T(8,128)(2,1)S(1)}, u32[]{:S(2)}, u32[]{:S(2)}) %collective-permute-start.25) | collective-permute-done | bytes 405536 | tf_op jit(solution)/shard_map/ppermute | solution.py:730
  144.7 3.7 %collective-permute-done.26.high_r = s16[528,384]{1,0:T(8,128)(2,1)S(1)} collective-permute-done((s16[528,384]{1,0:T(8,128)(2,1)S(1)}, s16[528,384]{1,0:T(8,128)(2,1)S(1)}, u32[]{:S(2)}, u32[]{:S(2)}) %collective-permute-start.26) | collective-permute-done | bytes 405536 | tf_op jit(solution)/shard_map/ppermute | solution.py:729
  148.4 4.2 %collective-permute-done.28.high_l = s16[528,384]{1,0:T(8,128)(2,1)S(1)} collective-permute-done((s16[528,384]{1,0:T(8,128)(2,1)S(1)}, s16[528,384]{1,0:T(8,128)(2,1)S(1)}, u32[]{:S(2)}, u32[]{:S(2)}) %collective-permute-start.28) | collective-permute-done | bytes 405536 | tf_op jit(solution)/shard_map/ppermute | solution.py:732
  152.6 3.4 %collective-permute-done.24.low_r = s16[528,384]{1,0:T(8,128)(2,1)S(1)} collective-permute-done((s16[528,384]{1,0:T(8,128)(2,1)S(1)}, s16[528,384]{1,0:T(8,128)(2,1)S(1)}, u32[]{:S(2)}, u32[]{:S(2)}) %collective-permute-start.24) | collective-permute-done | bytes 405536 | tf_op jit(solution)/shard_map/ppermute | solution.py:731
  156.0 2.4 %shard_map.98 = s16[32,112,128]{2,1,0:T(8,128)(2,1)} custom-call(f32[1,128]{1,0:T(1,128)S(1)} %get-tuple-element.63.loss_ref, f32[1024,384]{1,0:T(8,128)S(1)} %get-tuple-element.64.own_ref, s16[528,384]{1,0:T(8,128)(2,1)S(1)} %collective-permute-done.24.low_r, s16[528,384]{1,0:T(8,128)(2,1)S(1)} %collective-permute-done.25.low_l, ...), custom_call_target="tpu_custom_call" | custom-call | tf_op jit(solution)/shard_map/pallas_call | solution.py:574
  158.4 9.9 %all-to-all-start.2 = ((s16[32,112,128]{2,1,0:T(8,128)(2,1)}), s16[32,112,128]{2,1,0:T(8,128)(2,1)S(1)}, u32[]{:S(2)}, u32[]{:S(2)}) async-start(s16[32,112,128]{2,1,0:T(8,128)(2,1)} %shard_map.98), calls=%async_computation.2 | async-start | bytes 1835008 | tf_op jit(solution)/shard_map/all_to_all | solution.py:735
  169.7 2.8 %copy-done.6 = bf16[2,8,4,32,1536]{4,3,2,1,0:T(8,128)(2,1)S(1)} copy-done((bf16[2,8,4,32,1536]{4,3,2,1,0:T(8,128)(2,1)S(1)}, bf16[2,8,4,32,1536]{4,3,2,1,0:T(8,128)(2,1)}, u32[]{:S(2)}) %copy-start.6) | copy-done | bytes 6291480
  172.4 9.1 %shard_map.93 = f32[9216,128]{1,0:T(8,128)} custom-call(s32[1]{0:T(128)} %bitcast.c_ref, bf16[2,1024,1536]{2,1,0:T(8,128)(2,1)S(1)} %bitcast.12, bf16[1024,768]{1,0:T(8,128)(2,1)S(1)} %copy-done.7), custom_call_target="tpu_custom_call" | custom-call | flops 4831838208 | bytes 12582912 | tf_op jit(solution)/shard_map/pallas_call | solution.py:628
  181.6 11.2 %all-to-all-done.2.x_ref = s16[32,112,128]{2,1,0:T(8,128)(2,1)S(1)} async-done(((s16[32,112,128]{2,1,0:T(8,128)(2,1)}), s16[32,112,128]{2,1,0:T(8,128)(2,1)S(1)}, u32[]{:S(2)}, u32[]{:S(2)}) %all-to-all-start.2) | async-done | bytes 917536 | tf_op jit(solution)/shard_map/all_to_all | solution.py:735
  192.8 1.2 shard_map.99
  (82 shorter events, 17.6 us)
Async XLA Ops:
  0.6 0.9 copy-start
  1.6 11.8 %collective-permute-start.1 = (bf16[32,1536]{1,0:T(8,128)(2,1)S(1)}, bf16[32,1536]{1,0:T(8,128)(2,1)S(1)}, u32[]{:S(2)}, u32[]{:S(2)}) collective-permute-start(bf16[32,1536]{1,0:T(8,128)(2,1)S(1)} %constant_dynamic-slice_fusion.refs_0_), channel_id=1, source_target_pairs={{0,64},{8,72},{16,80},{24,88},{32,96},{40,104},{48,112},{56,120},{... | collective-permute-start | bytes 294920 | tf_op jit(solution)/shard_map/ppermute | solution.py:680
  4.9 11.3 %collective-permute-start.4 = (bf16[32,1536]{1,0:T(8,128)(2,1)S(1)}, bf16[32,1536]{1,0:T(8,128)(2,1)S(1)}, u32[]{:S(2)}, u32[]{:S(2)}) collective-permute-start(bf16[32,1536]{1,0:T(8,128)(2,1)S(1)} %constant_dynamic-slice_fusion.refs_0_), channel_id=1, source_target_pairs={{0,192},{8,200},{16,208},{24,216},{32,224},{40,232},{48,240},{56,2... | collective-permute-start | bytes 294920 | tf_op jit(solution)/shard_map/ppermute | solution.py:680
  8.0 9.6 %collective-permute-start = (bf16[32,1536]{1,0:T(8,128)(2,1)S(1)}, bf16[32,1536]{1,0:T(8,128)(2,1)S(1)}, u32[]{:S(2)}, u32[]{:S(2)}) collective-permute-start(bf16[32,1536]{1,0:T(8,128)(2,1)S(1)} %constant_dynamic-slice_fusion.refs_0_), channel_id=1, source_target_pairs={{0,32},{8,40},{16,48},{24,56},{32,64},{40,72},{48,80},{56,88},{64,... | collective-permute-start | bytes 294920 | tf_op jit(solution)/shard_map/ppermute | solution.py:680
  9.1 8.6 %collective-permute-start.6 = (bf16[32,1536]{1,0:T(8,128)(2,1)S(1)}, bf16[32,1536]{1,0:T(8,128)(2,1)S(1)}, u32[]{:S(2)}, u32[]{:S(2)}) collective-permute-start(bf16[32,1536]{1,0:T(8,128)(2,1)S(1)} %constant_dynamic-slice_fusion.refs_0_), channel_id=1, source_target_pairs={{0,224},{8,232},{16,240},{24,248},{32,0},{40,8},{48,16},{56,24},{6... | collective-permute-start | bytes 294920 | tf_op jit(solution)/shard_map/ppermute | solution.py:680
  13.4 7.0 %collective-permute-start.2 = (bf16[32,1536]{1,0:T(8,128)(2,1)S(1)}, bf16[32,1536]{1,0:T(8,128)(2,1)S(1)}, u32[]{:S(2)}, u32[]{:S(2)}) collective-permute-start(bf16[32,1536]{1,0:T(8,128)(2,1)S(1)} %collective-permute-done.1.refs_2_), channel_id=1, source_target_pairs={{0,32},{8,40},{16,48},{24,56},{32,64},{40,72},{48,80},{56,88},{64,... | collective-permute-start | bytes 294920 | tf_op jit(solution)/shard_map/ppermute | solution.py:682
  14.4 7.8 %collective-permute-start.3 = (bf16[32,1536]{1,0:T(8,128)(2,1)S(1)}, bf16[32,1536]{1,0:T(8,128)(2,1)S(1)}, u32[]{:S(2)}, u32[]{:S(2)}) collective-permute-start(bf16[32,1536]{1,0:T(8,128)(2,1)S(1)} %collective-permute-done.1.refs_2_), channel_id=1, source_target_pairs={{0,64},{8,72},{16,80},{24,88},{32,96},{40,104},{48,112},{56,120},{... | collective-permute-start | bytes 294920 | tf_op jit(solution)/shard_map/ppermute | solution.py:683
  16.3 5.9 %collective-permute-start.5 = (bf16[32,1536]{1,0:T(8,128)(2,1)S(1)}, bf16[32,1536]{1,0:T(8,128)(2,1)S(1)}, u32[]{:S(2)}, u32[]{:S(2)}) collective-permute-start(bf16[32,1536]{1,0:T(8,128)(2,1)S(1)} %collective-permute-done.4.refs_6_), channel_id=1, source_target_pairs={{0,224},{8,232},{16,240},{24,248},{32,0},{40,8},{48,16},{56,24},{6... | collective-permute-start | bytes 294920 | tf_op jit(solution)/shard_map/ppermute | solution.py:684
  22.3 20.6 %copy-start.1 = (bf16[8,32,1536]{2,1,0:T(8,128)(2,1)}, bf16[8,32,1536]{2,1,0:T(8,128)(2,1)S(1)}, u32[]{:S(2)}) copy-start(bf16[8,32,1536]{2,1,0:T(8,128)(2,1)S(1)} %shard_map.85.refs_0_) | copy-start | bytes 2359300
  22.4 12.1 %collective-permute-start.7 = (bf16[4,32,1536]{2,1,0:T(8,128)(2,1)S(1)}, bf16[4,32,1536]{2,1,0:T(8,128)(2,1)S(1)}, u32[]{:S(2)}, u32[]{:S(2)}) collective-permute-start(bf16[4,32,1536]{2,1,0:T(8,128)(2,1)S(1)} %get-tuple-element.77), channel_id=1, source_target_pairs={{0,8},{8,16},{16,24},{24,0},{32,40},{40,48},{48,56},{56,32},{64,72... | collective-permute-start | bytes 1179656 | tf_op jit(solution)/shard_map/ppermute | solution.py:695
  24.0 12.2 %collective-permute-start.8 = (bf16[4,32,1536]{2,1,0:T(8,128)(2,1)S(1)}, bf16[4,32,1536]{2,1,0:T(8,128)(2,1)}, u32[]{:S(2)}, u32[]{:S(2)}) collective-permute-start(bf16[4,32,1536]{2,1,0:T(8,128)(2,1)S(1)} %get-tuple-element.76), channel_id=1, source_target_pairs={{0,24},{8,0},{16,8},{24,16},{32,56},{40,32},{48,40},{56,48},{64,88... | collective-permute-start | bytes 1179656 | tf_op jit(solution)/shard_map/ppermute | solution.py:696
  24.5 15.6 %collective-permute-start.9 = (bf16[4,32,1536]{2,1,0:T(8,128)(2,1)S(1)}, bf16[4,32,1536]{2,1,0:T(8,128)(2,1)S(1)}, u32[]{:S(2)}, u32[]{:S(2)}) collective-permute-start(bf16[4,32,1536]{2,1,0:T(8,128)(2,1)S(1)} %get-tuple-element.76), channel_id=1, source_target_pairs={{0,8},{8,16},{16,24},{24,0},{32,40},{40,48},{48,56},{56,32},{64,72... | collective-permute-start | bytes 1179656 | tf_op jit(solution)/shard_map/ppermute | solution.py:697
  26.0 15.3 %collective-permute-start.10 = (bf16[4,32,1536]{2,1,0:T(8,128)(2,1)S(1)}, bf16[4,32,1536]{2,1,0:T(8,128)(2,1)S(1)}, u32[]{:S(2)}, u32[]{:S(2)}) collective-permute-start(bf16[4,32,1536]{2,1,0:T(8,128)(2,1)S(1)} %get-tuple-element.77), channel_id=1, source_target_pairs={{0,24},{8,0},{16,8},{24,16},{32,56},{40,32},{48,40},{56,48},{64,88... | collective-permute-start | bytes 1179656 | tf_op jit(solution)/shard_map/ppermute | solution.py:698
  41.4 9.3 %copy-start.9 = (bf16[16,32,1536]{2,1,0:T(8,128)(2,1)}, bf16[16,32,1536]{2,1,0:T(8,128)(2,1)S(1)}, u32[]{:S(2)}) copy-start(bf16[16,32,1536]{2,1,0:T(8,128)(2,1)S(1)} %constant_dynamic-update-slice_fusion.refs_1_) | copy-start | bytes 4718596
  41.4 14.5 %collective-permute-start.14 = (bf16[16,32,1536]{2,1,0:T(8,128)(2,1)S(1)}, bf16[16,32,1536]{2,1,0:T(8,128)(2,1)}, u32[]{:S(2)}, u32[]{:S(2)}) collective-permute-start(bf16[16,32,1536]{2,1,0:T(8,128)(2,1)S(1)} %constant_dynamic-update-slice_fusion.refs_1_), channel_id=1, source_target_pairs={{0,1},{1,0},{2,3},{3,2},{4,5},{5,4},{6,7},{7,6},{8,9},{9,8},{10,11... | collective-permute-start | bytes 4718600 | tf_op jit(solution)/shard_map/ppermute | solution.py:707
  41.5 11.5 %collective-permute-start.11 = (bf16[4,32,1536]{2,1,0:T(8,128)(2,1)S(1)}, bf16[4,32,1536]{2,1,0:T(8,128)(2,1)S(1)}, u32[]{:S(2)}, u32[]{:S(2)}) collective-permute-start(bf16[4,32,1536]{2,1,0:T(8,128)(2,1)S(1)} %collective-permute-done.7), channel_id=1, source_target_pairs={{0,8},{8,16},{16,24},{24,0},{32,40},{40,48},{48,56},{56,32},{64,72... | collective-permute-start | bytes 1179656 | tf_op jit(solution)/shard_map/ppermute | solution.py:699
  42.9 13.0 %collective-permute-start.13 = (bf16[8,32,1536]{2,1,0:T(8,128)(2,1)S(1)}, bf16[8,32,1536]{2,1,0:T(8,128)(2,1)}, u32[]{:S(2)}, u32[]{:S(2)}) collective-permute-start(bf16[8,32,1536]{2,1,0:T(8,128)(2,1)S(1)} %shard_map.85.refs_0_), channel_id=1, source_target_pairs={{0,1},{1,0},{2,3},{3,2},{4,5},{5,4},{6,7},{7,6},{8,9},{9,8},{10,11... | collective-permute-start | bytes 2359304 | tf_op jit(solution)/shard_map/ppermute | solution.py:707
  43.0 11.8 %collective-permute-start.12 = (bf16[4,32,1536]{2,1,0:T(8,128)(2,1)}, bf16[4,32,1536]{2,1,0:T(8,128)(2,1)}, u32[]{:S(2)}, u32[]{:S(2)}) collective-permute-start(bf16[4,32,1536]{2,1,0:T(8,128)(2,1)} %collective-permute-done.8), channel_id=1, source_target_pairs={{0,24},{8,0},{16,8},{24,16},{32,56},{40,32},{48,40},{56,48},{64,88... | collective-permute-start | bytes 1179656 | tf_op jit(solution)/shard_map/ppermute | solution.py:700
  53.0 0.7 copy-start.13
  55.8 12.5 %copy-start.10 = (bf16[8,32,1536]{2,1,0:T(8,128)(2,1)}, bf16[8,32,1536]{2,1,0:T(8,128)(2,1)S(1)}, u32[]{:S(2)}) copy-start(bf16[8,32,1536]{2,1,0:T(8,128)(2,1)S(1)} %constant_dynamic-update-slice_fusion.4.refs_2_) | copy-start | bytes 2359300
  55.9 34.0 %all-to-all-start = ((bf16[32,32,384]{2,1,0:T(8,128)(2,1)}), bf16[32,32,384]{2,1,0:T(8,128)(2,1)S(1)}, u32[]{:S(2)}, u32[]{:S(2)}) async-start(bf16[32,32,384]{2,1,0:T(8,128)(2,1)} %shard_map.86), calls=%async_computation | async-start | bytes 1572864 | tf_op jit(solution)/shard_map/all_to_all | solution.py:709
  66.0 2.4 %collective-permute-start.15 = (bf16[8,32,1536]{2,1,0:T(8,128)(2,1)S(1)}, bf16[8,32,1536]{2,1,0:T(8,128)(2,1)S(1)}, u32[]{:S(2)}, u32[]{:S(2)}) collective-permute-start(bf16[8,32,1536]{2,1,0:T(8,128)(2,1)S(1)} %constant_dynamic-update-slice_fusion.4.refs_2_), channel_id=1, source_target_pairs={{0,1},{1,0},{2,3},{3,2},{4,5},{5,4},{6,7},{7,6},{8,9},{9,8},{10,11... | collective-permute-start | bytes 2359304 | tf_op jit(solution)/shard_map/ppermute | solution.py:707
  68.4 0.9 copy-start.11
  77.7 1.5 collective-permute-start.16
  79.2 0.7 copy-start.5
  79.9 7.9 %copy-start.4 = (f32[8,128]{1,0:T(8,128)}, f32[8,128]{1,0:T(8,128)S(1)}, u32[]{:S(2)}) copy-start(f32[8,128]{1,0:T(8,128)S(1)} %shard_map.89.refs_0_) | copy-start | bytes 12292
  79.9 5.7 %collective-permute-start.17 = (f32[8,128]{1,0:T(8,128)S(1)}, f32[8,128]{1,0:T(8,128)S(1)}, u32[]{:S(2)}, u32[]{:S(2)}) collective-permute-start(f32[8,128]{1,0:T(8,128)S(1)} %shard_map.89.refs_0_), channel_id=1, source_target_pairs={{0,2},{1,3},{2,4},{3,5},{4,6},{5,7},{6,0},{7,1},{8,10},{9,11},{10,... | collective-permute-start | bytes 12296 | tf_op jit(solution)/shard_map/ppermute | solution.py:713
  81.5 5.1 %collective-permute-start.18 = (f32[8,128]{1,0:T(8,128)S(1)}, f32[8,128]{1,0:T(8,128)S(1)}, u32[]{:S(2)}, u32[]{:S(2)}) collective-permute-start(f32[8,128]{1,0:T(8,128)S(1)} %shard_map.89.refs_0_), channel_id=1, source_target_pairs={{0,4},{1,5},{2,6},{3,7},{4,0},{5,1},{6,2},{7,3},{8,12},{9,13},{10,... | collective-permute-start | bytes 12296 | tf_op jit(solution)/shard_map/ppermute | solution.py:713
  84.2 3.6 %collective-permute-start.19 = (f32[8,128]{1,0:T(8,128)S(1)}, f32[8,128]{1,0:T(8,128)S(1)}, u32[]{:S(2)}, u32[]{:S(2)}) collective-permute-start(f32[8,128]{1,0:T(8,128)S(1)} %shard_map.89.refs_0_), channel_id=1, source_target_pairs={{0,6},{1,7},{2,0},{3,1},{4,2},{5,3},{6,4},{7,5},{8,14},{9,15},{10,... | collective-permute-start | bytes 12296 | tf_op jit(solution)/shard_map/ppermute | solution.py:713
  85.7 2.2 %copy-start.14 = (f32[8,128]{1,0:T(8,128)}, f32[8,128]{1,0:T(8,128)S(1)}, u32[]{:S(2)}) copy-start(f32[8,128]{1,0:T(8,128)S(1)} %collective-permute-done.17.refs_1_) | copy-start | bytes 12292
  86.6 1.2 copy-start.15
  89.9 27.8 %collective-permute-start.22 = (bf16[384,1536]{1,0:T(8,128)(2,1)}, bf16[384,1536]{1,0:T(8,128)(2,1)S(1)}, u32[]{:S(2)}, u32[]{:S(2)}) collective-permute-start(bf16[384,1536]{1,0:T(8,128)(2,1)} %get-tuple-element.62), channel_id=1, source_target_pairs={{0,1},{1,0},{2,3},{3,2},{4,5},{5,4},{6,7},{7,6},{8,9},{9,8},{10,11... | collective-permute-start | bytes 3538952 | tf_op jit(solution)/shard_map/ppermute | solution.py:716
  89.9 9.8 %copy-start.8 = (bf16[32,32,384]{2,1,0:T(8,128)(2,1)}, bf16[32,32,384]{2,1,0:T(8,128)(2,1)S(1)}, u32[]{:S(2)}) copy-start(bf16[32,32,384]{2,1,0:T(8,128)(2,1)S(1)} %all-to-all-done) | copy-start | bytes 2359300
  89.9 19.2 %all-to-all-start.1 = ((f32[32,8,128]{2,1,0:T(8,128)}), f32[32,8,128]{2,1,0:T(8,128)S(1)}, u32[]{:S(2)}, u32[]{:S(2)}) async-start(f32[32,8,128]{2,1,0:T(8,128)} %shard_map.90), calls=%async_computation.1 | async-start | bytes 262144 | tf_op jit(solution)/shard_map/all_to_all | solution.py:718
  109.1 10.6 %copy-start.2 = (bf16[384,1536]{1,0:T(8,128)(2,1)S(1)}, bf16[384,1536]{1,0:T(8,128)(2,1)}, u32[]{:S(2)}) copy-start(bf16[384,1536]{1,0:T(8,128)(2,1)} %get-tuple-element.60.w_own) | copy-start | bytes 3538948
  117.0 2.7 %collective-permute-start.21 = (bf16[1024,384]{1,0:T(8,128)(2,1)}, bf16[1024,384]{1,0:T(8,128)(2,1)S(1)}, u32[]{:S(2)}, u32[]{:S(2)}) collective-permute-start(bf16[1024,384]{1,0:T(8,128)(2,1)} %get-tuple-element.59.own_ref), channel_id=1, source_target_pairs={{0,1},{1,0},{2,3},{3,2},{4,5},{5,4},{6,7},{7,6},{8,9},{9,8},{10,11... | collective-permute-start | bytes 2359304 | tf_op jit(solution)/shard_map/ppermute | solution.py:724
  117.1 2.6 %collective-permute-start.20 = (f32[1,1]{1,0:T(1,128)}, f32[1,1]{1,0:T(1,128)}, u32[]{:S(2)}, u32[]{:S(2)}) collective-permute-start(f32[1,1]{1,0:T(1,128)} %get-tuple-element.58.loss_ref), channel_id=1, source_target_pairs={{0,1},{1,0},{2,3},{3,2},{4,5},{5,4},{6,7},{7,6},{8,9},{9,8},{10,11... | collective-permute-start | bytes 20 | tf_op jit(solution)/shard_map/ppermute | solution.py:723
  119.7 1.1 copy-start.3
  123.5 12.5 %collective-permute-start.27 = (s16[528,384]{1,0:T(8,128)(2,1)S(1)}, s16[528,384]{1,0:T(8,128)(2,1)S(1)}, u32[]{:S(2)}, u32[]{:S(2)}) collective-permute-start(s16[528,384]{1,0:T(8,128)(2,1)S(1)} %get-tuple-element.70), channel_id=1, source_target_pairs={{0,6},{1,7},{2,0},{3,1},{4,2},{5,3},{6,4},{7,5},{8,14},{9,15},{10,... | collective-permute-start | bytes 1216520 | tf_op jit(solution)/shard_map/ppermute | solution.py:727
  126.2 13.9 %collective-permute-start.23 = (s16[528,384]{1,0:T(8,128)(2,1)S(1)}, s16[528,384]{1,0:T(8,128)(2,1)S(1)}, u32[]{:S(2)}, u32[]{:S(2)}) collective-permute-start(s16[528,384]{1,0:T(8,128)(2,1)S(1)} %get-tuple-element.66), channel_id=1, source_target_pairs={{0,2},{1,3},{2,4},{3,5},{4,6},{5,7},{6,0},{7,1},{8,10},{9,11},{10,... | collective-permute-start | bytes 1216520 | tf_op jit(solution)/shard_map/ppermute | solution.py:726
  128.8 15.9 %collective-permute-start.25 = (s16[528,384]{1,0:T(8,128)(2,1)S(1)}, s16[528,384]{1,0:T(8,128)(2,1)S(1)}, u32[]{:S(2)}, u32[]{:S(2)}) collective-permute-start(s16[528,384]{1,0:T(8,128)(2,1)S(1)} %get-tuple-element.67), channel_id=1, source_target_pairs={{0,6},{1,7},{2,0},{3,1},{4,2},{5,3},{6,4},{7,5},{8,14},{9,15},{10,... | collective-permute-start | bytes 1216520 | tf_op jit(solution)/shard_map/ppermute | solution.py:730
  132.1 16.3 %collective-permute-start.26 = (s16[528,384]{1,0:T(8,128)(2,1)S(1)}, s16[528,384]{1,0:T(8,128)(2,1)S(1)}, u32[]{:S(2)}, u32[]{:S(2)}) collective-permute-start(s16[528,384]{1,0:T(8,128)(2,1)S(1)} %get-tuple-element.68), channel_id=1, source_target_pairs={{0,2},{1,3},{2,4},{3,5},{4,6},{5,7},{6,0},{7,1},{8,10},{9,11},{10,... | collective-permute-start | bytes 1216520 | tf_op jit(solution)/shard_map/ppermute | solution.py:729
  136.4 16.2 %collective-permute-start.28 = (s16[528,384]{1,0:T(8,128)(2,1)S(1)}, s16[528,384]{1,0:T(8,128)(2,1)S(1)}, u32[]{:S(2)}, u32[]{:S(2)}) collective-permute-start(s16[528,384]{1,0:T(8,128)(2,1)S(1)} %shard_map.97), channel_id=1, source_target_pairs={{0,6},{1,7},{2,0},{3,1},{4,2},{5,3},{6,4},{7,5},{8,14},{9,15},{10,... | collective-permute-start | bytes 1216520 | tf_op jit(solution)/shard_map/ppermute | solution.py:732
  140.5 15.5 %collective-permute-start.24 = (s16[528,384]{1,0:T(8,128)(2,1)S(1)}, s16[528,384]{1,0:T(8,128)(2,1)S(1)}, u32[]{:S(2)}, u32[]{:S(2)}) collective-permute-start(s16[528,384]{1,0:T(8,128)(2,1)S(1)} %shard_map.96), channel_id=1, source_target_pairs={{0,2},{1,3},{2,4},{3,5},{4,6},{5,7},{6,0},{7,1},{8,10},{9,11},{10,... | collective-permute-start | bytes 1216520 | tf_op jit(solution)/shard_map/ppermute | solution.py:731
  158.4 9.9 %copy-start.17 = (s32[32]{0:T(128)S(1)}, s32[32]{0:T(128)}, u32[]{:S(2)}) copy-start(s32[32]{0:T(128)} %param.9) | copy-start | bytes 388
  158.4 11.2 %copy-start.7 = (bf16[1024,768]{1,0:T(8,128)(2,1)S(1)}, bf16[1024,768]{1,0:T(8,128)(2,1)}, u32[]{:S(2)}) copy-start(bf16[1024,768]{1,0:T(8,128)(2,1)} %get-tuple-element.57.sums_ref) | copy-start | bytes 4718596
  158.4 34.4 %all-to-all-start.2 = ((s16[32,112,128]{2,1,0:T(8,128)(2,1)}), s16[32,112,128]{2,1,0:T(8,128)(2,1)S(1)}, u32[]{:S(2)}, u32[]{:S(2)}) async-start(s16[32,112,128]{2,1,0:T(8,128)(2,1)} %shard_map.98), calls=%async_computation.2 | async-start | bytes 1835008 | tf_op jit(solution)/shard_map/all_to_all | solution.py:735
  169.7 2.8 %copy-start.6 = (bf16[2,8,4,32,1536]{4,3,2,1,0:T(8,128)(2,1)S(1)}, bf16[2,8,4,32,1536]{4,3,2,1,0:T(8,128)(2,1)}, u32[]{:S(2)}) copy-start(bf16[2,8,4,32,1536]{4,3,2,1,0:T(8,128)(2,1)} %get-tuple-element.44) | copy-start | bytes 18874372
  (2 other events, 1.2 us)

commit v3 on v2

--- a/solution.py
+++ b/solution.py
@@ -705,7 +705,7 @@
     low2, split, w_own, w_give = lax.optimization_barrier((low2, split, w_own, w_give))
     pieces = [plane, middle, jnp.concatenate([low2, high2])]
     pieces += [lax.ppermute(p, "vocab", PAIR) for p in pieces]
-    split, _ = lax.optimization_barrier((split, (pieces[2], pieces[3], pieces[4])))
+    split, _ = lax.optimization_barrier((split, (w_give, low2, high2, pieces[3])))
     probs = lax.all_to_all(split, "trainer", split_axis=0, concat_axis=0, tiled=True)
 
     table, logits, stats, top = logits_and_stats(at_cy, pieces, weight)

time: 197 us -> 194 us (0.985)
  starting transfers between devices: 66.2 us -> 59.8 us
  waiting for transfers between devices: 58.4 us -> 60.9 us
    ppermute x1, waiting for transfers between devices: 8 us -> 0.56 us  [on_device(): low1 = lax.ppermute(low0, 'trainer', along_y(1))]
    ppermute x1, waiting for transfers between devices: 1.64 us -> 8.1 us  [on_device(): high3 = lax.ppermute(high0, 'trainer', along_y(-1))]
    ppermute x1, waiting for transfers between devices: 0.01 us -> 5.52 us  [on_device(): low_r = lax.ppermute(l2, 'vocab', RIGHT)]
    ppermute x4, waiting for transfers between devices: 0.01 us -> 5.1 us  [on_device(): lax.ppermute(half, 'trainer', along_z(k))]
    ppermute x1, waiting for transfers between devices: 3.41 us -> 7.93 us  [on_device(): low_r = lax.ppermute(relay(l1, low_r), 'vocab', RIGHT)]
    ppermute x1, waiting for transfers between devices: 4.2 us -> 0.01 us  [on_device(): high_l = lax.ppermute(relay(h3, high_l), 'vocab', LEFT)]
    ppermute x1, waiting for transfers between devices: 3.86 us -> 0.01 us  [on_device(): high_l = lax.ppermute(h2, 'vocab', LEFT)]
    ppermute x1, waiting for transfers between devices: 3.73 us -> 0.42 us  [on_device(): high_r = lax.ppermute(h1, 'vocab', RIGHT)]
  transfers between devices with their start and end apart: 32 -> 32, of which waited for: 18 -> 17; matrix products, arithmetic and copies ran while one was open for 4% -> 5% of each run, Pallas kernels for 23% -> 23%
where the time goes in v3:
time: 194 us
  waiting for transfers between devices  60.9 us (31%)
  starting transfers between devices  59.8 us (31%)
  Pallas kernels  51.7 us (27%)
  local copies, waits for them, and re-layouts  13.7 us (7%)
  other arithmetic  3.95 us (2%)
  between operations  3.47 us (2%)
    unnamed x40, local copies, waits for them, and re-layouts  11.8 us
    all_to_all x1, waiting for transfers between devices, on_device(): lax.all_to_all(packed, 'trainer', split_axis=0, concat_axis=0, tiled=True)  11.6 us
    all_to_all x1, starting transfers between devices, on_device(): lax.all_to_all(packed, 'trainer', split_axis=0, concat_axis=0, tiled=True)  9.9 us
    all_to_all x1, starting transfers between devices, on_device(): lax.all_to_all(stats, 'trainer', split_axis=0, concat_axis=0, tiled=True)  9.79 us
    pallas_call x1, Pallas kernels, select_rows(): pl.pallas_call(select_kernel, out_shape=(jax.ShapeDtypeStruct((ROWS, LOCA...  9.42 us
    pallas_call x1, Pallas kernels, head_gradient(): pl.pallas_call(head_kernel, grid_spec=pltpu.PrefetchScalarGridSpec(num_sc...  9.13 us
    ppermute x4, starting transfers between devices, on_device(): lax.ppermute(half, 'trainer', along_z(k))  8.86 us
    pallas_call x1, Pallas kernels, logits_and_stats(): pl.pallas_call(logit_kernel, out_shape=(jax.ShapeDtypeStruct((2, Z, Y, SL...  8.42 us
  transfers between devices with their start and end apart: 32, of which 17 were waited for; matrix products, arithmetic and copies ran while one was open for 5% of the time, Pallas kernels for 23%

profile of v3, /device:TPU:8, one launch (start us, length us, event | category | flops | bytes accessed | tf_op | source)
XLA Modules:
  0.0 193.5 jit_solution(13763211087854261380)
XLA Ops:
  0.7 0.9 copy-done
  1.6 5.9 %collective-permute-start.6 = (bf16[32,1536]{1,0:T(8,128)(2,1)S(1)}, bf16[32,1536]{1,0:T(8,128)(2,1)S(1)}, u32[]{:S(2)}, u32[]{:S(2)}) collective-permute-start(bf16[32,1536]{1,0:T(8,128)(2,1)S(1)} %constant_dynamic-slice_fusion.refs_0_), channel_id=1, source_target_pairs={{0,224},{8,232},{16,240},{24,248},{32,0},{40,8},{48,16},{56,24},{6... | collective-permute-start | bytes 294920 | tf_op jit(solution)/shard_map/ppermute | solution.py:680
  7.5 1.5 collective-permute-start.4
  9.0 1.5 collective-permute-start.1
  10.4 1.3 add_convert_fusion
  12.5 5.1 %collective-permute-done.1.refs_2_ = bf16[32,1536]{1,0:T(8,128)(2,1)S(1)} collective-permute-done((bf16[32,1536]{1,0:T(8,128)(2,1)S(1)}, bf16[32,1536]{1,0:T(8,128)(2,1)S(1)}, u32[]{:S(2)}, u32[]{:S(2)}) %collective-permute-start.1) | collective-permute-done | bytes 98336 | tf_op jit(solution)/shard_map/ppermute | solution.py:680
  17.8 1.4 collective-permute-start.2
  19.2 2.7 %collective-permute-start.5 = (bf16[32,1536]{1,0:T(8,128)(2,1)S(1)}, bf16[32,1536]{1,0:T(8,128)(2,1)S(1)}, u32[]{:S(2)}, u32[]{:S(2)}) collective-permute-start(bf16[32,1536]{1,0:T(8,128)(2,1)S(1)} %collective-permute-done.4.refs_6_), channel_id=1, source_target_pairs={{0,224},{8,232},{16,240},{24,248},{32,0},{40,8},{48,16},{56,24},{6... | collective-permute-start | bytes 294920 | tf_op jit(solution)/shard_map/ppermute | solution.py:684
  22.5 1.6 collective-permute-done.5.refs_5_
  24.1 1.2 collective-permute-done.3.refs_4_
  25.3 1.3 collective-permute-done.2.refs_3_
  27.3 1.6 collective-permute-start.7
  28.9 1.6 collective-permute-start.9
  30.9 8.1 %collective-permute-done.8 = bf16[4,32,1536]{2,1,0:T(8,128)(2,1)} collective-permute-done((bf16[4,32,1536]{2,1,0:T(8,128)(2,1)S(1)}, bf16[4,32,1536]{2,1,0:T(8,128)(2,1)}, u32[]{:S(2)}, u32[]{:S(2)}) %collective-permute-start.8) | collective-permute-done | bytes 393248 | tf_op jit(solution)/shard_map/ppermute | solution.py:696
  41.0 1.1 constant_dynamic-update-slice_fusion.3
  42.1 1.0 constant_dynamic-update-slice_fusion.2
  43.1 4.6 %collective-permute-done.9 = bf16[4,32,1536]{2,1,0:T(8,128)(2,1)S(1)} collective-permute-done((bf16[4,32,1536]{2,1,0:T(8,128)(2,1)S(1)}, bf16[4,32,1536]{2,1,0:T(8,128)(2,1)S(1)}, u32[]{:S(2)}, u32[]{:S(2)}) %collective-permute-start.9) | collective-permute-done | bytes 393248 | tf_op jit(solution)/shard_map/ppermute | solution.py:697
  48.9 2.1 %shard_map.86 = bf16[32,32,384]{2,1,0:T(8,128)(2,1)} custom-call(bf16[32,12288]{1,0:T(8,128)(2,1)} %bitcast.17), custom_call_target="tpu_custom_call" | custom-call | tf_op jit(solution)/shard_map/pallas_call | solution.py:39
  51.0 4.1 %shard_map.87 = (bf16[384,1536]{1,0:T(8,128)(2,1)}, bf16[384,1536]{1,0:T(8,128)(2,1)}) custom-call(s32[2]{0:T(128)} %pad_add_fusion.1.at_ref, bf16[4,2,384,384]{3,2,1,0:T(8,128)(2,1)} %bitcast.13), custom_call_target="tpu_custom_call" | custom-call | tf_op jit(solution)/shard_map/pallas_call | solution.py:431
  56.1 7.0 %all-to-all-start = ((bf16[32,32,384]{2,1,0:T(8,128)(2,1)}), bf16[32,32,384]{2,1,0:T(8,128)(2,1)S(1)}, u32[]{:S(2)}, u32[]{:S(2)}) async-start(bf16[32,32,384]{2,1,0:T(8,128)(2,1)} %shard_map.86), calls=%async_computation | async-start | bytes 1572864 | tf_op jit(solution)/shard_map/all_to_all | solution.py:709
  63.1 1.0 constant_dynamic-update-slice_fusion.5
  64.1 1.0 constant_dynamic-update-slice_fusion.4.refs_2_
  65.9 1.6 collective-permute-done.15.refs_5_
  67.5 0.9 copy-done.12
  68.4 8.4 %shard_map.88 = (bf16[2,8,4,32,1536]{4,3,2,1,0:T(8,128)(2,1)}, f32[1024,384]{1,0:T(8,128)}, f32[8,128]{1,0:T(8,128)}, f32[8,128]{1,0:T(8,128)}) custom-call(s32[2]{0:T(128)} %pad_add_fusion.at_ref, bf16[8,32,1536]{2,1,0:T(8,128)(2,1)} %copy-done.1, bf16[16,32,1536]{2,1,0:T(8,128)(2,1)} %copy-done.9, bf16[8,32,1536]{2,1,0:T(8,128)(2,1)} %copy-done.10, ...), custom_call_target="tpu_custom_call" | custom-call | tf_op jit(solution)/shard_map/pallas_call | solution.py:131
  77.1 1.2 collective-permute-done.16.refs_1_
  79.0 2.8 %collective-permute-start.19 = (f32[8,128]{1,0:T(8,128)S(1)}, f32[8,128]{1,0:T(8,128)S(1)}, u32[]{:S(2)}, u32[]{:S(2)}) collective-permute-start(f32[8,128]{1,0:T(8,128)S(1)} %shard_map.89.refs_0_), channel_id=1, source_target_pairs={{0,6},{1,7},{2,0},{3,1},{4,2},{5,3},{6,4},{7,5},{8,14},{9,15},{10,... | collective-permute-start | bytes 12296 | tf_op jit(solution)/shard_map/ppermute | solution.py:713
  83.6 3.4 %collective-permute-done.18.refs_2_ = f32[8,128]{1,0:T(8,128)S(1)} collective-permute-done((f32[8,128]{1,0:T(8,128)S(1)}, f32[8,128]{1,0:T(8,128)S(1)}, u32[]{:S(2)}, u32[]{:S(2)}) %collective-permute-start.18) | collective-permute-done | bytes 4128 | tf_op jit(solution)/shard_map/ppermute | solution.py:713
  88.2 1.4 shard_map.90
  89.6 9.8 %all-to-all-start.1 = ((f32[32,8,128]{2,1,0:T(8,128)}), f32[32,8,128]{2,1,0:T(8,128)S(1)}, u32[]{:S(2)}, u32[]{:S(2)}) async-start(f32[32,8,128]{2,1,0:T(8,128)} %shard_map.90), calls=%async_computation.1 | async-start | bytes 262144 | tf_op jit(solution)/shard_map/all_to_all | solution.py:718
  99.4 9.4 %shard_map.91 = (f32[1024,384]{1,0:T(8,128)}, f32[8,128]{1,0:T(8,128)}, f32[1,1]{1,0:T(1,128)}) custom-call(f32[8,128]{1,0:T(8,128)} %get-tuple-element.50.top_ref, f32[1024,384]{1,0:T(8,128)} %get-tuple-element.51.far_ref, bf16[1024,384]{1,0:T(8,128)(2,1)} %bitcast.15, f32[1,1024]{1,0:T(1,128)} %bitcast.18, f32[1,1024]{1,0:T(1,128)} %compare_convert_fusion.live_ref), custom_call_target="tpu_custom_call" | custom-call | flops 3221225472 | bytes 8388608 | tf_op jit(solution)/shard_map/pallas_call | solution.py:244
  109.5 7.2 %shard_map.92 = (bf16[1024,384]{1,0:T(8,128)(2,1)}, bf16[1024,768]{1,0:T(8,128)(2,1)}, f32[1,1]{1,0:T(1,128)}) custom-call(f32[32,8,128]{2,1,0:T(8,128)} %copy-done.13, f32[8,128]{1,0:T(8,128)} %get-tuple-element.50.top_ref, f32[8,128]{1,0:T(8,128)} %get-tuple-element.55.mass_ref, f32[1,1]{1,0:T(1,128)} %get-tuple-element.56.cross_ref, ...), custom_call_target="tpu_custom_call" | custom-call | tf_op jit(solution)/shard_map/pallas_call | solution.py:320
  117.3 2.1 %collective-permute-done.20.more_ref = f32[1,1]{1,0:T(1,128)} collective-permute-done((f32[1,1]{1,0:T(1,128)}, f32[1,1]{1,0:T(1,128)}, u32[]{:S(2)}, u32[]{:S(2)}) %collective-permute-start.20) | collective-permute-done | bytes 36 | tf_op jit(solution)/shard_map/ppermute | solution.py:723
  119.4 1.1 copy-done.3
  120.6 2.7 %shard_map.94 = (s16[528,384]{1,0:T(8,128)(2,1)S(1)}, s16[528,384]{1,0:T(8,128)(2,1)S(1)}, f32[1,128]{1,0:T(1,128)S(1)}) custom-call(f32[1,1]{1,0:T(1,128)} %get-tuple-element.59.loss_ref, f32[1,1]{1,0:T(1,128)} %collective-permute-done.20.more_ref, bf16[1024,384]{1,0:T(8,128)(2,1)S(1)} %copy-done.3, ...), custom_call_target="tpu_custom_call" | custom-call | tf_op jit(solution)/shard_map/pallas_call | solution.py:503
  123.3 3.2 %collective-permute-start.27 = (s16[528,384]{1,0:T(8,128)(2,1)S(1)}, s16[528,384]{1,0:T(8,128)(2,1)S(1)}, u32[]{:S(2)}, u32[]{:S(2)}) collective-permute-start(s16[528,384]{1,0:T(8,128)(2,1)S(1)} %get-tuple-element.70), channel_id=1, source_target_pairs={{0,6},{1,7},{2,0},{3,1},{4,2},{5,3},{6,4},{7,5},{8,14},{9,15},{10,... | collective-permute-start | bytes 1216520 | tf_op jit(solution)/shard_map/ppermute | solution.py:727
  126.6 2.6 %shard_map.95 = (f32[512,384]{1,0:T(8,128)S(1)}, s16[528,384]{1,0:T(8,128)(2,1)S(1)}, s16[528,384]{1,0:T(8,128)(2,1)S(1)}, f32[512,384]{1,0:T(8,128)S(1)}, f32[1024,384]{1,0:T(8,128)S(1)}) custom-call(f32[1,128]{1,0:T(1,128)S(1)} %get-tuple-element.63.loss_ref, bf16[1024,384]{1,0:T(8,128)(2,1)S(1)} %copy-done.3, ...), custom_call_target="tpu_custom_call" | custom-call | tf_op jit(solution)/shard_map/pallas_call | solution.py:515
  129.2 2.0 %collective-permute-start.26 = (s16[528,384]{1,0:T(8,128)(2,1)S(1)}, s16[528,384]{1,0:T(8,128)(2,1)S(1)}, u32[]{:S(2)}, u32[]{:S(2)}) collective-permute-start(s16[528,384]{1,0:T(8,128)(2,1)S(1)} %get-tuple-element.68), channel_id=1, source_target_pairs={{0,2},{1,3},{2,4},{3,5},{4,6},{5,7},{6,0},{7,1},{8,10},{9,11},{10,... | collective-permute-start | bytes 1216520 | tf_op jit(solution)/shard_map/ppermute | solution.py:729
  131.2 5.5 %collective-permute-done.23.got_ref = s16[528,384]{1,0:T(8,128)(2,1)S(1)} collective-permute-done((s16[528,384]{1,0:T(8,128)(2,1)S(1)}, s16[528,384]{1,0:T(8,128)(2,1)S(1)}, u32[]{:S(2)}, u32[]{:S(2)}) %collective-permute-start.23) | collective-permute-done | bytes 405536 | tf_op jit(solution)/shard_map/ppermute | solution.py:726
  137.7 3.3 %collective-permute-start.28 = (s16[528,384]{1,0:T(8,128)(2,1)S(1)}, s16[528,384]{1,0:T(8,128)(2,1)S(1)}, u32[]{:S(2)}, u32[]{:S(2)}) collective-permute-start(s16[528,384]{1,0:T(8,128)(2,1)S(1)} %shard_map.97), channel_id=1, source_target_pairs={{0,6},{1,7},{2,0},{3,1},{4,2},{5,3},{6,4},{7,5},{8,14},{9,15},{10,... | collective-permute-start | bytes 1216520 | tf_op jit(solution)/shard_map/ppermute | solution.py:732
  140.9 4.1 %collective-permute-done.25.low_l = s16[528,384]{1,0:T(8,128)(2,1)S(1)} collective-permute-done((s16[528,384]{1,0:T(8,128)(2,1)S(1)}, s16[528,384]{1,0:T(8,128)(2,1)S(1)}, u32[]{:S(2)}, u32[]{:S(2)}) %collective-permute-start.25) | collective-permute-done | bytes 405536 | tf_op jit(solution)/shard_map/ppermute | solution.py:730
  145.5 7.9 %collective-permute-done.24.low_r = s16[528,384]{1,0:T(8,128)(2,1)S(1)} collective-permute-done((s16[528,384]{1,0:T(8,128)(2,1)S(1)}, s16[528,384]{1,0:T(8,128)(2,1)S(1)}, u32[]{:S(2)}, u32[]{:S(2)}) %collective-permute-start.24) | collective-permute-done | bytes 405536 | tf_op jit(solution)/shard_map/ppermute | solution.py:731
  153.4 2.4 %shard_map.98 = s16[32,112,128]{2,1,0:T(8,128)(2,1)} custom-call(f32[1,128]{1,0:T(1,128)S(1)} %get-tuple-element.63.loss_ref, f32[1024,384]{1,0:T(8,128)S(1)} %get-tuple-element.64.own_ref, s16[528,384]{1,0:T(8,128)(2,1)S(1)} %collective-permute-done.24.low_r, s16[528,384]{1,0:T(8,128)(2,1)S(1)} %collective-permute-done.25.low_l, ...), custom_call_target="tpu_custom_call" | custom-call | tf_op jit(solution)/shard_map/pallas_call | solution.py:574
  155.8 9.9 %all-to-all-start.2 = ((s16[32,112,128]{2,1,0:T(8,128)(2,1)}), s16[32,112,128]{2,1,0:T(8,128)(2,1)S(1)}, u32[]{:S(2)}, u32[]{:S(2)}) async-start(s16[32,112,128]{2,1,0:T(8,128)(2,1)} %shard_map.98), calls=%async_computation.2 | async-start | bytes 1835008 | tf_op jit(solution)/shard_map/all_to_all | solution.py:735
  167.1 2.8 %copy-done.6 = bf16[2,8,4,32,1536]{4,3,2,1,0:T(8,128)(2,1)S(1)} copy-done((bf16[2,8,4,32,1536]{4,3,2,1,0:T(8,128)(2,1)S(1)}, bf16[2,8,4,32,1536]{4,3,2,1,0:T(8,128)(2,1)}, u32[]{:S(2)}) %copy-start.6) | copy-done | bytes 6291480
  169.8 9.1 %shard_map.93 = f32[9216,128]{1,0:T(8,128)} custom-call(s32[1]{0:T(128)} %bitcast.c_ref, bf16[2,1024,1536]{2,1,0:T(8,128)(2,1)S(1)} %bitcast.12, bf16[1024,768]{1,0:T(8,128)(2,1)S(1)} %copy-done.7), custom_call_target="tpu_custom_call" | custom-call | flops 4831838208 | bytes 12582912 | tf_op jit(solution)/shard_map/pallas_call | solution.py:628
  179.0 11.6 %all-to-all-done.2.x_ref = s16[32,112,128]{2,1,0:T(8,128)(2,1)S(1)} async-done(((s16[32,112,128]{2,1,0:T(8,128)(2,1)}), s16[32,112,128]{2,1,0:T(8,128)(2,1)S(1)}, u32[]{:S(2)}, u32[]{:S(2)}) %all-to-all-start.2) | async-done | bytes 917536 | tf_op jit(solution)/shard_map/all_to_all | solution.py:735
  190.5 1.2 shard_map.99
  (82 shorter events, 14.7 us)
Async XLA Ops:
  0.6 0.9 copy-start
  1.6 20.9 %collective-permute-start.6 = (bf16[32,1536]{1,0:T(8,128)(2,1)S(1)}, bf16[32,1536]{1,0:T(8,128)(2,1)S(1)}, u32[]{:S(2)}, u32[]{:S(2)}) collective-permute-start(bf16[32,1536]{1,0:T(8,128)(2,1)S(1)} %constant_dynamic-slice_fusion.refs_0_), channel_id=1, source_target_pairs={{0,224},{8,232},{16,240},{24,248},{32,0},{40,8},{48,16},{56,24},{6... | collective-permute-start | bytes 294920 | tf_op jit(solution)/shard_map/ppermute | solution.py:680
  7.5 11.7 %collective-permute-start.4 = (bf16[32,1536]{1,0:T(8,128)(2,1)S(1)}, bf16[32,1536]{1,0:T(8,128)(2,1)S(1)}, u32[]{:S(2)}, u32[]{:S(2)}) collective-permute-start(bf16[32,1536]{1,0:T(8,128)(2,1)S(1)} %constant_dynamic-slice_fusion.refs_0_), channel_id=1, source_target_pairs={{0,192},{8,200},{16,208},{24,216},{32,224},{40,232},{48,240},{56,2... | collective-permute-start | bytes 294920 | tf_op jit(solution)/shard_map/ppermute | solution.py:680
  9.0 8.7 %collective-permute-start.1 = (bf16[32,1536]{1,0:T(8,128)(2,1)S(1)}, bf16[32,1536]{1,0:T(8,128)(2,1)S(1)}, u32[]{:S(2)}, u32[]{:S(2)}) collective-permute-start(bf16[32,1536]{1,0:T(8,128)(2,1)S(1)} %constant_dynamic-slice_fusion.refs_0_), channel_id=1, source_target_pairs={{0,64},{8,72},{16,80},{24,88},{32,96},{40,104},{48,112},{56,120},{... | collective-permute-start | bytes 294920 | tf_op jit(solution)/shard_map/ppermute | solution.py:680
  10.4 12.1 %collective-permute-start = (bf16[32,1536]{1,0:T(8,128)(2,1)S(1)}, bf16[32,1536]{1,0:T(8,128)(2,1)S(1)}, u32[]{:S(2)}, u32[]{:S(2)}) collective-permute-start(bf16[32,1536]{1,0:T(8,128)(2,1)S(1)} %constant_dynamic-slice_fusion.refs_0_), channel_id=1, source_target_pairs={{0,32},{8,40},{16,48},{24,56},{32,64},{40,72},{48,80},{56,88},{64,... | collective-permute-start | bytes 294920 | tf_op jit(solution)/shard_map/ppermute | solution.py:680
  17.6 7.6 %collective-permute-start.3 = (bf16[32,1536]{1,0:T(8,128)(2,1)S(1)}, bf16[32,1536]{1,0:T(8,128)(2,1)S(1)}, u32[]{:S(2)}, u32[]{:S(2)}) collective-permute-start(bf16[32,1536]{1,0:T(8,128)(2,1)S(1)} %collective-permute-done.1.refs_2_), channel_id=1, source_target_pairs={{0,64},{8,72},{16,80},{24,88},{32,96},{40,104},{48,112},{56,120},{... | collective-permute-start | bytes 294920 | tf_op jit(solution)/shard_map/ppermute | solution.py:683
  17.8 8.8 %collective-permute-start.2 = (bf16[32,1536]{1,0:T(8,128)(2,1)S(1)}, bf16[32,1536]{1,0:T(8,128)(2,1)S(1)}, u32[]{:S(2)}, u32[]{:S(2)}) collective-permute-start(bf16[32,1536]{1,0:T(8,128)(2,1)S(1)} %collective-permute-done.1.refs_2_), channel_id=1, source_target_pairs={{0,32},{8,40},{16,48},{24,56},{32,64},{40,72},{48,80},{56,88},{64,... | collective-permute-start | bytes 294920 | tf_op jit(solution)/shard_map/ppermute | solution.py:682
  19.2 4.9 %collective-permute-start.5 = (bf16[32,1536]{1,0:T(8,128)(2,1)S(1)}, bf16[32,1536]{1,0:T(8,128)(2,1)S(1)}, u32[]{:S(2)}, u32[]{:S(2)}) collective-permute-start(bf16[32,1536]{1,0:T(8,128)(2,1)S(1)} %collective-permute-done.4.refs_6_), channel_id=1, source_target_pairs={{0,224},{8,232},{16,240},{24,248},{32,0},{40,8},{48,16},{56,24},{6... | collective-permute-start | bytes 294920 | tf_op jit(solution)/shard_map/ppermute | solution.py:684
  26.7 16.4 %copy-start.1 = (bf16[8,32,1536]{2,1,0:T(8,128)(2,1)}, bf16[8,32,1536]{2,1,0:T(8,128)(2,1)S(1)}, u32[]{:S(2)}) copy-start(bf16[8,32,1536]{2,1,0:T(8,128)(2,1)S(1)} %shard_map.85.refs_0_) | copy-start | bytes 2359300
  26.7 12.2 %collective-permute-start.8 = (bf16[4,32,1536]{2,1,0:T(8,128)(2,1)S(1)}, bf16[4,32,1536]{2,1,0:T(8,128)(2,1)}, u32[]{:S(2)}, u32[]{:S(2)}) collective-permute-start(bf16[4,32,1536]{2,1,0:T(8,128)(2,1)S(1)} %get-tuple-element.76), channel_id=1, source_target_pairs={{0,24},{8,0},{16,8},{24,16},{32,56},{40,32},{48,40},{56,48},{64,88... | collective-permute-start | bytes 1179656 | tf_op jit(solution)/shard_map/ppermute | solution.py:696
  27.3 13.1 %collective-permute-start.7 = (bf16[4,32,1536]{2,1,0:T(8,128)(2,1)S(1)}, bf16[4,32,1536]{2,1,0:T(8,128)(2,1)}, u32[]{:S(2)}, u32[]{:S(2)}) collective-permute-start(bf16[4,32,1536]{2,1,0:T(8,128)(2,1)S(1)} %get-tuple-element.77), channel_id=1, source_target_pairs={{0,8},{8,16},{16,24},{24,0},{32,40},{40,48},{48,56},{56,32},{64,72... | collective-permute-start | bytes 1179656 | tf_op jit(solution)/shard_map/ppermute | solution.py:695
  28.9 18.9 %collective-permute-start.9 = (bf16[4,32,1536]{2,1,0:T(8,128)(2,1)S(1)}, bf16[4,32,1536]{2,1,0:T(8,128)(2,1)S(1)}, u32[]{:S(2)}, u32[]{:S(2)}) collective-permute-start(bf16[4,32,1536]{2,1,0:T(8,128)(2,1)S(1)} %get-tuple-element.76), channel_id=1, source_target_pairs={{0,8},{8,16},{16,24},{24,0},{32,40},{40,48},{48,56},{56,32},{64,72... | collective-permute-start | bytes 1179656 | tf_op jit(solution)/shard_map/ppermute | solution.py:697
  30.4 17.3 %collective-permute-start.10 = (bf16[4,32,1536]{2,1,0:T(8,128)(2,1)S(1)}, bf16[4,32,1536]{2,1,0:T(8,128)(2,1)S(1)}, u32[]{:S(2)}, u32[]{:S(2)}) collective-permute-start(bf16[4,32,1536]{2,1,0:T(8,128)(2,1)S(1)} %get-tuple-element.77), channel_id=1, source_target_pairs={{0,24},{8,0},{16,8},{24,16},{32,56},{40,32},{48,40},{56,48},{64,88... | collective-permute-start | bytes 1179656 | tf_op jit(solution)/shard_map/ppermute | solution.py:698
  30.9 24.3 %collective-permute-start.13 = (bf16[8,32,1536]{2,1,0:T(8,128)(2,1)S(1)}, bf16[8,32,1536]{2,1,0:T(8,128)(2,1)S(1)}, u32[]{:S(2)}, u32[]{:S(2)}) collective-permute-start(bf16[8,32,1536]{2,1,0:T(8,128)(2,1)S(1)} %shard_map.85.refs_0_), channel_id=1, source_target_pairs={{0,1},{1,0},{2,3},{3,2},{4,5},{5,4},{6,7},{7,6},{8,9},{9,8},{10,11... | collective-permute-start | bytes 2359304 | tf_op jit(solution)/shard_map/ppermute | solution.py:707
  39.0 16.2 %collective-permute-start.12 = (bf16[4,32,1536]{2,1,0:T(8,128)(2,1)}, bf16[4,32,1536]{2,1,0:T(8,128)(2,1)}, u32[]{:S(2)}, u32[]{:S(2)}) collective-permute-start(bf16[4,32,1536]{2,1,0:T(8,128)(2,1)} %collective-permute-done.8), channel_id=1, source_target_pairs={{0,24},{8,0},{16,8},{24,16},{32,56},{40,32},{48,40},{56,48},{64,88... | collective-permute-start | bytes 1179656 | tf_op jit(solution)/shard_map/ppermute | solution.py:700
  40.4 14.7 %collective-permute-start.11 = (bf16[4,32,1536]{2,1,0:T(8,128)(2,1)}, bf16[4,32,1536]{2,1,0:T(8,128)(2,1)}, u32[]{:S(2)}, u32[]{:S(2)}) collective-permute-start(bf16[4,32,1536]{2,1,0:T(8,128)(2,1)} %collective-permute-done.7), channel_id=1, source_target_pairs={{0,8},{8,16},{16,24},{24,0},{32,40},{40,48},{48,56},{56,32},{64,72... | collective-permute-start | bytes 1179656 | tf_op jit(solution)/shard_map/ppermute | solution.py:699
  47.8 7.4 %copy-start.9 = (bf16[16,32,1536]{2,1,0:T(8,128)(2,1)}, bf16[16,32,1536]{2,1,0:T(8,128)(2,1)S(1)}, u32[]{:S(2)}) copy-start(bf16[16,32,1536]{2,1,0:T(8,128)(2,1)S(1)} %constant_dynamic-update-slice_fusion.refs_1_) | copy-start | bytes 4718596
  47.8 19.7 %collective-permute-start.14 = (bf16[16,32,1536]{2,1,0:T(8,128)(2,1)S(1)}, bf16[16,32,1536]{2,1,0:T(8,128)(2,1)}, u32[]{:S(2)}, u32[]{:S(2)}) collective-permute-start(bf16[16,32,1536]{2,1,0:T(8,128)(2,1)S(1)} %constant_dynamic-update-slice_fusion.refs_1_), channel_id=1, source_target_pairs={{0,1},{1,0},{2,3},{3,2},{4,5},{5,4},{6,7},{7,6},{8,9},{9,8},{10,11... | collective-permute-start | bytes 4718600 | tf_op jit(solution)/shard_map/ppermute | solution.py:707
  55.2 0.9 copy-start.11
  56.1 33.5 %all-to-all-start = ((bf16[32,32,384]{2,1,0:T(8,128)(2,1)}), bf16[32,32,384]{2,1,0:T(8,128)(2,1)S(1)}, u32[]{:S(2)}, u32[]{:S(2)}) async-start(bf16[32,32,384]{2,1,0:T(8,128)(2,1)} %shard_map.86), calls=%async_computation | async-start | bytes 1572864 | tf_op jit(solution)/shard_map/all_to_all | solution.py:709
  65.1 3.3 %copy-start.10 = (bf16[8,32,1536]{2,1,0:T(8,128)(2,1)}, bf16[8,32,1536]{2,1,0:T(8,128)(2,1)S(1)}, u32[]{:S(2)}) copy-start(bf16[8,32,1536]{2,1,0:T(8,128)(2,1)S(1)} %constant_dynamic-update-slice_fusion.4.refs_2_) | copy-start | bytes 2359300
  65.1 2.4 %collective-permute-start.15 = (bf16[8,32,1536]{2,1,0:T(8,128)(2,1)S(1)}, bf16[8,32,1536]{2,1,0:T(8,128)(2,1)S(1)}, u32[]{:S(2)}, u32[]{:S(2)}) collective-permute-start(bf16[8,32,1536]{2,1,0:T(8,128)(2,1)S(1)} %constant_dynamic-update-slice_fusion.4.refs_2_), channel_id=1, source_target_pairs={{0,1},{1,0},{2,3},{3,2},{4,5},{5,4},{6,7},{7,6},{8,9},{9,8},{10,11... | collective-permute-start | bytes 2359304 | tf_op jit(solution)/shard_map/ppermute | solution.py:707
  67.5 0.9 copy-start.12
  76.9 1.5 collective-permute-start.16
  78.3 0.7 copy-start.5
  79.0 8.5 %copy-start.4 = (f32[8,128]{1,0:T(8,128)}, f32[8,128]{1,0:T(8,128)S(1)}, u32[]{:S(2)}) copy-start(f32[8,128]{1,0:T(8,128)S(1)} %shard_map.89.refs_0_) | copy-start | bytes 12292
  79.0 4.5 %collective-permute-start.19 = (f32[8,128]{1,0:T(8,128)S(1)}, f32[8,128]{1,0:T(8,128)S(1)}, u32[]{:S(2)}, u32[]{:S(2)}) collective-permute-start(f32[8,128]{1,0:T(8,128)S(1)} %shard_map.89.refs_0_), channel_id=1, source_target_pairs={{0,6},{1,7},{2,0},{3,1},{4,2},{5,3},{6,4},{7,5},{8,14},{9,15},{10,... | collective-permute-start | bytes 12296 | tf_op jit(solution)/shard_map/ppermute | solution.py:713
  81.9 5.1 %collective-permute-start.18 = (f32[8,128]{1,0:T(8,128)S(1)}, f32[8,128]{1,0:T(8,128)S(1)}, u32[]{:S(2)}, u32[]{:S(2)}) collective-permute-start(f32[8,128]{1,0:T(8,128)S(1)} %shard_map.89.refs_0_), channel_id=1, source_target_pairs={{0,4},{1,5},{2,6},{3,7},{4,0},{5,1},{6,2},{7,3},{8,12},{9,13},{10,... | collective-permute-start | bytes 12296 | tf_op jit(solution)/shard_map/ppermute | solution.py:713
  82.7 4.8 %collective-permute-start.17 = (f32[8,128]{1,0:T(8,128)S(1)}, f32[8,128]{1,0:T(8,128)S(1)}, u32[]{:S(2)}, u32[]{:S(2)}) collective-permute-start(f32[8,128]{1,0:T(8,128)S(1)} %shard_map.89.refs_0_), channel_id=1, source_target_pairs={{0,2},{1,3},{2,4},{3,5},{4,6},{5,7},{6,0},{7,1},{8,10},{9,11},{10,... | collective-permute-start | bytes 12296 | tf_op jit(solution)/shard_map/ppermute | solution.py:713
  83.6 3.9 %copy-start.14 = (f32[8,128]{1,0:T(8,128)}, f32[8,128]{1,0:T(8,128)S(1)}, u32[]{:S(2)}) copy-start(f32[8,128]{1,0:T(8,128)S(1)} %collective-permute-done.19.refs_3_) | copy-start | bytes 12292
  89.6 29.8 %collective-permute-start.22 = (bf16[384,1536]{1,0:T(8,128)(2,1)}, bf16[384,1536]{1,0:T(8,128)(2,1)S(1)}, u32[]{:S(2)}, u32[]{:S(2)}) collective-permute-start(bf16[384,1536]{1,0:T(8,128)(2,1)} %get-tuple-element.62), channel_id=1, source_target_pairs={{0,1},{1,0},{2,3},{3,2},{4,5},{5,4},{6,7},{7,6},{8,9},{9,8},{10,11... | collective-permute-start | bytes 3538952 | tf_op jit(solution)/shard_map/ppermute | solution.py:716
  89.6 9.8 %copy-start.8 = (bf16[32,32,384]{2,1,0:T(8,128)(2,1)}, bf16[32,32,384]{2,1,0:T(8,128)(2,1)S(1)}, u32[]{:S(2)}) copy-start(bf16[32,32,384]{2,1,0:T(8,128)(2,1)S(1)} %all-to-all-done) | copy-start | bytes 2359300
  89.6 19.2 %all-to-all-start.1 = ((f32[32,8,128]{2,1,0:T(8,128)}), f32[32,8,128]{2,1,0:T(8,128)S(1)}, u32[]{:S(2)}, u32[]{:S(2)}) async-start(f32[32,8,128]{2,1,0:T(8,128)} %shard_map.90), calls=%async_computation.1 | async-start | bytes 262144 | tf_op jit(solution)/shard_map/all_to_all | solution.py:718
  108.8 10.6 %copy-start.2 = (bf16[384,1536]{1,0:T(8,128)(2,1)S(1)}, bf16[384,1536]{1,0:T(8,128)(2,1)}, u32[]{:S(2)}) copy-start(bf16[384,1536]{1,0:T(8,128)(2,1)} %get-tuple-element.61.w_own) | copy-start | bytes 3538948
  108.9 0.6 copy-start.13
  116.7 2.7 %collective-permute-start.21 = (bf16[1024,384]{1,0:T(8,128)(2,1)}, bf16[1024,384]{1,0:T(8,128)(2,1)S(1)}, u32[]{:S(2)}, u32[]{:S(2)}) collective-permute-start(bf16[1024,384]{1,0:T(8,128)(2,1)} %get-tuple-element.60.own_ref), channel_id=1, source_target_pairs={{0,1},{1,0},{2,3},{3,2},{4,5},{5,4},{6,7},{7,6},{8,9},{9,8},{10,11... | collective-permute-start | bytes 2359304 | tf_op jit(solution)/shard_map/ppermute | solution.py:724
  116.8 2.6 %collective-permute-start.20 = (f32[1,1]{1,0:T(1,128)}, f32[1,1]{1,0:T(1,128)}, u32[]{:S(2)}, u32[]{:S(2)}) collective-permute-start(f32[1,1]{1,0:T(1,128)} %get-tuple-element.59.loss_ref), channel_id=1, source_target_pairs={{0,1},{1,0},{2,3},{3,2},{4,5},{5,4},{6,7},{7,6},{8,9},{9,8},{10,11... | collective-permute-start | bytes 20 | tf_op jit(solution)/shard_map/ppermute | solution.py:723
  119.4 1.1 copy-start.3
  123.3 13.5 %collective-permute-start.23 = (s16[528,384]{1,0:T(8,128)(2,1)S(1)}, s16[528,384]{1,0:T(8,128)(2,1)S(1)}, u32[]{:S(2)}, u32[]{:S(2)}) collective-permute-start(s16[528,384]{1,0:T(8,128)(2,1)S(1)} %get-tuple-element.66), channel_id=1, source_target_pairs={{0,2},{1,3},{2,4},{3,5},{4,6},{5,7},{6,0},{7,1},{8,10},{9,11},{10,... | collective-permute-start | bytes 1216520 | tf_op jit(solution)/shard_map/ppermute | solution.py:726
  123.3 13.9 %collective-permute-start.27 = (s16[528,384]{1,0:T(8,128)(2,1)S(1)}, s16[528,384]{1,0:T(8,128)(2,1)S(1)}, u32[]{:S(2)}, u32[]{:S(2)}) collective-permute-start(s16[528,384]{1,0:T(8,128)(2,1)S(1)} %get-tuple-element.70), channel_id=1, source_target_pairs={{0,6},{1,7},{2,0},{3,1},{4,2},{5,3},{6,4},{7,5},{8,14},{9,15},{10,... | collective-permute-start | bytes 1216520 | tf_op jit(solution)/shard_map/ppermute | solution.py:727
  129.1 15.9 %collective-permute-start.25 = (s16[528,384]{1,0:T(8,128)(2,1)S(1)}, s16[528,384]{1,0:T(8,128)(2,1)S(1)}, u32[]{:S(2)}, u32[]{:S(2)}) collective-permute-start(s16[528,384]{1,0:T(8,128)(2,1)S(1)} %get-tuple-element.67), channel_id=1, source_target_pairs={{0,6},{1,7},{2,0},{3,1},{4,2},{5,3},{6,4},{7,5},{8,14},{9,15},{10,... | collective-permute-start | bytes 1216520 | tf_op jit(solution)/shard_map/ppermute | solution.py:730
  129.2 16.2 %collective-permute-start.26 = (s16[528,384]{1,0:T(8,128)(2,1)S(1)}, s16[528,384]{1,0:T(8,128)(2,1)S(1)}, u32[]{:S(2)}, u32[]{:S(2)}) collective-permute-start(s16[528,384]{1,0:T(8,128)(2,1)S(1)} %get-tuple-element.68), channel_id=1, source_target_pairs={{0,2},{1,3},{2,4},{3,5},{4,6},{5,7},{6,0},{7,1},{8,10},{9,11},{10,... | collective-permute-start | bytes 1216520 | tf_op jit(solution)/shard_map/ppermute | solution.py:729
  137.2 16.2 %collective-permute-start.24 = (s16[528,384]{1,0:T(8,128)(2,1)S(1)}, s16[528,384]{1,0:T(8,128)(2,1)S(1)}, u32[]{:S(2)}, u32[]{:S(2)}) collective-permute-start(s16[528,384]{1,0:T(8,128)(2,1)S(1)} %shard_map.96), channel_id=1, source_target_pairs={{0,2},{1,3},{2,4},{3,5},{4,6},{5,7},{6,0},{7,1},{8,10},{9,11},{10,... | collective-permute-start | bytes 1216520 | tf_op jit(solution)/shard_map/ppermute | solution.py:731
  137.7 15.7 %collective-permute-start.28 = (s16[528,384]{1,0:T(8,128)(2,1)S(1)}, s16[528,384]{1,0:T(8,128)(2,1)S(1)}, u32[]{:S(2)}, u32[]{:S(2)}) collective-permute-start(s16[528,384]{1,0:T(8,128)(2,1)S(1)} %shard_map.97), channel_id=1, source_target_pairs={{0,6},{1,7},{2,0},{3,1},{4,2},{5,3},{6,4},{7,5},{8,14},{9,15},{10,... | collective-permute-start | bytes 1216520 | tf_op jit(solution)/shard_map/ppermute | solution.py:732
  155.8 9.9 %copy-start.17 = (s32[32]{0:T(128)S(1)}, s32[32]{0:T(128)}, u32[]{:S(2)}) copy-start(s32[32]{0:T(128)} %param.9) | copy-start | bytes 388
  155.8 11.2 %copy-start.7 = (bf16[1024,768]{1,0:T(8,128)(2,1)S(1)}, bf16[1024,768]{1,0:T(8,128)(2,1)}, u32[]{:S(2)}) copy-start(bf16[1024,768]{1,0:T(8,128)(2,1)} %get-tuple-element.58.sums_ref) | copy-start | bytes 4718596
  155.8 34.7 %all-to-all-start.2 = ((s16[32,112,128]{2,1,0:T(8,128)(2,1)}), s16[32,112,128]{2,1,0:T(8,128)(2,1)S(1)}, u32[]{:S(2)}, u32[]{:S(2)}) async-start(s16[32,112,128]{2,1,0:T(8,128)(2,1)} %shard_map.98), calls=%async_computation.2 | async-start | bytes 1835008 | tf_op jit(solution)/shard_map/all_to_all | solution.py:735
  167.0 2.8 %copy-start.6 = (bf16[2,8,4,32,1536]{4,3,2,1,0:T(8,128)(2,1)S(1)}, bf16[2,8,4,32,1536]{4,3,2,1,0:T(8,128)(2,1)}, u32[]{:S(2)}) copy-start(bf16[2,8,4,32,1536]{4,3,2,1,0:T(8,128)(2,1)} %get-tuple-element.44) | copy-start | bytes 18874372
  (2 other events, 1.2 us)

commit v4 on v3

--- a/solution.py
+++ b/solution.py
@@ -696,13 +696,15 @@
     high3 = lax.ppermute(high0, "trainer", along_y(-1))
     high1 = lax.ppermute(high0, "trainer", along_y(1))
     low3 = lax.ppermute(low0, "trainer", along_y(-1))
+    at_cx, _ = lax.optimization_barrier((at_cx, plane))
+    w_own, w_give = turn_weights(at_cx, weight.reshape(4, 2, LOCAL, LOCAL))
+    low1, high3, w_own, w_give = lax.optimization_barrier((low1, high3, w_own, w_give))
     low2 = lax.ppermute(low1, "trainer", along_y(1))
     high2 = lax.ppermute(high3, "trainer", along_y(-1))
+    targets, _ = lax.optimization_barrier((targets, (low1, high3)))
+    split = split_targets(targets[:, 0, :])
+    high1, split = lax.optimization_barrier((high1, split))
     middle = jnp.concatenate([low1, high3, high1, low3])
-    at_cx, targets, _ = lax.optimization_barrier((at_cx, targets, middle))
-    split = split_targets(targets[:, 0, :])
-    w_own, w_give = turn_weights(at_cx, weight.reshape(4, 2, LOCAL, LOCAL))
-    low2, split, w_own, w_give = lax.optimization_barrier((low2, split, w_own, w_give))
     pieces = [plane, middle, jnp.concatenate([low2, high2])]
     pieces += [lax.ppermute(p, "vocab", PAIR) for p in pieces]
     split, _ = lax.optimization_barrier((split, (w_give, low2, high2, pieces[3])))

time: 194 us -> 192 us (0.990)
  waiting for transfers between devices: 60.9 us -> 55.5 us
    ppermute x1, waiting for transfers between devices: 8.1 us -> 2.49 us  [on_device(): high3 = lax.ppermute(high0, 'trainer', along_y(-1))]
    ppermute x1, waiting for transfers between devices: 4.59 us -> 1.74 us  [on_device(): high1 = lax.ppermute(high0, 'trainer', along_y(1))]
    ppermute x1, waiting for transfers between devices: 0.01 us -> 2.4 us  [on_device(): low2 = lax.ppermute(low1, 'trainer', along_y(1))]
  transfers between devices with their start and end apart: 32 -> 32, of which waited for: 17 -> 19; matrix products, arithmetic and copies ran while one was open for 5% -> 5% of each run, Pallas kernels for 23% -> 24%
where the time goes in v4:
time: 192 us; the launch traced here: 191 us
  starting transfers between devices  61.4 us (32%)
  waiting for transfers between devices  55.5 us (29%)
  Pallas kernels  51.8 us (27%)
  local copies, waits for them, and re-layouts  14.8 us (8%)
  other arithmetic  3.81 us (2%)
  between operations  3.42 us (2%)
    unnamed x40, local copies, waits for them, and re-layouts  11.9 us
    all_to_all x1, waiting for transfers between devices, on_device(): lax.all_to_all(packed, 'trainer', split_axis=0, concat_axis=0, tiled=True)  11.5 us
    all_to_all x1, starting transfers between devices, on_device(): lax.all_to_all(packed, 'trainer', split_axis=0, concat_axis=0, tiled=True)  9.91 us
    all_to_all x1, starting transfers between devices, on_device(): lax.all_to_all(stats, 'trainer', split_axis=0, concat_axis=0, tiled=True)  9.79 us
    pallas_call x1, Pallas kernels, select_rows(): pl.pallas_call(select_kernel, out_shape=(jax.ShapeDtypeStruct((ROWS, LOCA...  9.4 us
    pallas_call x1, Pallas kernels, head_gradient(): pl.pallas_call(head_kernel, grid_spec=pltpu.PrefetchScalarGridSpec(num_sc...  9.12 us
    ppermute x4, starting transfers between devices, on_device(): lax.ppermute(half, 'trainer', along_z(k))  8.86 us
    pallas_call x1, Pallas kernels, logits_and_stats(): pl.pallas_call(logit_kernel, out_shape=(jax.ShapeDtypeStruct((2, Z, Y, SL...  8.53 us
  transfers between devices with their start and end apart: 32, of which 19 were waited for; matrix products, arithmetic and copies ran while one was open for 5% of the time, Pallas kernels for 24%

profile of v4, /device:TPU:8, one launch (start us, length us, event | category | flops | bytes accessed | tf_op | source)
XLA Modules:
  0.0 190.8 jit_solution(4161653914885927607)
XLA Ops:
  1.6 5.9 %collective-permute-start.6 = (bf16[32,1536]{1,0:T(8,128)(2,1)S(1)}, bf16[32,1536]{1,0:T(8,128)(2,1)S(1)}, u32[]{:S(2)}, u32[]{:S(2)}) collective-permute-start(bf16[32,1536]{1,0:T(8,128)(2,1)S(1)} %constant_dynamic-slice_fusion.refs_0_), channel_id=1, source_target_pairs={{0,224},{8,232},{16,240},{24,248},{32,0},{40,8},{48,16},{56,24},{6... | collective-permute-start | bytes 294920 | tf_op jit(solution)/shard_map/ppermute | solution.py:680
  7.5 1.5 collective-permute-start.4
  9.0 1.5 collective-permute-start.1
  10.4 1.3 add_convert_fusion
  12.5 5.1 %collective-permute-done.1.refs_2_ = bf16[32,1536]{1,0:T(8,128)(2,1)S(1)} collective-permute-done((bf16[32,1536]{1,0:T(8,128)(2,1)S(1)}, bf16[32,1536]{1,0:T(8,128)(2,1)S(1)}, u32[]{:S(2)}, u32[]{:S(2)}) %collective-permute-start.1) | collective-permute-done | bytes 98336 | tf_op jit(solution)/shard_map/ppermute | solution.py:680
  17.8 1.4 collective-permute-start.2
  19.2 2.7 %collective-permute-start.5 = (bf16[32,1536]{1,0:T(8,128)(2,1)S(1)}, bf16[32,1536]{1,0:T(8,128)(2,1)S(1)}, u32[]{:S(2)}, u32[]{:S(2)}) collective-permute-start(bf16[32,1536]{1,0:T(8,128)(2,1)S(1)} %collective-permute-done.4.refs_6_), channel_id=1, source_target_pairs={{0,224},{8,232},{16,240},{24,248},{32,0},{40,8},{48,16},{56,24},{6... | collective-permute-start | bytes 294920 | tf_op jit(solution)/shard_map/ppermute | solution.py:684
  22.5 1.6 collective-permute-done.5.refs_5_
  24.1 1.2 collective-permute-done.3.refs_4_
  25.3 1.3 collective-permute-done.2.refs_3_
  26.7 1.0 fusion
  28.2 1.6 collective-permute-start.7
  29.7 1.6 collective-permute-start.9
  32.4 4.1 %shard_map.86 = (bf16[384,1536]{1,0:T(8,128)(2,1)}, bf16[384,1536]{1,0:T(8,128)(2,1)}) custom-call(s32[2]{0:T(128)} %pad_add_fusion.1.at_ref, bf16[4,2,384,384]{3,2,1,0:T(8,128)(2,1)} %bitcast.13), custom_call_target="tpu_custom_call" | custom-call | tf_op jit(solution)/shard_map/pallas_call | solution.py:431
  36.6 2.5 %collective-permute-done.8 = bf16[4,32,1536]{2,1,0:T(8,128)(2,1)} collective-permute-done((bf16[4,32,1536]{2,1,0:T(8,128)(2,1)}, bf16[4,32,1536]{2,1,0:T(8,128)(2,1)}, u32[]{:S(2)}, u32[]{:S(2)}) %collective-permute-start.8) | collective-permute-done | bytes 393248 | tf_op jit(solution)/shard_map/ppermute | solution.py:696
  39.0 1.4 collective-permute-done.7
  40.8 2.7 %collective-permute-start.12 = (bf16[4,32,1536]{2,1,0:T(8,128)(2,1)}, bf16[4,32,1536]{2,1,0:T(8,128)(2,1)}, u32[]{:S(2)}, u32[]{:S(2)}) collective-permute-start(bf16[4,32,1536]{2,1,0:T(8,128)(2,1)} %collective-permute-done.8), channel_id=1, source_target_pairs={{0,24},{8,0},{16,8},{24,16},{32,56},{40,32},{48,40},{56,48},{64,88... | collective-permute-start | bytes 1179656 | tf_op jit(solution)/shard_map/ppermute | solution.py:703
  43.4 2.1 %shard_map.87 = bf16[32,32,384]{2,1,0:T(8,128)(2,1)} custom-call(bf16[32,12288]{1,0:T(8,128)(2,1)} %bitcast.17), custom_call_target="tpu_custom_call" | custom-call | tf_op jit(solution)/shard_map/pallas_call | solution.py:39
  46.6 1.7 collective-permute-done.9
  49.3 1.0 constant_dynamic-update-slice_fusion.1
  50.7 2.4 %collective-permute-done.11 = bf16[4,32,1536]{2,1,0:T(8,128)(2,1)} collective-permute-done((bf16[4,32,1536]{2,1,0:T(8,128)(2,1)}, bf16[4,32,1536]{2,1,0:T(8,128)(2,1)}, u32[]{:S(2)}, u32[]{:S(2)}) %collective-permute-start.11) | collective-permute-done | bytes 393248 | tf_op jit(solution)/shard_map/ppermute | solution.py:702
  53.1 7.2 %all-to-all-start = ((bf16[32,32,384]{2,1,0:T(8,128)(2,1)}), bf16[32,32,384]{2,1,0:T(8,128)(2,1)S(1)}, u32[]{:S(2)}, u32[]{:S(2)}) async-start(bf16[32,32,384]{2,1,0:T(8,128)(2,1)} %shard_map.87), calls=%async_computation | async-start | bytes 1572864 | tf_op jit(solution)/shard_map/all_to_all | solution.py:711
  61.3 1.0 constant_dynamic-update-slice_fusion.4.refs_2_
  63.1 1.6 collective-permute-done.15.refs_5_
  65.7 8.5 %shard_map.88 = (bf16[2,8,4,32,1536]{4,3,2,1,0:T(8,128)(2,1)}, f32[1024,384]{1,0:T(8,128)}, f32[8,128]{1,0:T(8,128)}, f32[8,128]{1,0:T(8,128)}) custom-call(s32[2]{0:T(128)} %pad_add_fusion.at_ref, bf16[8,32,1536]{2,1,0:T(8,128)(2,1)} %copy-done.1, bf16[16,32,1536]{2,1,0:T(8,128)(2,1)} %copy-done.9, bf16[8,32,1536]{2,1,0:T(8,128)(2,1)} %copy-done.10, ...), custom_call_target="tpu_custom_call" | custom-call | tf_op jit(solution)/shard_map/pallas_call | solution.py:131
  74.5 1.2 collective-permute-done.16.refs_1_
  76.4 2.8 %collective-permute-start.19 = (f32[8,128]{1,0:T(8,128)S(1)}, f32[8,128]{1,0:T(8,128)S(1)}, u32[]{:S(2)}, u32[]{:S(2)}) collective-permute-start(f32[8,128]{1,0:T(8,128)S(1)} %shard_map.89.refs_0_), channel_id=1, source_target_pairs={{0,6},{1,7},{2,0},{3,1},{4,2},{5,3},{6,4},{7,5},{8,14},{9,15},{10,... | collective-permute-start | bytes 12296 | tf_op jit(solution)/shard_map/ppermute | solution.py:715
  80.9 3.4 %collective-permute-done.18.refs_2_ = f32[8,128]{1,0:T(8,128)S(1)} collective-permute-done((f32[8,128]{1,0:T(8,128)S(1)}, f32[8,128]{1,0:T(8,128)S(1)}, u32[]{:S(2)}, u32[]{:S(2)}) %collective-permute-start.18) | collective-permute-done | bytes 4128 | tf_op jit(solution)/shard_map/ppermute | solution.py:715
  85.5 1.4 shard_map.90
  86.9 9.8 %all-to-all-start.1 = ((f32[32,8,128]{2,1,0:T(8,128)}), f32[32,8,128]{2,1,0:T(8,128)S(1)}, u32[]{:S(2)}, u32[]{:S(2)}) async-start(f32[32,8,128]{2,1,0:T(8,128)} %shard_map.90), calls=%async_computation.1 | async-start | bytes 262144 | tf_op jit(solution)/shard_map/all_to_all | solution.py:720
  96.7 9.4 %shard_map.91 = (f32[1024,384]{1,0:T(8,128)}, f32[8,128]{1,0:T(8,128)}, f32[1,1]{1,0:T(1,128)}) custom-call(f32[8,128]{1,0:T(8,128)} %get-tuple-element.54.top_ref, f32[1024,384]{1,0:T(8,128)} %get-tuple-element.55.far_ref, bf16[1024,384]{1,0:T(8,128)(2,1)} %bitcast.15, f32[1,1024]{1,0:T(1,128)} %bitcast.18, f32[1,1024]{1,0:T(1,128)} %compare_convert_fusion.live_ref), custom_call_target="tpu_custom_call" | custom-call | flops 3221225472 | bytes 8388608 | tf_op jit(solution)/shard_map/pallas_call | solution.py:244
  106.8 7.4 %shard_map.92 = (bf16[1024,384]{1,0:T(8,128)(2,1)}, bf16[1024,768]{1,0:T(8,128)(2,1)}, f32[1,1]{1,0:T(1,128)}) custom-call(f32[32,8,128]{2,1,0:T(8,128)} %copy-done.13, f32[8,128]{1,0:T(8,128)} %get-tuple-element.54.top_ref, f32[8,128]{1,0:T(8,128)} %get-tuple-element.59.mass_ref, f32[1,1]{1,0:T(1,128)} %get-tuple-element.60.cross_ref, ...), custom_call_target="tpu_custom_call" | custom-call | tf_op jit(solution)/shard_map/pallas_call | solution.py:320
  114.8 1.9 %collective-permute-done.20.more_ref = f32[1,1]{1,0:T(1,128)} collective-permute-done((f32[1,1]{1,0:T(1,128)}, f32[1,1]{1,0:T(1,128)}, u32[]{:S(2)}, u32[]{:S(2)}) %collective-permute-start.20) | collective-permute-done | bytes 36 | tf_op jit(solution)/shard_map/ppermute | solution.py:725
  116.8 1.1 copy-done.3
  117.9 2.7 %shard_map.94 = (s16[528,384]{1,0:T(8,128)(2,1)S(1)}, s16[528,384]{1,0:T(8,128)(2,1)S(1)}, f32[1,128]{1,0:T(1,128)S(1)}) custom-call(f32[1,1]{1,0:T(1,128)} %get-tuple-element.63.loss_ref, f32[1,1]{1,0:T(1,128)} %collective-permute-done.20.more_ref, bf16[1024,384]{1,0:T(8,128)(2,1)S(1)} %copy-done.3, ...), custom_call_target="tpu_custom_call" | custom-call | tf_op jit(solution)/shard_map/pallas_call | solution.py:503
  120.7 3.2 %collective-permute-start.27 = (s16[528,384]{1,0:T(8,128)(2,1)S(1)}, s16[528,384]{1,0:T(8,128)(2,1)S(1)}, u32[]{:S(2)}, u32[]{:S(2)}) collective-permute-start(s16[528,384]{1,0:T(8,128)(2,1)S(1)} %get-tuple-element.74), channel_id=1, source_target_pairs={{0,6},{1,7},{2,0},{3,1},{4,2},{5,3},{6,4},{7,5},{8,14},{9,15},{10,... | collective-permute-start | bytes 1216520 | tf_op jit(solution)/shard_map/ppermute | solution.py:729
  123.9 2.6 %shard_map.95 = (f32[512,384]{1,0:T(8,128)S(1)}, s16[528,384]{1,0:T(8,128)(2,1)S(1)}, s16[528,384]{1,0:T(8,128)(2,1)S(1)}, f32[512,384]{1,0:T(8,128)S(1)}, f32[1024,384]{1,0:T(8,128)S(1)}) custom-call(f32[1,128]{1,0:T(1,128)S(1)} %get-tuple-element.67.loss_ref, bf16[1024,384]{1,0:T(8,128)(2,1)S(1)} %copy-done.3, ...), custom_call_target="tpu_custom_call" | custom-call | tf_op jit(solution)/shard_map/pallas_call | solution.py:515
  126.6 2.0 %collective-permute-start.26 = (s16[528,384]{1,0:T(8,128)(2,1)S(1)}, s16[528,384]{1,0:T(8,128)(2,1)S(1)}, u32[]{:S(2)}, u32[]{:S(2)}) collective-permute-start(s16[528,384]{1,0:T(8,128)(2,1)S(1)} %get-tuple-element.72), channel_id=1, source_target_pairs={{0,2},{1,3},{2,4},{3,5},{4,6},{5,7},{6,0},{7,1},{8,10},{9,11},{10,... | collective-permute-start | bytes 1216520 | tf_op jit(solution)/shard_map/ppermute | solution.py:731
  128.6 5.5 %collective-permute-done.23.got_ref = s16[528,384]{1,0:T(8,128)(2,1)S(1)} collective-permute-done((s16[528,384]{1,0:T(8,128)(2,1)S(1)}, s16[528,384]{1,0:T(8,128)(2,1)S(1)}, u32[]{:S(2)}, u32[]{:S(2)}) %collective-permute-start.23) | collective-permute-done | bytes 405536 | tf_op jit(solution)/shard_map/ppermute | solution.py:728
  135.0 3.3 %collective-permute-start.28 = (s16[528,384]{1,0:T(8,128)(2,1)S(1)}, s16[528,384]{1,0:T(8,128)(2,1)S(1)}, u32[]{:S(2)}, u32[]{:S(2)}) collective-permute-start(s16[528,384]{1,0:T(8,128)(2,1)S(1)} %shard_map.97), channel_id=1, source_target_pairs={{0,6},{1,7},{2,0},{3,1},{4,2},{5,3},{6,4},{7,5},{8,14},{9,15},{10,... | collective-permute-start | bytes 1216520 | tf_op jit(solution)/shard_map/ppermute | solution.py:734
  138.3 4.1 %collective-permute-done.25.low_l = s16[528,384]{1,0:T(8,128)(2,1)S(1)} collective-permute-done((s16[528,384]{1,0:T(8,128)(2,1)S(1)}, s16[528,384]{1,0:T(8,128)(2,1)S(1)}, u32[]{:S(2)}, u32[]{:S(2)}) %collective-permute-start.25) | collective-permute-done | bytes 405536 | tf_op jit(solution)/shard_map/ppermute | solution.py:732
  142.8 7.9 %collective-permute-done.24.low_r = s16[528,384]{1,0:T(8,128)(2,1)S(1)} collective-permute-done((s16[528,384]{1,0:T(8,128)(2,1)S(1)}, s16[528,384]{1,0:T(8,128)(2,1)S(1)}, u32[]{:S(2)}, u32[]{:S(2)}) %collective-permute-start.24) | collective-permute-done | bytes 405536 | tf_op jit(solution)/shard_map/ppermute | solution.py:733
  150.7 2.4 %shard_map.98 = s16[32,112,128]{2,1,0:T(8,128)(2,1)} custom-call(f32[1,128]{1,0:T(1,128)S(1)} %get-tuple-element.67.loss_ref, f32[1024,384]{1,0:T(8,128)S(1)} %get-tuple-element.68.own_ref, s16[528,384]{1,0:T(8,128)(2,1)S(1)} %collective-permute-done.24.low_r, s16[528,384]{1,0:T(8,128)(2,1)S(1)} %collective-permute-done.25.low_l, ...), custom_call_target="tpu_custom_call" | custom-call | tf_op jit(solution)/shard_map/pallas_call | solution.py:574
  153.2 9.9 %all-to-all-start.2 = ((s16[32,112,128]{2,1,0:T(8,128)(2,1)}), s16[32,112,128]{2,1,0:T(8,128)(2,1)S(1)}, u32[]{:S(2)}, u32[]{:S(2)}) async-start(s16[32,112,128]{2,1,0:T(8,128)(2,1)} %shard_map.98), calls=%async_computation.2 | async-start | bytes 1835008 | tf_op jit(solution)/shard_map/all_to_all | solution.py:737
  164.4 2.8 %copy-done.6 = bf16[2,8,4,32,1536]{4,3,2,1,0:T(8,128)(2,1)S(1)} copy-done((bf16[2,8,4,32,1536]{4,3,2,1,0:T(8,128)(2,1)S(1)}, bf16[2,8,4,32,1536]{4,3,2,1,0:T(8,128)(2,1)}, u32[]{:S(2)}) %copy-start.6) | copy-done | bytes 6291480
  167.2 9.1 %shard_map.93 = f32[9216,128]{1,0:T(8,128)} custom-call(s32[1]{0:T(128)} %bitcast.c_ref, bf16[2,1024,1536]{2,1,0:T(8,128)(2,1)S(1)} %bitcast.12, bf16[1024,768]{1,0:T(8,128)(2,1)S(1)} %copy-done.7), custom_call_target="tpu_custom_call" | custom-call | flops 4831838208 | bytes 12582912 | tf_op jit(solution)/shard_map/pallas_call | solution.py:628
  176.3 11.5 %all-to-all-done.2.x_ref = s16[32,112,128]{2,1,0:T(8,128)(2,1)S(1)} async-done(((s16[32,112,128]{2,1,0:T(8,128)(2,1)}), s16[32,112,128]{2,1,0:T(8,128)(2,1)S(1)}, u32[]{:S(2)}, u32[]{:S(2)}) %all-to-all-start.2) | async-done | bytes 917536 | tf_op jit(solution)/shard_map/all_to_all | solution.py:737
  187.8 1.2 shard_map.99
  (82 shorter events, 16.7 us)
Async XLA Ops:
  0.6 0.9 copy-start
  1.6 20.9 %collective-permute-start.6 = (bf16[32,1536]{1,0:T(8,128)(2,1)S(1)}, bf16[32,1536]{1,0:T(8,128)(2,1)S(1)}, u32[]{:S(2)}, u32[]{:S(2)}) collective-permute-start(bf16[32,1536]{1,0:T(8,128)(2,1)S(1)} %constant_dynamic-slice_fusion.refs_0_), channel_id=1, source_target_pairs={{0,224},{8,232},{16,240},{24,248},{32,0},{40,8},{48,16},{56,24},{6... | collective-permute-start | bytes 294920 | tf_op jit(solution)/shard_map/ppermute | solution.py:680
  7.5 11.7 %collective-permute-start.4 = (bf16[32,1536]{1,0:T(8,128)(2,1)S(1)}, bf16[32,1536]{1,0:T(8,128)(2,1)S(1)}, u32[]{:S(2)}, u32[]{:S(2)}) collective-permute-start(bf16[32,1536]{1,0:T(8,128)(2,1)S(1)} %constant_dynamic-slice_fusion.refs_0_), channel_id=1, source_target_pairs={{0,192},{8,200},{16,208},{24,216},{32,224},{40,232},{48,240},{56,2... | collective-permute-start | bytes 294920 | tf_op jit(solution)/shard_map/ppermute | solution.py:680
  9.0 8.7 %collective-permute-start.1 = (bf16[32,1536]{1,0:T(8,128)(2,1)S(1)}, bf16[32,1536]{1,0:T(8,128)(2,1)S(1)}, u32[]{:S(2)}, u32[]{:S(2)}) collective-permute-start(bf16[32,1536]{1,0:T(8,128)(2,1)S(1)} %constant_dynamic-slice_fusion.refs_0_), channel_id=1, source_target_pairs={{0,64},{8,72},{16,80},{24,88},{32,96},{40,104},{48,112},{56,120},{... | collective-permute-start | bytes 294920 | tf_op jit(solution)/shard_map/ppermute | solution.py:680
  10.4 12.1 %collective-permute-start = (bf16[32,1536]{1,0:T(8,128)(2,1)S(1)}, bf16[32,1536]{1,0:T(8,128)(2,1)S(1)}, u32[]{:S(2)}, u32[]{:S(2)}) collective-permute-start(bf16[32,1536]{1,0:T(8,128)(2,1)S(1)} %constant_dynamic-slice_fusion.refs_0_), channel_id=1, source_target_pairs={{0,32},{8,40},{16,48},{24,56},{32,64},{40,72},{48,80},{56,88},{64,... | collective-permute-start | bytes 294920 | tf_op jit(solution)/shard_map/ppermute | solution.py:680
  17.6 7.6 %collective-permute-start.3 = (bf16[32,1536]{1,0:T(8,128)(2,1)S(1)}, bf16[32,1536]{1,0:T(8,128)(2,1)S(1)}, u32[]{:S(2)}, u32[]{:S(2)}) collective-permute-start(bf16[32,1536]{1,0:T(8,128)(2,1)S(1)} %collective-permute-done.1.refs_2_), channel_id=1, source_target_pairs={{0,64},{8,72},{16,80},{24,88},{32,96},{40,104},{48,112},{56,120},{... | collective-permute-start | bytes 294920 | tf_op jit(solution)/shard_map/ppermute | solution.py:683
  17.8 8.8 %collective-permute-start.2 = (bf16[32,1536]{1,0:T(8,128)(2,1)S(1)}, bf16[32,1536]{1,0:T(8,128)(2,1)S(1)}, u32[]{:S(2)}, u32[]{:S(2)}) collective-permute-start(bf16[32,1536]{1,0:T(8,128)(2,1)S(1)} %collective-permute-done.1.refs_2_), channel_id=1, source_target_pairs={{0,32},{8,40},{16,48},{24,56},{32,64},{40,72},{48,80},{56,88},{64,... | collective-permute-start | bytes 294920 | tf_op jit(solution)/shard_map/ppermute | solution.py:682
  19.2 4.9 %collective-permute-start.5 = (bf16[32,1536]{1,0:T(8,128)(2,1)S(1)}, bf16[32,1536]{1,0:T(8,128)(2,1)S(1)}, u32[]{:S(2)}, u32[]{:S(2)}) collective-permute-start(bf16[32,1536]{1,0:T(8,128)(2,1)S(1)} %collective-permute-done.4.refs_6_), channel_id=1, source_target_pairs={{0,224},{8,232},{16,240},{24,248},{32,0},{40,8},{48,16},{56,24},{6... | collective-permute-start | bytes 294920 | tf_op jit(solution)/shard_map/ppermute | solution.py:684
  26.7 9.9 %copy-start.1 = (bf16[8,32,1536]{2,1,0:T(8,128)(2,1)}, bf16[8,32,1536]{2,1,0:T(8,128)(2,1)S(1)}, u32[]{:S(2)}) copy-start(bf16[8,32,1536]{2,1,0:T(8,128)(2,1)S(1)} %shard_map.85.refs_0_) | copy-start | bytes 2359300
  27.7 11.3 %collective-permute-start.8 = (bf16[4,32,1536]{2,1,0:T(8,128)(2,1)}, bf16[4,32,1536]{2,1,0:T(8,128)(2,1)}, u32[]{:S(2)}, u32[]{:S(2)}) collective-permute-start(bf16[4,32,1536]{2,1,0:T(8,128)(2,1)} %get-tuple-element.80), channel_id=1, source_target_pairs={{0,24},{8,0},{16,8},{24,16},{32,56},{40,32},{48,40},{56,48},{64,88... | collective-permute-start | bytes 1179656 | tf_op jit(solution)/shard_map/ppermute | solution.py:696
  28.2 12.3 %collective-permute-start.7 = (bf16[4,32,1536]{2,1,0:T(8,128)(2,1)}, bf16[4,32,1536]{2,1,0:T(8,128)(2,1)}, u32[]{:S(2)}, u32[]{:S(2)}) collective-permute-start(bf16[4,32,1536]{2,1,0:T(8,128)(2,1)} %get-tuple-element.81), channel_id=1, source_target_pairs={{0,8},{8,16},{16,24},{24,0},{32,40},{40,48},{48,56},{56,32},{64,72... | collective-permute-start | bytes 1179656 | tf_op jit(solution)/shard_map/ppermute | solution.py:695
  29.7 18.6 %collective-permute-start.9 = (bf16[4,32,1536]{2,1,0:T(8,128)(2,1)}, bf16[4,32,1536]{2,1,0:T(8,128)(2,1)}, u32[]{:S(2)}, u32[]{:S(2)}) collective-permute-start(bf16[4,32,1536]{2,1,0:T(8,128)(2,1)} %get-tuple-element.80), channel_id=1, source_target_pairs={{0,8},{8,16},{16,24},{24,0},{32,40},{40,48},{48,56},{56,32},{64,72... | collective-permute-start | bytes 1179656 | tf_op jit(solution)/shard_map/ppermute | solution.py:697
  32.0 18.4 %collective-permute-start.10 = (bf16[4,32,1536]{2,1,0:T(8,128)(2,1)}, bf16[4,32,1536]{2,1,0:T(8,128)(2,1)S(1)}, u32[]{:S(2)}, u32[]{:S(2)}) collective-permute-start(bf16[4,32,1536]{2,1,0:T(8,128)(2,1)} %get-tuple-element.81), channel_id=1, source_target_pairs={{0,24},{8,0},{16,8},{24,16},{32,56},{40,32},{48,40},{56,48},{64,88... | collective-permute-start | bytes 1179656 | tf_op jit(solution)/shard_map/ppermute | solution.py:698
  32.4 18.3 %collective-permute-start.13 = (bf16[8,32,1536]{2,1,0:T(8,128)(2,1)S(1)}, bf16[8,32,1536]{2,1,0:T(8,128)(2,1)S(1)}, u32[]{:S(2)}, u32[]{:S(2)}) collective-permute-start(bf16[8,32,1536]{2,1,0:T(8,128)(2,1)S(1)} %shard_map.85.refs_0_), channel_id=1, source_target_pairs={{0,1},{1,0},{2,3},{3,2},{4,5},{5,4},{6,7},{7,6},{8,9},{9,8},{10,11... | collective-permute-start | bytes 2359304 | tf_op jit(solution)/shard_map/ppermute | solution.py:709
  40.5 12.6 %collective-permute-start.11 = (bf16[4,32,1536]{2,1,0:T(8,128)(2,1)}, bf16[4,32,1536]{2,1,0:T(8,128)(2,1)}, u32[]{:S(2)}, u32[]{:S(2)}) collective-permute-start(bf16[4,32,1536]{2,1,0:T(8,128)(2,1)} %collective-permute-done.7), channel_id=1, source_target_pairs={{0,8},{8,16},{16,24},{24,0},{32,40},{40,48},{48,56},{56,32},{64,72... | collective-permute-start | bytes 1179656 | tf_op jit(solution)/shard_map/ppermute | solution.py:702
  40.8 12.3 %collective-permute-start.12 = (bf16[4,32,1536]{2,1,0:T(8,128)(2,1)}, bf16[4,32,1536]{2,1,0:T(8,128)(2,1)}, u32[]{:S(2)}, u32[]{:S(2)}) collective-permute-start(bf16[4,32,1536]{2,1,0:T(8,128)(2,1)} %collective-permute-done.8), channel_id=1, source_target_pairs={{0,24},{8,0},{16,8},{24,16},{32,56},{40,32},{48,40},{56,48},{64,88... | collective-permute-start | bytes 1179656 | tf_op jit(solution)/shard_map/ppermute | solution.py:703
  50.4 12.0 %copy-start.9 = (bf16[16,32,1536]{2,1,0:T(8,128)(2,1)}, bf16[16,32,1536]{2,1,0:T(8,128)(2,1)S(1)}, u32[]{:S(2)}) copy-start(bf16[16,32,1536]{2,1,0:T(8,128)(2,1)S(1)} %constant_dynamic-update-slice_fusion.refs_1_) | copy-start | bytes 4718596
  50.4 14.3 %collective-permute-start.14 = (bf16[16,32,1536]{2,1,0:T(8,128)(2,1)S(1)}, bf16[16,32,1536]{2,1,0:T(8,128)(2,1)}, u32[]{:S(2)}, u32[]{:S(2)}) collective-permute-start(bf16[16,32,1536]{2,1,0:T(8,128)(2,1)S(1)} %constant_dynamic-update-slice_fusion.refs_1_), channel_id=1, source_target_pairs={{0,1},{1,0},{2,3},{3,2},{4,5},{5,4},{6,7},{7,6},{8,9},{9,8},{10,11... | collective-permute-start | bytes 4718600 | tf_op jit(solution)/shard_map/ppermute | solution.py:709
  50.7 2.4 %copy-start.11 = (bf16[8,32,1536]{2,1,0:T(8,128)(2,1)}, bf16[8,32,1536]{2,1,0:T(8,128)(2,1)S(1)}, u32[]{:S(2)}) copy-start(bf16[8,32,1536]{2,1,0:T(8,128)(2,1)S(1)} %collective-permute-done.13.refs_3_) | copy-start | bytes 2359300
  53.1 33.8 %all-to-all-start = ((bf16[32,32,384]{2,1,0:T(8,128)(2,1)}), bf16[32,32,384]{2,1,0:T(8,128)(2,1)S(1)}, u32[]{:S(2)}, u32[]{:S(2)}) async-start(bf16[32,32,384]{2,1,0:T(8,128)(2,1)} %shard_map.87), calls=%async_computation | async-start | bytes 1572864 | tf_op jit(solution)/shard_map/all_to_all | solution.py:711
  62.4 3.3 %copy-start.10 = (bf16[8,32,1536]{2,1,0:T(8,128)(2,1)}, bf16[8,32,1536]{2,1,0:T(8,128)(2,1)S(1)}, u32[]{:S(2)}) copy-start(bf16[8,32,1536]{2,1,0:T(8,128)(2,1)S(1)} %constant_dynamic-update-slice_fusion.4.refs_2_) | copy-start | bytes 2359300
  62.4 2.4 %collective-permute-start.15 = (bf16[8,32,1536]{2,1,0:T(8,128)(2,1)S(1)}, bf16[8,32,1536]{2,1,0:T(8,128)(2,1)S(1)}, u32[]{:S(2)}, u32[]{:S(2)}) collective-permute-start(bf16[8,32,1536]{2,1,0:T(8,128)(2,1)S(1)} %constant_dynamic-update-slice_fusion.4.refs_2_), channel_id=1, source_target_pairs={{0,1},{1,0},{2,3},{3,2},{4,5},{5,4},{6,7},{7,6},{8,9},{9,8},{10,11... | collective-permute-start | bytes 2359304 | tf_op jit(solution)/shard_map/ppermute | solution.py:709
  64.8 0.9 copy-start.12
  74.2 1.5 collective-permute-start.16
  75.7 0.7 copy-start.5
  76.4 8.5 %copy-start.4 = (f32[8,128]{1,0:T(8,128)}, f32[8,128]{1,0:T(8,128)S(1)}, u32[]{:S(2)}) copy-start(f32[8,128]{1,0:T(8,128)S(1)} %shard_map.89.refs_0_) | copy-start | bytes 12292
  76.4 4.5 %collective-permute-start.19 = (f32[8,128]{1,0:T(8,128)S(1)}, f32[8,128]{1,0:T(8,128)S(1)}, u32[]{:S(2)}, u32[]{:S(2)}) collective-permute-start(f32[8,128]{1,0:T(8,128)S(1)} %shard_map.89.refs_0_), channel_id=1, source_target_pairs={{0,6},{1,7},{2,0},{3,1},{4,2},{5,3},{6,4},{7,5},{8,14},{9,15},{10,... | collective-permute-start | bytes 12296 | tf_op jit(solution)/shard_map/ppermute | solution.py:715
  79.2 5.1 %collective-permute-start.18 = (f32[8,128]{1,0:T(8,128)S(1)}, f32[8,128]{1,0:T(8,128)S(1)}, u32[]{:S(2)}, u32[]{:S(2)}) collective-permute-start(f32[8,128]{1,0:T(8,128)S(1)} %shard_map.89.refs_0_), channel_id=1, source_target_pairs={{0,4},{1,5},{2,6},{3,7},{4,0},{5,1},{6,2},{7,3},{8,12},{9,13},{10,... | collective-permute-start | bytes 12296 | tf_op jit(solution)/shard_map/ppermute | solution.py:715
  80.0 4.8 %collective-permute-start.17 = (f32[8,128]{1,0:T(8,128)S(1)}, f32[8,128]{1,0:T(8,128)S(1)}, u32[]{:S(2)}, u32[]{:S(2)}) collective-permute-start(f32[8,128]{1,0:T(8,128)S(1)} %shard_map.89.refs_0_), channel_id=1, source_target_pairs={{0,2},{1,3},{2,4},{3,5},{4,6},{5,7},{6,0},{7,1},{8,10},{9,11},{10,... | collective-permute-start | bytes 12296 | tf_op jit(solution)/shard_map/ppermute | solution.py:715
  80.9 3.9 %copy-start.14 = (f32[8,128]{1,0:T(8,128)}, f32[8,128]{1,0:T(8,128)S(1)}, u32[]{:S(2)}) copy-start(f32[8,128]{1,0:T(8,128)S(1)} %collective-permute-done.19.refs_3_) | copy-start | bytes 12292
  86.9 29.8 %collective-permute-start.22 = (bf16[384,1536]{1,0:T(8,128)(2,1)}, bf16[384,1536]{1,0:T(8,128)(2,1)S(1)}, u32[]{:S(2)}, u32[]{:S(2)}) collective-permute-start(bf16[384,1536]{1,0:T(8,128)(2,1)} %get-tuple-element.66), channel_id=1, source_target_pairs={{0,1},{1,0},{2,3},{3,2},{4,5},{5,4},{6,7},{7,6},{8,9},{9,8},{10,11... | collective-permute-start | bytes 3538952 | tf_op jit(solution)/shard_map/ppermute | solution.py:718
  86.9 9.8 %copy-start.8 = (bf16[32,32,384]{2,1,0:T(8,128)(2,1)}, bf16[32,32,384]{2,1,0:T(8,128)(2,1)S(1)}, u32[]{:S(2)}) copy-start(bf16[32,32,384]{2,1,0:T(8,128)(2,1)S(1)} %all-to-all-done) | copy-start | bytes 2359300
  86.9 19.2 %all-to-all-start.1 = ((f32[32,8,128]{2,1,0:T(8,128)}), f32[32,8,128]{2,1,0:T(8,128)S(1)}, u32[]{:S(2)}, u32[]{:S(2)}) async-start(f32[32,8,128]{2,1,0:T(8,128)} %shard_map.90), calls=%async_computation.1 | async-start | bytes 262144 | tf_op jit(solution)/shard_map/all_to_all | solution.py:720
  106.1 10.6 %copy-start.2 = (bf16[384,1536]{1,0:T(8,128)(2,1)S(1)}, bf16[384,1536]{1,0:T(8,128)(2,1)}, u32[]{:S(2)}) copy-start(bf16[384,1536]{1,0:T(8,128)(2,1)} %get-tuple-element.65.w_own) | copy-start | bytes 3538948
  106.2 0.7 copy-start.13
  114.2 2.6 %collective-permute-start.21 = (bf16[1024,384]{1,0:T(8,128)(2,1)}, bf16[1024,384]{1,0:T(8,128)(2,1)S(1)}, u32[]{:S(2)}, u32[]{:S(2)}) collective-permute-start(bf16[1024,384]{1,0:T(8,128)(2,1)} %get-tuple-element.64.own_ref), channel_id=1, source_target_pairs={{0,1},{1,0},{2,3},{3,2},{4,5},{5,4},{6,7},{7,6},{8,9},{9,8},{10,11... | collective-permute-start | bytes 2359304 | tf_op jit(solution)/shard_map/ppermute | solution.py:726
  114.3 2.4 %collective-permute-start.20 = (f32[1,1]{1,0:T(1,128)}, f32[1,1]{1,0:T(1,128)}, u32[]{:S(2)}, u32[]{:S(2)}) collective-permute-start(f32[1,1]{1,0:T(1,128)} %get-tuple-element.63.loss_ref), channel_id=1, source_target_pairs={{0,1},{1,0},{2,3},{3,2},{4,5},{5,4},{6,7},{7,6},{8,9},{9,8},{10,11... | collective-permute-start | bytes 20 | tf_op jit(solution)/shard_map/ppermute | solution.py:725
  116.8 1.1 copy-start.3
  120.6 13.5 %collective-permute-start.23 = (s16[528,384]{1,0:T(8,128)(2,1)S(1)}, s16[528,384]{1,0:T(8,128)(2,1)S(1)}, u32[]{:S(2)}, u32[]{:S(2)}) collective-permute-start(s16[528,384]{1,0:T(8,128)(2,1)S(1)} %get-tuple-element.70), channel_id=1, source_target_pairs={{0,2},{1,3},{2,4},{3,5},{4,6},{5,7},{6,0},{7,1},{8,10},{9,11},{10,... | collective-permute-start | bytes 1216520 | tf_op jit(solution)/shard_map/ppermute | solution.py:728
  120.7 13.9 %collective-permute-start.27 = (s16[528,384]{1,0:T(8,128)(2,1)S(1)}, s16[528,384]{1,0:T(8,128)(2,1)S(1)}, u32[]{:S(2)}, u32[]{:S(2)}) collective-permute-start(s16[528,384]{1,0:T(8,128)(2,1)S(1)} %get-tuple-element.74), channel_id=1, source_target_pairs={{0,6},{1,7},{2,0},{3,1},{4,2},{5,3},{6,4},{7,5},{8,14},{9,15},{10,... | collective-permute-start | bytes 1216520 | tf_op jit(solution)/shard_map/ppermute | solution.py:729
  126.5 15.9 %collective-permute-start.25 = (s16[528,384]{1,0:T(8,128)(2,1)S(1)}, s16[528,384]{1,0:T(8,128)(2,1)S(1)}, u32[]{:S(2)}, u32[]{:S(2)}) collective-permute-start(s16[528,384]{1,0:T(8,128)(2,1)S(1)} %get-tuple-element.71), channel_id=1, source_target_pairs={{0,6},{1,7},{2,0},{3,1},{4,2},{5,3},{6,4},{7,5},{8,14},{9,15},{10,... | collective-permute-start | bytes 1216520 | tf_op jit(solution)/shard_map/ppermute | solution.py:732
  126.6 16.2 %collective-permute-start.26 = (s16[528,384]{1,0:T(8,128)(2,1)S(1)}, s16[528,384]{1,0:T(8,128)(2,1)S(1)}, u32[]{:S(2)}, u32[]{:S(2)}) collective-permute-start(s16[528,384]{1,0:T(8,128)(2,1)S(1)} %get-tuple-element.72), channel_id=1, source_target_pairs={{0,2},{1,3},{2,4},{3,5},{4,6},{5,7},{6,0},{7,1},{8,10},{9,11},{10,... | collective-permute-start | bytes 1216520 | tf_op jit(solution)/shard_map/ppermute | solution.py:731
  134.5 16.2 %collective-permute-start.24 = (s16[528,384]{1,0:T(8,128)(2,1)S(1)}, s16[528,384]{1,0:T(8,128)(2,1)S(1)}, u32[]{:S(2)}, u32[]{:S(2)}) collective-permute-start(s16[528,384]{1,0:T(8,128)(2,1)S(1)} %shard_map.96), channel_id=1, source_target_pairs={{0,2},{1,3},{2,4},{3,5},{4,6},{5,7},{6,0},{7,1},{8,10},{9,11},{10,... | collective-permute-start | bytes 1216520 | tf_op jit(solution)/shard_map/ppermute | solution.py:733
  135.0 15.7 %collective-permute-start.28 = (s16[528,384]{1,0:T(8,128)(2,1)S(1)}, s16[528,384]{1,0:T(8,128)(2,1)S(1)}, u32[]{:S(2)}, u32[]{:S(2)}) collective-permute-start(s16[528,384]{1,0:T(8,128)(2,1)S(1)} %shard_map.97), channel_id=1, source_target_pairs={{0,6},{1,7},{2,0},{3,1},{4,2},{5,3},{6,4},{7,5},{8,14},{9,15},{10,... | collective-permute-start | bytes 1216520 | tf_op jit(solution)/shard_map/ppermute | solution.py:734
  153.2 9.9 %copy-start.17 = (s32[32]{0:T(128)S(1)}, s32[32]{0:T(128)}, u32[]{:S(2)}) copy-start(s32[32]{0:T(128)} %param.9) | copy-start | bytes 388
  153.2 11.2 %copy-start.7 = (bf16[1024,768]{1,0:T(8,128)(2,1)S(1)}, bf16[1024,768]{1,0:T(8,128)(2,1)}, u32[]{:S(2)}) copy-start(bf16[1024,768]{1,0:T(8,128)(2,1)} %get-tuple-element.62.sums_ref) | copy-start | bytes 4718596
  153.2 34.6 %all-to-all-start.2 = ((s16[32,112,128]{2,1,0:T(8,128)(2,1)}), s16[32,112,128]{2,1,0:T(8,128)(2,1)S(1)}, u32[]{:S(2)}, u32[]{:S(2)}) async-start(s16[32,112,128]{2,1,0:T(8,128)(2,1)} %shard_map.98), calls=%async_computation.2 | async-start | bytes 1835008 | tf_op jit(solution)/shard_map/all_to_all | solution.py:737
  164.4 2.8 %copy-start.6 = (bf16[2,8,4,32,1536]{4,3,2,1,0:T(8,128)(2,1)S(1)}, bf16[2,8,4,32,1536]{4,3,2,1,0:T(8,128)(2,1)}, u32[]{:S(2)}) copy-start(bf16[2,8,4,32,1536]{4,3,2,1,0:T(8,128)(2,1)} %get-tuple-element.48) | copy-start | bytes 18874372
  (2 other events, 1.2 us)

commit v5 on v4

--- a/solution.py
+++ b/solution.py
@@ -546,9 +546,27 @@
 PACKED = 3 * SLOTS + TAIL
 
 
+def collect_kernel(own_ref, low_l, high_r, o_ref, *tails):
+    for i, (ref, tail_ref) in enumerate(zip((low_l, high_r), tails)):
+        read_tail(ref, tail_ref)
+        for j in range(ROWS2 // 128):
+            rows = pl.ds(i * ROWS2 + j * 128, 128)
+            o_ref[rows, :] = own_ref[rows, :] + read_message(ref, tail_ref, j)
+
+
+def collect(own, low_l, high_r):
+    return pl.pallas_call(
+        collect_kernel,
+        out_shape=jax.ShapeDtypeStruct((ROWS, LOCAL), F32),
+        in_specs=[VMEM] * 3,
+        out_specs=VMEM,
+        scratch_shapes=[TAIL_REF] * 2,
+        compiler_params=PARAMS,
+    )(own, low_l, high_r)
+
+
 def pack_kernel(loss_ref, own_ref, low_r, low_l, high_r, high_l, o_ref, *tails):
-    messages = (low_r, low_l, high_r, high_l)
-    for ref, tail_ref in zip(messages, tails):
+    for ref, tail_ref in zip((low_r, low_l, high_r, high_l), tails):
         read_tail(ref, tail_ref)
     codes = [loss_ref[...]] + [tail_loss(tail_ref) for tail_ref in tails[:3]]
     loss = decode_loss(jnp.concatenate(codes, axis=0))
@@ -559,8 +577,7 @@
         for j in range(ROWS2 // 128):
             at = i * (ROWS2 // 128) + j
             val = own_ref[pl.ds(at * 128, 128), :]
-            got = [read_message(messages[n], tails[n], j) for n in (2 * i, 2 * i + 1)]
-            code, e = encode(val + (got[0] + got[1]))
+            code, e = encode(val + read_message((low_r, high_l)[i], tails[3 * i], j))
             tail = to16(jnp.concatenate([e, loss, pad], axis=0))
             for n in range(128 // SLOTS):
                 for k in range(3):
@@ -733,7 +750,7 @@
     low_r = lax.ppermute(relay(l1, low_r), "vocab", RIGHT)
     high_l = lax.ppermute(relay(h3, high_l), "vocab", LEFT)
     head = head_gradient(c1, table, sums)
-    packed = pack(loss, t0, low_r, low_l, high_r, high_l)
+    packed = pack(loss, collect(t0, low_l, high_r), low_r, low_l, high_r, high_l)
     packed = lax.all_to_all(packed, "trainer", split_axis=0, concat_axis=0, tiled=True)
     table_grad, loss = finish(lax.rem(trainer, 4).reshape(1).astype(jnp.int32), packed)
     mean_loss = loss[0, 0] / jnp.sum(counts).astype(F32)

time: 192 us -> 191 us (level)
  no operation moved by 1% of the time
where the time goes in v5:
time: 191 us; the launch traced here: 190 us
  starting transfers between devices  61.4 us (32%)
  waiting for transfers between devices  55.2 us (29%)
  Pallas kernels  51.6 us (27%)
  local copies, waits for them, and re-layouts  14.8 us (8%)
  other arithmetic  3.81 us (2%)
  between operations  3.43 us (2%)
    unnamed x40, local copies, waits for them, and re-layouts  11.9 us
    all_to_all x1, waiting for transfers between devices, on_device(): lax.all_to_all(packed, 'trainer', split_axis=0, concat_axis=0, tiled=True)  11.5 us
    all_to_all x1, starting transfers between devices, on_device(): lax.all_to_all(packed, 'trainer', split_axis=0, concat_axis=0, tiled=True)  9.91 us
    all_to_all x1, starting transfers between devices, on_device(): lax.all_to_all(stats, 'trainer', split_axis=0, concat_axis=0, tiled=True)  9.79 us
    pallas_call x1, Pallas kernels, select_rows(): pl.pallas_call(select_kernel, out_shape=(jax.ShapeDtypeStruct((ROWS, LOCA...  9.4 us
    pallas_call x1, Pallas kernels, head_gradient(): pl.pallas_call(head_kernel, grid_spec=pltpu.PrefetchScalarGridSpec(num_sc...  9.12 us
    ppermute x4, starting transfers between devices, on_device(): lax.ppermute(half, 'trainer', along_z(k))  8.86 us
    pallas_call x1, Pallas kernels, logits_and_stats(): pl.pallas_call(logit_kernel, out_shape=(jax.ShapeDtypeStruct((2, Z, Y, SL...  8.53 us
  transfers between devices with their start and end apart: 32, of which 19 were waited for; matrix products, arithmetic and copies ran while one was open for 5% of the time, Pallas kernels for 24%

profile of v5, /device:TPU:8, one launch (start us, length us, event | category | flops | bytes accessed | tf_op | source)
XLA Modules:
  0.0 190.3 jit_solution(15076079985544056542)
XLA Ops:
  1.6 5.9 %collective-permute-start.6 = (bf16[32,1536]{1,0:T(8,128)(2,1)S(1)}, bf16[32,1536]{1,0:T(8,128)(2,1)S(1)}, u32[]{:S(2)}, u32[]{:S(2)}) collective-permute-start(bf16[32,1536]{1,0:T(8,128)(2,1)S(1)} %constant_dynamic-slice_fusion.refs_0_), channel_id=1, source_target_pairs={{0,224},{8,232},{16,240},{24,248},{32,0},{40,8},{48,16},{56,24},{6... | collective-permute-start | bytes 294920 | tf_op jit(solution)/shard_map/ppermute | solution.py:697
  7.5 1.5 collective-permute-start.4
  9.0 1.5 collective-permute-start.1
  10.4 1.3 add_convert_fusion
  12.5 5.1 %collective-permute-done.1.refs_2_ = bf16[32,1536]{1,0:T(8,128)(2,1)S(1)} collective-permute-done((bf16[32,1536]{1,0:T(8,128)(2,1)S(1)}, bf16[32,1536]{1,0:T(8,128)(2,1)S(1)}, u32[]{:S(2)}, u32[]{:S(2)}) %collective-permute-start.1) | collective-permute-done | bytes 98336 | tf_op jit(solution)/shard_map/ppermute | solution.py:697
  17.8 1.4 collective-permute-start.2
  19.2 2.7 %collective-permute-start.5 = (bf16[32,1536]{1,0:T(8,128)(2,1)S(1)}, bf16[32,1536]{1,0:T(8,128)(2,1)S(1)}, u32[]{:S(2)}, u32[]{:S(2)}) collective-permute-start(bf16[32,1536]{1,0:T(8,128)(2,1)S(1)} %collective-permute-done.4.refs_6_), channel_id=1, source_target_pairs={{0,224},{8,232},{16,240},{24,248},{32,0},{40,8},{48,16},{56,24},{6... | collective-permute-start | bytes 294920 | tf_op jit(solution)/shard_map/ppermute | solution.py:701
  22.5 1.6 collective-permute-done.5.refs_5_
  24.1 1.2 collective-permute-done.3.refs_4_
  25.3 1.3 collective-permute-done.2.refs_3_
  26.7 1.0 fusion
  28.2 1.6 collective-permute-start.7
  29.7 1.6 collective-permute-start.9
  32.4 4.1 %shard_map.86 = (bf16[384,1536]{1,0:T(8,128)(2,1)}, bf16[384,1536]{1,0:T(8,128)(2,1)}) custom-call(s32[2]{0:T(128)} %pad_add_fusion.1.at_ref, bf16[4,2,384,384]{3,2,1,0:T(8,128)(2,1)} %bitcast.13), custom_call_target="tpu_custom_call" | custom-call | tf_op jit(solution)/shard_map/pallas_call | solution.py:431
  36.6 2.5 %collective-permute-done.8 = bf16[4,32,1536]{2,1,0:T(8,128)(2,1)} collective-permute-done((bf16[4,32,1536]{2,1,0:T(8,128)(2,1)}, bf16[4,32,1536]{2,1,0:T(8,128)(2,1)}, u32[]{:S(2)}, u32[]{:S(2)}) %collective-permute-start.8) | collective-permute-done | bytes 393248 | tf_op jit(solution)/shard_map/ppermute | solution.py:713
  39.0 1.4 collective-permute-done.7
  40.8 2.7 %collective-permute-start.12 = (bf16[4,32,1536]{2,1,0:T(8,128)(2,1)}, bf16[4,32,1536]{2,1,0:T(8,128)(2,1)}, u32[]{:S(2)}, u32[]{:S(2)}) collective-permute-start(bf16[4,32,1536]{2,1,0:T(8,128)(2,1)} %collective-permute-done.8), channel_id=1, source_target_pairs={{0,24},{8,0},{16,8},{24,16},{32,56},{40,32},{48,40},{56,48},{64,88... | collective-permute-start | bytes 1179656 | tf_op jit(solution)/shard_map/ppermute | solution.py:720
  43.4 2.1 %shard_map.87 = bf16[32,32,384]{2,1,0:T(8,128)(2,1)} custom-call(bf16[32,12288]{1,0:T(8,128)(2,1)} %bitcast.17), custom_call_target="tpu_custom_call" | custom-call | tf_op jit(solution)/shard_map/pallas_call | solution.py:39
  46.6 1.7 collective-permute-done.9
  49.3 1.0 constant_dynamic-update-slice_fusion.1
  50.7 2.4 %collective-permute-done.11 = bf16[4,32,1536]{2,1,0:T(8,128)(2,1)} collective-permute-done((bf16[4,32,1536]{2,1,0:T(8,128)(2,1)}, bf16[4,32,1536]{2,1,0:T(8,128)(2,1)}, u32[]{:S(2)}, u32[]{:S(2)}) %collective-permute-start.11) | collective-permute-done | bytes 393248 | tf_op jit(solution)/shard_map/ppermute | solution.py:719
  53.1 7.2 %all-to-all-start = ((bf16[32,32,384]{2,1,0:T(8,128)(2,1)}), bf16[32,32,384]{2,1,0:T(8,128)(2,1)S(1)}, u32[]{:S(2)}, u32[]{:S(2)}) async-start(bf16[32,32,384]{2,1,0:T(8,128)(2,1)} %shard_map.87), calls=%async_computation | async-start | bytes 1572864 | tf_op jit(solution)/shard_map/all_to_all | solution.py:728
  61.3 1.0 constant_dynamic-update-slice_fusion.4.refs_2_
  63.1 1.6 collective-permute-done.15.refs_5_
  65.7 8.5 %shard_map.88 = (bf16[2,8,4,32,1536]{4,3,2,1,0:T(8,128)(2,1)}, f32[1024,384]{1,0:T(8,128)}, f32[8,128]{1,0:T(8,128)}, f32[8,128]{1,0:T(8,128)}) custom-call(s32[2]{0:T(128)} %pad_add_fusion.at_ref, bf16[8,32,1536]{2,1,0:T(8,128)(2,1)} %copy-done.1, bf16[16,32,1536]{2,1,0:T(8,128)(2,1)} %copy-done.9, bf16[8,32,1536]{2,1,0:T(8,128)(2,1)} %copy-done.10, ...), custom_call_target="tpu_custom_call" | custom-call | tf_op jit(solution)/shard_map/pallas_call | solution.py:131
  74.5 1.2 collective-permute-done.16.refs_1_
  76.4 2.8 %collective-permute-start.19 = (f32[8,128]{1,0:T(8,128)S(1)}, f32[8,128]{1,0:T(8,128)S(1)}, u32[]{:S(2)}, u32[]{:S(2)}) collective-permute-start(f32[8,128]{1,0:T(8,128)S(1)} %shard_map.89.refs_0_), channel_id=1, source_target_pairs={{0,6},{1,7},{2,0},{3,1},{4,2},{5,3},{6,4},{7,5},{8,14},{9,15},{10,... | collective-permute-start | bytes 12296 | tf_op jit(solution)/shard_map/ppermute | solution.py:732
  80.9 3.4 %collective-permute-done.18.refs_2_ = f32[8,128]{1,0:T(8,128)S(1)} collective-permute-done((f32[8,128]{1,0:T(8,128)S(1)}, f32[8,128]{1,0:T(8,128)S(1)}, u32[]{:S(2)}, u32[]{:S(2)}) %collective-permute-start.18) | collective-permute-done | bytes 4128 | tf_op jit(solution)/shard_map/ppermute | solution.py:732
  85.5 1.4 shard_map.90
  86.9 9.8 %all-to-all-start.1 = ((f32[32,8,128]{2,1,0:T(8,128)}), f32[32,8,128]{2,1,0:T(8,128)S(1)}, u32[]{:S(2)}, u32[]{:S(2)}) async-start(f32[32,8,128]{2,1,0:T(8,128)} %shard_map.90), calls=%async_computation.1 | async-start | bytes 262144 | tf_op jit(solution)/shard_map/all_to_all | solution.py:737
  96.7 9.4 %shard_map.91 = (f32[1024,384]{1,0:T(8,128)}, f32[8,128]{1,0:T(8,128)}, f32[1,1]{1,0:T(1,128)}) custom-call(f32[8,128]{1,0:T(8,128)} %get-tuple-element.54.top_ref, f32[1024,384]{1,0:T(8,128)} %get-tuple-element.55.far_ref, bf16[1024,384]{1,0:T(8,128)(2,1)} %bitcast.15, f32[1,1024]{1,0:T(1,128)} %bitcast.18, f32[1,1024]{1,0:T(1,128)} %compare_convert_fusion.live_ref), custom_call_target="tpu_custom_call" | custom-call | flops 3221225472 | bytes 8388608 | tf_op jit(solution)/shard_map/pallas_call | solution.py:244
  106.8 7.4 %shard_map.92 = (bf16[1024,384]{1,0:T(8,128)(2,1)}, bf16[1024,768]{1,0:T(8,128)(2,1)}, f32[1,1]{1,0:T(1,128)}) custom-call(f32[32,8,128]{2,1,0:T(8,128)} %copy-done.13, f32[8,128]{1,0:T(8,128)} %get-tuple-element.54.top_ref, f32[8,128]{1,0:T(8,128)} %get-tuple-element.59.mass_ref, f32[1,1]{1,0:T(1,128)} %get-tuple-element.60.cross_ref, ...), custom_call_target="tpu_custom_call" | custom-call | tf_op jit(solution)/shard_map/pallas_call | solution.py:320
  114.8 1.9 %collective-permute-done.20.more_ref = f32[1,1]{1,0:T(1,128)} collective-permute-done((f32[1,1]{1,0:T(1,128)}, f32[1,1]{1,0:T(1,128)}, u32[]{:S(2)}, u32[]{:S(2)}) %collective-permute-start.20) | collective-permute-done | bytes 36 | tf_op jit(solution)/shard_map/ppermute | solution.py:742
  116.8 1.1 copy-done.3
  117.9 2.7 %shard_map.94 = (s16[528,384]{1,0:T(8,128)(2,1)S(1)}, s16[528,384]{1,0:T(8,128)(2,1)S(1)}, f32[1,128]{1,0:T(1,128)S(1)}) custom-call(f32[1,1]{1,0:T(1,128)} %get-tuple-element.63.loss_ref, f32[1,1]{1,0:T(1,128)} %collective-permute-done.20.more_ref, bf16[1024,384]{1,0:T(8,128)(2,1)S(1)} %copy-done.3, ...), custom_call_target="tpu_custom_call" | custom-call | tf_op jit(solution)/shard_map/pallas_call | solution.py:503
  120.7 3.2 %collective-permute-start.27 = (s16[528,384]{1,0:T(8,128)(2,1)S(1)}, s16[528,384]{1,0:T(8,128)(2,1)S(1)}, u32[]{:S(2)}, u32[]{:S(2)}) collective-permute-start(s16[528,384]{1,0:T(8,128)(2,1)S(1)} %get-tuple-element.74), channel_id=1, source_target_pairs={{0,6},{1,7},{2,0},{3,1},{4,2},{5,3},{6,4},{7,5},{8,14},{9,15},{10,... | collective-permute-start | bytes 1216520 | tf_op jit(solution)/shard_map/ppermute | solution.py:746
  123.9 2.6 %shard_map.95 = (f32[512,384]{1,0:T(8,128)S(1)}, s16[528,384]{1,0:T(8,128)(2,1)S(1)}, s16[528,384]{1,0:T(8,128)(2,1)S(1)}, f32[512,384]{1,0:T(8,128)S(1)}, f32[1024,384]{1,0:T(8,128)S(1)}) custom-call(f32[1,128]{1,0:T(1,128)S(1)} %get-tuple-element.67.loss_ref, bf16[1024,384]{1,0:T(8,128)(2,1)S(1)} %copy-done.3, ...), custom_call_target="tpu_custom_call" | custom-call | tf_op jit(solution)/shard_map/pallas_call | solution.py:515
  126.6 2.0 %collective-permute-start.24 = (s16[528,384]{1,0:T(8,128)(2,1)S(1)}, s16[528,384]{1,0:T(8,128)(2,1)S(1)}, u32[]{:S(2)}, u32[]{:S(2)}) collective-permute-start(s16[528,384]{1,0:T(8,128)(2,1)S(1)} %get-tuple-element.70), channel_id=1, source_target_pairs={{0,2},{1,3},{2,4},{3,5},{4,6},{5,7},{6,0},{7,1},{8,10},{9,11},{10,... | collective-permute-start | bytes 1216520 | tf_op jit(solution)/shard_map/ppermute | solution.py:748
  128.6 5.5 %collective-permute-done.25.got_ref = s16[528,384]{1,0:T(8,128)(2,1)S(1)} collective-permute-done((s16[528,384]{1,0:T(8,128)(2,1)S(1)}, s16[528,384]{1,0:T(8,128)(2,1)S(1)}, u32[]{:S(2)}, u32[]{:S(2)}) %collective-permute-start.25) | collective-permute-done | bytes 405536 | tf_op jit(solution)/shard_map/ppermute | solution.py:745
  135.0 3.3 %collective-permute-start.28 = (s16[528,384]{1,0:T(8,128)(2,1)S(1)}, s16[528,384]{1,0:T(8,128)(2,1)S(1)}, u32[]{:S(2)}, u32[]{:S(2)}) collective-permute-start(s16[528,384]{1,0:T(8,128)(2,1)S(1)} %shard_map.98), channel_id=1, source_target_pairs={{0,6},{1,7},{2,0},{3,1},{4,2},{5,3},{6,4},{7,5},{8,14},{9,15},{10,... | collective-permute-start | bytes 1216520 | tf_op jit(solution)/shard_map/ppermute | solution.py:751
  138.3 4.1 %collective-permute-done.23.low_l = s16[528,384]{1,0:T(8,128)(2,1)S(1)} collective-permute-done((s16[528,384]{1,0:T(8,128)(2,1)S(1)}, s16[528,384]{1,0:T(8,128)(2,1)S(1)}, u32[]{:S(2)}, u32[]{:S(2)}) %collective-permute-start.23) | collective-permute-done | bytes 405536 | tf_op jit(solution)/shard_map/ppermute | solution.py:749
  143.1 7.6 %collective-permute-done.26.low_r = s16[528,384]{1,0:T(8,128)(2,1)S(1)} collective-permute-done((s16[528,384]{1,0:T(8,128)(2,1)S(1)}, s16[528,384]{1,0:T(8,128)(2,1)S(1)}, u32[]{:S(2)}, u32[]{:S(2)}) %collective-permute-start.26) | collective-permute-done | bytes 405536 | tf_op jit(solution)/shard_map/ppermute | solution.py:750
  150.7 1.9 %shard_map.99 = s16[32,112,128]{2,1,0:T(8,128)(2,1)} custom-call(f32[1,128]{1,0:T(1,128)S(1)} %get-tuple-element.67.loss_ref, f32[1024,384]{1,0:T(8,128)S(1)} %shard_map.96.own_ref, s16[528,384]{1,0:T(8,128)(2,1)S(1)} %collective-permute-done.26.low_r, s16[528,384]{1,0:T(8,128)(2,1)S(1)} %collective-permute-done.23.low_l, ...), custom_call_target="tpu_custom_call" | custom-call | tf_op jit(solution)/shard_map/pallas_call | solution.py:591
  152.6 9.9 %all-to-all-start.2 = ((s16[32,112,128]{2,1,0:T(8,128)(2,1)}), s16[32,112,128]{2,1,0:T(8,128)(2,1)S(1)}, u32[]{:S(2)}, u32[]{:S(2)}) async-start(s16[32,112,128]{2,1,0:T(8,128)(2,1)} %shard_map.99), calls=%async_computation.2 | async-start | bytes 1835008 | tf_op jit(solution)/shard_map/all_to_all | solution.py:754
  163.8 2.8 %copy-done.6 = bf16[2,8,4,32,1536]{4,3,2,1,0:T(8,128)(2,1)S(1)} copy-done((bf16[2,8,4,32,1536]{4,3,2,1,0:T(8,128)(2,1)S(1)}, bf16[2,8,4,32,1536]{4,3,2,1,0:T(8,128)(2,1)}, u32[]{:S(2)}) %copy-start.6) | copy-done | bytes 6291480
  166.6 9.1 %shard_map.93 = f32[9216,128]{1,0:T(8,128)} custom-call(s32[1]{0:T(128)} %bitcast.c_ref, bf16[2,1024,1536]{2,1,0:T(8,128)(2,1)S(1)} %bitcast.12, bf16[1024,768]{1,0:T(8,128)(2,1)S(1)} %copy-done.7), custom_call_target="tpu_custom_call" | custom-call | flops 4831838208 | bytes 12582912 | tf_op jit(solution)/shard_map/pallas_call | solution.py:645
  175.7 11.5 %all-to-all-done.2.x_ref = s16[32,112,128]{2,1,0:T(8,128)(2,1)S(1)} async-done(((s16[32,112,128]{2,1,0:T(8,128)(2,1)}), s16[32,112,128]{2,1,0:T(8,128)(2,1)S(1)}, u32[]{:S(2)}, u32[]{:S(2)}) %all-to-all-start.2) | async-done | bytes 917536 | tf_op jit(solution)/shard_map/all_to_all | solution.py:754
  187.3 1.2 shard_map.100
  (83 shorter events, 17.0 us)
Async XLA Ops:
  0.6 0.9 copy-start
  1.6 20.9 %collective-permute-start.6 = (bf16[32,1536]{1,0:T(8,128)(2,1)S(1)}, bf16[32,1536]{1,0:T(8,128)(2,1)S(1)}, u32[]{:S(2)}, u32[]{:S(2)}) collective-permute-start(bf16[32,1536]{1,0:T(8,128)(2,1)S(1)} %constant_dynamic-slice_fusion.refs_0_), channel_id=1, source_target_pairs={{0,224},{8,232},{16,240},{24,248},{32,0},{40,8},{48,16},{56,24},{6... | collective-permute-start | bytes 294920 | tf_op jit(solution)/shard_map/ppermute | solution.py:697
  7.5 11.7 %collective-permute-start.4 = (bf16[32,1536]{1,0:T(8,128)(2,1)S(1)}, bf16[32,1536]{1,0:T(8,128)(2,1)S(1)}, u32[]{:S(2)}, u32[]{:S(2)}) collective-permute-start(bf16[32,1536]{1,0:T(8,128)(2,1)S(1)} %constant_dynamic-slice_fusion.refs_0_), channel_id=1, source_target_pairs={{0,192},{8,200},{16,208},{24,216},{32,224},{40,232},{48,240},{56,2... | collective-permute-start | bytes 294920 | tf_op jit(solution)/shard_map/ppermute | solution.py:697
  9.0 8.7 %collective-permute-start.1 = (bf16[32,1536]{1,0:T(8,128)(2,1)S(1)}, bf16[32,1536]{1,0:T(8,128)(2,1)S(1)}, u32[]{:S(2)}, u32[]{:S(2)}) collective-permute-start(bf16[32,1536]{1,0:T(8,128)(2,1)S(1)} %constant_dynamic-slice_fusion.refs_0_), channel_id=1, source_target_pairs={{0,64},{8,72},{16,80},{24,88},{32,96},{40,104},{48,112},{56,120},{... | collective-permute-start | bytes 294920 | tf_op jit(solution)/shard_map/ppermute | solution.py:697
  10.4 12.1 %collective-permute-start = (bf16[32,1536]{1,0:T(8,128)(2,1)S(1)}, bf16[32,1536]{1,0:T(8,128)(2,1)S(1)}, u32[]{:S(2)}, u32[]{:S(2)}) collective-permute-start(bf16[32,1536]{1,0:T(8,128)(2,1)S(1)} %constant_dynamic-slice_fusion.refs_0_), channel_id=1, source_target_pairs={{0,32},{8,40},{16,48},{24,56},{32,64},{40,72},{48,80},{56,88},{64,... | collective-permute-start | bytes 294920 | tf_op jit(solution)/shard_map/ppermute | solution.py:697
  17.6 7.6 %collective-permute-start.3 = (bf16[32,1536]{1,0:T(8,128)(2,1)S(1)}, bf16[32,1536]{1,0:T(8,128)(2,1)S(1)}, u32[]{:S(2)}, u32[]{:S(2)}) collective-permute-start(bf16[32,1536]{1,0:T(8,128)(2,1)S(1)} %collective-permute-done.1.refs_2_), channel_id=1, source_target_pairs={{0,64},{8,72},{16,80},{24,88},{32,96},{40,104},{48,112},{56,120},{... | collective-permute-start | bytes 294920 | tf_op jit(solution)/shard_map/ppermute | solution.py:700
  17.8 8.8 %collective-permute-start.2 = (bf16[32,1536]{1,0:T(8,128)(2,1)S(1)}, bf16[32,1536]{1,0:T(8,128)(2,1)S(1)}, u32[]{:S(2)}, u32[]{:S(2)}) collective-permute-start(bf16[32,1536]{1,0:T(8,128)(2,1)S(1)} %collective-permute-done.1.refs_2_), channel_id=1, source_target_pairs={{0,32},{8,40},{16,48},{24,56},{32,64},{40,72},{48,80},{56,88},{64,... | collective-permute-start | bytes 294920 | tf_op jit(solution)/shard_map/ppermute | solution.py:699
  19.2 4.9 %collective-permute-start.5 = (bf16[32,1536]{1,0:T(8,128)(2,1)S(1)}, bf16[32,1536]{1,0:T(8,128)(2,1)S(1)}, u32[]{:S(2)}, u32[]{:S(2)}) collective-permute-start(bf16[32,1536]{1,0:T(8,128)(2,1)S(1)} %collective-permute-done.4.refs_6_), channel_id=1, source_target_pairs={{0,224},{8,232},{16,240},{24,248},{32,0},{40,8},{48,16},{56,24},{6... | collective-permute-start | bytes 294920 | tf_op jit(solution)/shard_map/ppermute | solution.py:701
  26.7 9.9 %copy-start.1 = (bf16[8,32,1536]{2,1,0:T(8,128)(2,1)}, bf16[8,32,1536]{2,1,0:T(8,128)(2,1)S(1)}, u32[]{:S(2)}) copy-start(bf16[8,32,1536]{2,1,0:T(8,128)(2,1)S(1)} %shard_map.85.refs_0_) | copy-start | bytes 2359300
  27.7 11.3 %collective-permute-start.8 = (bf16[4,32,1536]{2,1,0:T(8,128)(2,1)}, bf16[4,32,1536]{2,1,0:T(8,128)(2,1)}, u32[]{:S(2)}, u32[]{:S(2)}) collective-permute-start(bf16[4,32,1536]{2,1,0:T(8,128)(2,1)} %get-tuple-element.80), channel_id=1, source_target_pairs={{0,24},{8,0},{16,8},{24,16},{32,56},{40,32},{48,40},{56,48},{64,88... | collective-permute-start | bytes 1179656 | tf_op jit(solution)/shard_map/ppermute | solution.py:713
  28.2 12.3 %collective-permute-start.7 = (bf16[4,32,1536]{2,1,0:T(8,128)(2,1)}, bf16[4,32,1536]{2,1,0:T(8,128)(2,1)}, u32[]{:S(2)}, u32[]{:S(2)}) collective-permute-start(bf16[4,32,1536]{2,1,0:T(8,128)(2,1)} %get-tuple-element.81), channel_id=1, source_target_pairs={{0,8},{8,16},{16,24},{24,0},{32,40},{40,48},{48,56},{56,32},{64,72... | collective-permute-start | bytes 1179656 | tf_op jit(solution)/shard_map/ppermute | solution.py:712
  29.7 18.6 %collective-permute-start.9 = (bf16[4,32,1536]{2,1,0:T(8,128)(2,1)}, bf16[4,32,1536]{2,1,0:T(8,128)(2,1)}, u32[]{:S(2)}, u32[]{:S(2)}) collective-permute-start(bf16[4,32,1536]{2,1,0:T(8,128)(2,1)} %get-tuple-element.80), channel_id=1, source_target_pairs={{0,8},{8,16},{16,24},{24,0},{32,40},{40,48},{48,56},{56,32},{64,72... | collective-permute-start | bytes 1179656 | tf_op jit(solution)/shard_map/ppermute | solution.py:714
  32.0 18.4 %collective-permute-start.10 = (bf16[4,32,1536]{2,1,0:T(8,128)(2,1)}, bf16[4,32,1536]{2,1,0:T(8,128)(2,1)S(1)}, u32[]{:S(2)}, u32[]{:S(2)}) collective-permute-start(bf16[4,32,1536]{2,1,0:T(8,128)(2,1)} %get-tuple-element.81), channel_id=1, source_target_pairs={{0,24},{8,0},{16,8},{24,16},{32,56},{40,32},{48,40},{56,48},{64,88... | collective-permute-start | bytes 1179656 | tf_op jit(solution)/shard_map/ppermute | solution.py:715
  32.4 18.3 %collective-permute-start.13 = (bf16[8,32,1536]{2,1,0:T(8,128)(2,1)S(1)}, bf16[8,32,1536]{2,1,0:T(8,128)(2,1)S(1)}, u32[]{:S(2)}, u32[]{:S(2)}) collective-permute-start(bf16[8,32,1536]{2,1,0:T(8,128)(2,1)S(1)} %shard_map.85.refs_0_), channel_id=1, source_target_pairs={{0,1},{1,0},{2,3},{3,2},{4,5},{5,4},{6,7},{7,6},{8,9},{9,8},{10,11... | collective-permute-start | bytes 2359304 | tf_op jit(solution)/shard_map/ppermute | solution.py:726
  40.5 12.6 %collective-permute-start.11 = (bf16[4,32,1536]{2,1,0:T(8,128)(2,1)}, bf16[4,32,1536]{2,1,0:T(8,128)(2,1)}, u32[]{:S(2)}, u32[]{:S(2)}) collective-permute-start(bf16[4,32,1536]{2,1,0:T(8,128)(2,1)} %collective-permute-done.7), channel_id=1, source_target_pairs={{0,8},{8,16},{16,24},{24,0},{32,40},{40,48},{48,56},{56,32},{64,72... | collective-permute-start | bytes 1179656 | tf_op jit(solution)/shard_map/ppermute | solution.py:719
  40.8 12.3 %collective-permute-start.12 = (bf16[4,32,1536]{2,1,0:T(8,128)(2,1)}, bf16[4,32,1536]{2,1,0:T(8,128)(2,1)}, u32[]{:S(2)}, u32[]{:S(2)}) collective-permute-start(bf16[4,32,1536]{2,1,0:T(8,128)(2,1)} %collective-permute-done.8), channel_id=1, source_target_pairs={{0,24},{8,0},{16,8},{24,16},{32,56},{40,32},{48,40},{56,48},{64,88... | collective-permute-start | bytes 1179656 | tf_op jit(solution)/shard_map/ppermute | solution.py:720
  50.4 12.0 %copy-start.9 = (bf16[16,32,1536]{2,1,0:T(8,128)(2,1)}, bf16[16,32,1536]{2,1,0:T(8,128)(2,1)S(1)}, u32[]{:S(2)}) copy-start(bf16[16,32,1536]{2,1,0:T(8,128)(2,1)S(1)} %constant_dynamic-update-slice_fusion.refs_1_) | copy-start | bytes 4718596
  50.4 14.3 %collective-permute-start.14 = (bf16[16,32,1536]{2,1,0:T(8,128)(2,1)S(1)}, bf16[16,32,1536]{2,1,0:T(8,128)(2,1)}, u32[]{:S(2)}, u32[]{:S(2)}) collective-permute-start(bf16[16,32,1536]{2,1,0:T(8,128)(2,1)S(1)} %constant_dynamic-update-slice_fusion.refs_1_), channel_id=1, source_target_pairs={{0,1},{1,0},{2,3},{3,2},{4,5},{5,4},{6,7},{7,6},{8,9},{9,8},{10,11... | collective-permute-start | bytes 4718600 | tf_op jit(solution)/shard_map/ppermute | solution.py:726
  50.7 2.4 %copy-start.11 = (bf16[8,32,1536]{2,1,0:T(8,128)(2,1)}, bf16[8,32,1536]{2,1,0:T(8,128)(2,1)S(1)}, u32[]{:S(2)}) copy-start(bf16[8,32,1536]{2,1,0:T(8,128)(2,1)S(1)} %collective-permute-done.13.refs_3_) | copy-start | bytes 2359300
  53.1 33.8 %all-to-all-start = ((bf16[32,32,384]{2,1,0:T(8,128)(2,1)}), bf16[32,32,384]{2,1,0:T(8,128)(2,1)S(1)}, u32[]{:S(2)}, u32[]{:S(2)}) async-start(bf16[32,32,384]{2,1,0:T(8,128)(2,1)} %shard_map.87), calls=%async_computation | async-start | bytes 1572864 | tf_op jit(solution)/shard_map/all_to_all | solution.py:728
  62.4 3.3 %copy-start.10 = (bf16[8,32,1536]{2,1,0:T(8,128)(2,1)}, bf16[8,32,1536]{2,1,0:T(8,128)(2,1)S(1)}, u32[]{:S(2)}) copy-start(bf16[8,32,1536]{2,1,0:T(8,128)(2,1)S(1)} %constant_dynamic-update-slice_fusion.4.refs_2_) | copy-start | bytes 2359300
  62.4 2.4 %collective-permute-start.15 = (bf16[8,32,1536]{2,1,0:T(8,128)(2,1)S(1)}, bf16[8,32,1536]{2,1,0:T(8,128)(2,1)S(1)}, u32[]{:S(2)}, u32[]{:S(2)}) collective-permute-start(bf16[8,32,1536]{2,1,0:T(8,128)(2,1)S(1)} %constant_dynamic-update-slice_fusion.4.refs_2_), channel_id=1, source_target_pairs={{0,1},{1,0},{2,3},{3,2},{4,5},{5,4},{6,7},{7,6},{8,9},{9,8},{10,11... | collective-permute-start | bytes 2359304 | tf_op jit(solution)/shard_map/ppermute | solution.py:726
  64.8 0.9 copy-start.12
  74.2 1.5 collective-permute-start.16
  75.7 0.7 copy-start.5
  76.4 8.5 %copy-start.4 = (f32[8,128]{1,0:T(8,128)}, f32[8,128]{1,0:T(8,128)S(1)}, u32[]{:S(2)}) copy-start(f32[8,128]{1,0:T(8,128)S(1)} %shard_map.89.refs_0_) | copy-start | bytes 12292
  76.4 4.5 %collective-permute-start.19 = (f32[8,128]{1,0:T(8,128)S(1)}, f32[8,128]{1,0:T(8,128)S(1)}, u32[]{:S(2)}, u32[]{:S(2)}) collective-permute-start(f32[8,128]{1,0:T(8,128)S(1)} %shard_map.89.refs_0_), channel_id=1, source_target_pairs={{0,6},{1,7},{2,0},{3,1},{4,2},{5,3},{6,4},{7,5},{8,14},{9,15},{10,... | collective-permute-start | bytes 12296 | tf_op jit(solution)/shard_map/ppermute | solution.py:732
  79.2 5.1 %collective-permute-start.18 = (f32[8,128]{1,0:T(8,128)S(1)}, f32[8,128]{1,0:T(8,128)S(1)}, u32[]{:S(2)}, u32[]{:S(2)}) collective-permute-start(f32[8,128]{1,0:T(8,128)S(1)} %shard_map.89.refs_0_), channel_id=1, source_target_pairs={{0,4},{1,5},{2,6},{3,7},{4,0},{5,1},{6,2},{7,3},{8,12},{9,13},{10,... | collective-permute-start | bytes 12296 | tf_op jit(solution)/shard_map/ppermute | solution.py:732
  80.0 4.8 %collective-permute-start.17 = (f32[8,128]{1,0:T(8,128)S(1)}, f32[8,128]{1,0:T(8,128)S(1)}, u32[]{:S(2)}, u32[]{:S(2)}) collective-permute-start(f32[8,128]{1,0:T(8,128)S(1)} %shard_map.89.refs_0_), channel_id=1, source_target_pairs={{0,2},{1,3},{2,4},{3,5},{4,6},{5,7},{6,0},{7,1},{8,10},{9,11},{10,... | collective-permute-start | bytes 12296 | tf_op jit(solution)/shard_map/ppermute | solution.py:732
  80.9 3.9 %copy-start.14 = (f32[8,128]{1,0:T(8,128)}, f32[8,128]{1,0:T(8,128)S(1)}, u32[]{:S(2)}) copy-start(f32[8,128]{1,0:T(8,128)S(1)} %collective-permute-done.19.refs_3_) | copy-start | bytes 12292
  86.9 29.8 %collective-permute-start.22 = (bf16[384,1536]{1,0:T(8,128)(2,1)}, bf16[384,1536]{1,0:T(8,128)(2,1)S(1)}, u32[]{:S(2)}, u32[]{:S(2)}) collective-permute-start(bf16[384,1536]{1,0:T(8,128)(2,1)} %get-tuple-element.66), channel_id=1, source_target_pairs={{0,1},{1,0},{2,3},{3,2},{4,5},{5,4},{6,7},{7,6},{8,9},{9,8},{10,11... | collective-permute-start | bytes 3538952 | tf_op jit(solution)/shard_map/ppermute | solution.py:735
  86.9 9.8 %copy-start.8 = (bf16[32,32,384]{2,1,0:T(8,128)(2,1)}, bf16[32,32,384]{2,1,0:T(8,128)(2,1)S(1)}, u32[]{:S(2)}) copy-start(bf16[32,32,384]{2,1,0:T(8,128)(2,1)S(1)} %all-to-all-done) | copy-start | bytes 2359300
  86.9 19.2 %all-to-all-start.1 = ((f32[32,8,128]{2,1,0:T(8,128)}), f32[32,8,128]{2,1,0:T(8,128)S(1)}, u32[]{:S(2)}, u32[]{:S(2)}) async-start(f32[32,8,128]{2,1,0:T(8,128)} %shard_map.90), calls=%async_computation.1 | async-start | bytes 262144 | tf_op jit(solution)/shard_map/all_to_all | solution.py:737
  106.1 10.6 %copy-start.2 = (bf16[384,1536]{1,0:T(8,128)(2,1)S(1)}, bf16[384,1536]{1,0:T(8,128)(2,1)}, u32[]{:S(2)}) copy-start(bf16[384,1536]{1,0:T(8,128)(2,1)} %get-tuple-element.65.w_own) | copy-start | bytes 3538948
  106.2 0.7 copy-start.13
  114.2 2.6 %collective-permute-start.21 = (bf16[1024,384]{1,0:T(8,128)(2,1)}, bf16[1024,384]{1,0:T(8,128)(2,1)S(1)}, u32[]{:S(2)}, u32[]{:S(2)}) collective-permute-start(bf16[1024,384]{1,0:T(8,128)(2,1)} %get-tuple-element.64.own_ref), channel_id=1, source_target_pairs={{0,1},{1,0},{2,3},{3,2},{4,5},{5,4},{6,7},{7,6},{8,9},{9,8},{10,11... | collective-permute-start | bytes 2359304 | tf_op jit(solution)/shard_map/ppermute | solution.py:743
  114.3 2.4 %collective-permute-start.20 = (f32[1,1]{1,0:T(1,128)}, f32[1,1]{1,0:T(1,128)}, u32[]{:S(2)}, u32[]{:S(2)}) collective-permute-start(f32[1,1]{1,0:T(1,128)} %get-tuple-element.63.loss_ref), channel_id=1, source_target_pairs={{0,1},{1,0},{2,3},{3,2},{4,5},{5,4},{6,7},{7,6},{8,9},{9,8},{10,11... | collective-permute-start | bytes 20 | tf_op jit(solution)/shard_map/ppermute | solution.py:742
  116.8 1.1 copy-start.3
  120.6 13.5 %collective-permute-start.25 = (s16[528,384]{1,0:T(8,128)(2,1)S(1)}, s16[528,384]{1,0:T(8,128)(2,1)S(1)}, u32[]{:S(2)}, u32[]{:S(2)}) collective-permute-start(s16[528,384]{1,0:T(8,128)(2,1)S(1)} %get-tuple-element.72), channel_id=1, source_target_pairs={{0,2},{1,3},{2,4},{3,5},{4,6},{5,7},{6,0},{7,1},{8,10},{9,11},{10,... | collective-permute-start | bytes 1216520 | tf_op jit(solution)/shard_map/ppermute | solution.py:745
  120.7 13.9 %collective-permute-start.27 = (s16[528,384]{1,0:T(8,128)(2,1)S(1)}, s16[528,384]{1,0:T(8,128)(2,1)S(1)}, u32[]{:S(2)}, u32[]{:S(2)}) collective-permute-start(s16[528,384]{1,0:T(8,128)(2,1)S(1)} %get-tuple-element.74), channel_id=1, source_target_pairs={{0,6},{1,7},{2,0},{3,1},{4,2},{5,3},{6,4},{7,5},{8,14},{9,15},{10,... | collective-permute-start | bytes 1216520 | tf_op jit(solution)/shard_map/ppermute | solution.py:746
  126.5 15.9 %collective-permute-start.23 = (s16[528,384]{1,0:T(8,128)(2,1)S(1)}, s16[528,384]{1,0:T(8,128)(2,1)S(1)}, u32[]{:S(2)}, u32[]{:S(2)}) collective-permute-start(s16[528,384]{1,0:T(8,128)(2,1)S(1)} %get-tuple-element.69), channel_id=1, source_target_pairs={{0,6},{1,7},{2,0},{3,1},{4,2},{5,3},{6,4},{7,5},{8,14},{9,15},{10,... | collective-permute-start | bytes 1216520 | tf_op jit(solution)/shard_map/ppermute | solution.py:749
  126.6 16.2 %collective-permute-start.24 = (s16[528,384]{1,0:T(8,128)(2,1)S(1)}, s16[528,384]{1,0:T(8,128)(2,1)S(1)}, u32[]{:S(2)}, u32[]{:S(2)}) collective-permute-start(s16[528,384]{1,0:T(8,128)(2,1)S(1)} %get-tuple-element.70), channel_id=1, source_target_pairs={{0,2},{1,3},{2,4},{3,5},{4,6},{5,7},{6,0},{7,1},{8,10},{9,11},{10,... | collective-permute-start | bytes 1216520 | tf_op jit(solution)/shard_map/ppermute | solution.py:748
  134.5 16.2 %collective-permute-start.26 = (s16[528,384]{1,0:T(8,128)(2,1)S(1)}, s16[528,384]{1,0:T(8,128)(2,1)S(1)}, u32[]{:S(2)}, u32[]{:S(2)}) collective-permute-start(s16[528,384]{1,0:T(8,128)(2,1)S(1)} %shard_map.97), channel_id=1, source_target_pairs={{0,2},{1,3},{2,4},{3,5},{4,6},{5,7},{6,0},{7,1},{8,10},{9,11},{10,... | collective-permute-start | bytes 1216520 | tf_op jit(solution)/shard_map/ppermute | solution.py:750
  135.0 15.7 %collective-permute-start.28 = (s16[528,384]{1,0:T(8,128)(2,1)S(1)}, s16[528,384]{1,0:T(8,128)(2,1)S(1)}, u32[]{:S(2)}, u32[]{:S(2)}) collective-permute-start(s16[528,384]{1,0:T(8,128)(2,1)S(1)} %shard_map.98), channel_id=1, source_target_pairs={{0,6},{1,7},{2,0},{3,1},{4,2},{5,3},{6,4},{7,5},{8,14},{9,15},{10,... | collective-permute-start | bytes 1216520 | tf_op jit(solution)/shard_map/ppermute | solution.py:751
  152.6 9.9 %copy-start.17 = (s32[32]{0:T(128)S(1)}, s32[32]{0:T(128)}, u32[]{:S(2)}) copy-start(s32[32]{0:T(128)} %param.9) | copy-start | bytes 388
  152.6 11.2 %copy-start.7 = (bf16[1024,768]{1,0:T(8,128)(2,1)S(1)}, bf16[1024,768]{1,0:T(8,128)(2,1)}, u32[]{:S(2)}) copy-start(bf16[1024,768]{1,0:T(8,128)(2,1)} %get-tuple-element.62.sums_ref) | copy-start | bytes 4718596
  152.6 34.6 %all-to-all-start.2 = ((s16[32,112,128]{2,1,0:T(8,128)(2,1)}), s16[32,112,128]{2,1,0:T(8,128)(2,1)S(1)}, u32[]{:S(2)}, u32[]{:S(2)}) async-start(s16[32,112,128]{2,1,0:T(8,128)(2,1)} %shard_map.99), calls=%async_computation.2 | async-start | bytes 1835008 | tf_op jit(solution)/shard_map/all_to_all | solution.py:754
  163.8 2.8 %copy-start.6 = (bf16[2,8,4,32,1536]{4,3,2,1,0:T(8,128)(2,1)S(1)}, bf16[2,8,4,32,1536]{4,3,2,1,0:T(8,128)(2,1)}, u32[]{:S(2)}) copy-start(bf16[2,8,4,32,1536]{4,3,2,1,0:T(8,128)(2,1)} %get-tuple-element.48) | copy-start | bytes 18874372
  (2 other events, 1.2 us)
